TPU v7x, 32 devices: a whole 2x2x4 slice. The times are simulated.
32 devices in a mesh: ctx: 8 (over z, core), fsdp: 4 (over y, x).
Axes of the slice: x: 2, y: 2, z: 4, core: 2. Of those that a mesh axis runs over, the one named last changes fastest.
Arguments:
- tokens: bfloat16 [4, 1024, 1536], P('fsdp', 'ctx'), may hold values from -6 to 6
- segments: int32 [4, 1024], P('fsdp', 'ctx'), may hold values from 0 to 11, as said below
- positions: int32 [4, 1024], P('fsdp', 'ctx'), may hold values from 0 to 511, as said below
- norm1_gain: bfloat16 [1536], P(('ctx', 'fsdp')), may hold values from 0.5 to 1.5
- qkv_weight: bfloat16 [1536, 2048], P(('ctx', 'fsdp')), may hold values from -0.21875 to 0.21875
- qkv_bias: bfloat16 [2048], P(('ctx', 'fsdp')), may hold values from -3 to 3
- out_weight: bfloat16 [1536, 1536], P(('ctx', 'fsdp')), may hold values from -0.5 to 0.5
- norm2_gain: bfloat16 [1536], P(('ctx', 'fsdp')), may hold values from 0.5 to 1.5
- gate_up_weight: bfloat16 [1536, 17920], P(('ctx', 'fsdp')), may hold values from -0.15625 to 0.15625
- down_weight: bfloat16 [8960, 1536], P(('ctx', 'fsdp')), may hold values from -0.125 to 0.125
- cotangent: bfloat16 [4, 1024, 1536], P('fsdp', 'ctx'), may hold values from -6 to 6
Outputs:
- output: bfloat16 [4, 1024, 1536], P('fsdp', 'ctx')
- input_grad: float32 [4, 1024, 1536], P('fsdp', 'ctx')
- norm1_grad: float32 [1536], P(('ctx', 'fsdp'))
- qkv_weight_grad: float32 [1536, 2048], P(('ctx', 'fsdp'))
- qkv_bias_grad: float32 [2048], P(('ctx', 'fsdp'))
- out_weight_grad: float32 [1536, 1536], P(('ctx', 'fsdp'))
- norm2_grad: float32 [1536], P(('ctx', 'fsdp'))
- gate_up_grad: float32 [1536, 17920], P(('ctx', 'fsdp'))
- down_grad: float32 [8960, 1536], P(('ctx', 'fsdp'))
Inputs may be any that keep to these rules, and one draw needn't show every extreme that they name: `segments`: within each sequence documents are numbered 0, 1, 2 and so on in order; each whole document has 51 to 512 tokens, the last one may be cut by the sequence's end, and one of the first two has exactly 512. `positions`: A token's place within its document, 0 at the document's first token.
All inputs are finite; a program needn't handle non-finite values.
Results may differ from a plain program's by a relative error of at most 0.033.
Values may be sent and summed in bfloat16 or wider, within the bound.
No kernel may reach another device: no remote copies, remote signals or barrier semaphores. Data moves between devices by JAX's collectives and lax.ppermute only.
A program may use at most 512 MiB of HBM per device.

v0:
```python
import jax
import jax.numpy as jnp
from jax import lax
from jax.sharding import PartitionSpec as P

FF = 8960
Q_HEADS = 12
KV_HEADS = 2
HEAD_DIM = 128


EPSILON = 1e-06


def passed_along(value, axis, steps):
    count = lax.axis_size(axis)
    leading, last = (max(0, -steps), min(count, count - steps))
    return lax.ppermute(value, axis, [(source, source + steps) for source in range(leading, last)])


def matmul_tn(left, right):
    return lax.dot_general(
        left, right, (((0,), (0,)), ((), ())), preferred_element_type=jnp.float32
    )


def matmul_nt(left, right):
    return lax.dot_general(
        left, right, (((1,), (1,)), ((), ())), preferred_element_type=jnp.float32
    )


def angle_tables(place_ids):
    steps_half = jnp.arange(0, HEAD_DIM, 2).astype(jnp.float32)
    inverse = 10000.0 ** (-steps_half / HEAD_DIM)
    turns = place_ids.astype(jnp.float32)[:, None] * inverse[None, :]
    turns = jnp.concatenate([turns, turns], axis=-1)
    return (jnp.cos(turns), jnp.sin(turns))


def rotate(heads_in, cosine, sine):
    half = heads_in.shape[-1] // 2
    turned = jnp.concatenate([-heads_in[..., half:], heads_in[..., :half]], axis=-1)
    return heads_in * cosine[:, None, :] + turned * sine[:, None, :]


def rotate_back(grad_in, cosine, sine):
    half = grad_in.shape[-1] // 2
    scaled = grad_in * sine[:, None, :]
    turned = jnp.concatenate([scaled[..., half:], -scaled[..., :half]], axis=-1)
    return grad_in * cosine[:, None, :] + turned


def group_heads(heads_in, tok_rows):
    group_size = Q_HEADS // KV_HEADS
    shaped = heads_in.reshape(tok_rows, KV_HEADS, group_size, HEAD_DIM).transpose(1, 2, 0, 3)
    return shaped.reshape(KV_HEADS, group_size * tok_rows, HEAD_DIM)


def ungroup_heads(grouped, tok_rows):
    group_size = Q_HEADS // KV_HEADS
    shaped = grouped.reshape(KV_HEADS, group_size, tok_rows, HEAD_DIM).transpose(2, 0, 1, 3)
    return shaped.reshape(tok_rows, Q_HEADS * HEAD_DIM)


def visible(query_seg, query_place, key_seg, key_place):
    allowed = (query_seg[:, None] == key_seg[None, :]) & (
        query_place[:, None] >= key_place[None, :]
    )
    return jnp.tile(allowed, (Q_HEADS // KV_HEADS, 1))


def attend_block(softmax_state, query_group, key_block, value_block, allowed, score_scale):
    row_max, row_sum, weighted = softmax_state
    scores = (
        jnp.einsum("grd,kgd->grk", query_group, key_block, preferred_element_type=jnp.float32)
        * score_scale
    )
    scores = jnp.where(allowed[None], scores, -jnp.inf)
    fresh_max = jnp.maximum(row_max, jnp.max(scores, axis=-1))
    exps = jnp.exp(scores - fresh_max[..., None])
    factor = jnp.exp(row_max - fresh_max)
    row_sum = row_sum * factor + jnp.sum(exps, axis=-1)
    weighted = weighted * factor[..., None] + jnp.einsum(
        "grk,kgd->grd", exps.astype(jnp.bfloat16), value_block, preferred_element_type=jnp.float32
    )
    return (fresh_max, row_sum, weighted)


def attend_back(
    query_group, grad_group, key_block, value_block, allowed, logsum, offset, score_scale
):
    scores = (
        jnp.einsum("grd,kgd->grk", query_group, key_block, preferred_element_type=jnp.float32)
        * score_scale
    )
    probs_full = jnp.where(allowed[None], jnp.exp(scores - logsum[..., None]), 0.0)
    grad_probs = jnp.einsum(
        "grd,kgd->grk", grad_group, value_block, preferred_element_type=jnp.float32
    )
    grad_scores = (probs_full * (grad_probs - offset[..., None])).astype(jnp.bfloat16)
    grad_query = (
        jnp.einsum("grk,kgd->grd", grad_scores, key_block, preferred_element_type=jnp.float32)
        * score_scale
    )
    grad_key = (
        jnp.einsum("grk,grd->kgd", grad_scores, query_group, preferred_element_type=jnp.float32)
        * score_scale
    )
    grad_value = jnp.einsum(
        "grk,grd->kgd",
        probs_full.astype(jnp.bfloat16),
        grad_group,
        preferred_element_type=jnp.float32,
    )
    return (grad_query, grad_key, grad_value)


def norm_back(grad_normed, values_in, factor, gain):
    weighted = grad_normed * gain
    gain_grad = jnp.sum(grad_normed * values_in * factor, axis=0)
    value_grad = factor * weighted - values_in * factor * factor * factor * jnp.mean(
        weighted * values_in, axis=-1, keepdims=True
    )
    return (value_grad, gain_grad)


def shards(
    tokens,
    segments,
    positions,
    norm1_gain,
    qkv_weight,
    qkv_bias,
    out_weight,
    norm2_gain,
    gate_up_weight,
    down_weight,
    cotangent,
):
    inputs = tokens[0].astype(jnp.float32)
    tok_rows = inputs.shape[0]
    query_seg = segments[0].astype(jnp.float32)
    ctx_count = lax.axis_size("ctx")
    my_block = lax.axis_index("ctx")
    group_size = Q_HEADS // KV_HEADS
    lane_count = group_size * tok_rows
    score_scale = HEAD_DIM ** (-0.5)
    width_q = Q_HEADS * HEAD_DIM
    width_k = KV_HEADS * HEAD_DIM
    query_place = my_block * tok_rows + jnp.arange(tok_rows, dtype=jnp.int32)
    gain_one, w_qkv, b_qkv, w_out, gain_two = (
        lax.all_gather(norm1_gain, ("ctx", "fsdp"), axis=0, tiled=True),
        lax.all_gather(qkv_weight, ("ctx", "fsdp"), axis=0, tiled=True),
        lax.all_gather(qkv_bias, ("ctx", "fsdp"), axis=0, tiled=True),
        lax.all_gather(out_weight, ("ctx", "fsdp"), axis=0, tiled=True),
        lax.all_gather(norm2_gain, ("ctx", "fsdp"), axis=0, tiled=True),
    )
    gain_one = gain_one.astype(jnp.float32)
    gain_two = gain_two.astype(jnp.float32)
    rms_one = lax.rsqrt(jnp.mean(inputs * inputs, axis=-1, keepdims=True) + EPSILON)
    normed_one = (inputs * rms_one * gain_one).astype(jnp.bfloat16)
    projected = jnp.dot(normed_one, w_qkv, preferred_element_type=jnp.float32) + b_qkv.astype(
        jnp.float32
    )
    cosine, sine = angle_tables(positions[0])
    queries = rotate(
        projected[:, :width_q].reshape(tok_rows, Q_HEADS, HEAD_DIM), cosine, sine
    ).astype(jnp.bfloat16)
    key_heads = rotate(
        projected[:, width_q : width_q + width_k].reshape(tok_rows, KV_HEADS, HEAD_DIM),
        cosine,
        sine,
    ).astype(jnp.bfloat16)
    values = (
        projected[:, width_q + width_k :].reshape(tok_rows, KV_HEADS, HEAD_DIM).astype(jnp.bfloat16)
    )
    query_group = group_heads(queries, tok_rows)
    local_block = (key_heads, values, query_seg.astype(jnp.bfloat16))

    def block_mask(seg_block, owner_index):
        key_place = owner_index * tok_rows + jnp.arange(tok_rows, dtype=jnp.int32)
        return visible(query_seg, query_place, seg_block.astype(jnp.float32), key_place)

    def apply_block(softmax_state, kv_block, owner_index):
        allowed = block_mask(kv_block[2], owner_index)
        return attend_block(
            softmax_state, query_group, kv_block[0], kv_block[1], allowed, score_scale
        )

    start_state = (
        jnp.full((KV_HEADS, lane_count), -1e30, jnp.float32),
        jnp.zeros((KV_HEADS, lane_count), jnp.float32),
        jnp.zeros((KV_HEADS, lane_count, HEAD_DIM), jnp.float32),
    )
    first_state = apply_block(start_state, local_block, my_block)

    def forward_step(step_index, carry):
        softmax_state, kv_block = carry
        kv_block = passed_along((kv_block[0], kv_block[1], kv_block[2]), "ctx", 1)
        owner_index = my_block - step_index
        softmax_state = lax.cond(
            owner_index >= 0,
            lambda: apply_block(softmax_state, kv_block, owner_index),
            lambda: softmax_state,
        )
        return (softmax_state, kv_block)

    softmax_state, _ = lax.fori_loop(1, ctx_count, forward_step, (first_state, local_block))
    row_max, row_sum, weighted = softmax_state
    logsum = row_max + jnp.log(row_sum)
    attended = weighted / row_sum[..., None]
    context = ungroup_heads(attended, tok_rows).astype(jnp.bfloat16)
    middle = inputs + matmul_nt(context, w_out)
    rms_two = lax.rsqrt(jnp.mean(middle * middle, axis=-1, keepdims=True) + EPSILON)
    normed_two = (middle * rms_two * gain_two).astype(jnp.bfloat16)
    grad_out = cotangent[0]
    columns = normed_two
    gate_up = jnp.dot(
        columns,
        lax.all_gather(gate_up_weight, ("ctx", "fsdp"), axis=0, tiled=True),
        preferred_element_type=jnp.float32,
    )
    gate_part = gate_up[:, :FF]
    up_part = gate_up[:, FF:]
    gate_sig = jax.nn.sigmoid(gate_part)
    swished = gate_part * gate_sig
    hidden = (swished * up_part).astype(jnp.bfloat16)
    columns = hidden
    branch = jnp.dot(
        columns,
        lax.all_gather(down_weight, ("ctx", "fsdp"), axis=0, tiled=True),
        preferred_element_type=jnp.float32,
    )
    result = (middle + branch).astype(jnp.bfloat16)
    grad_hidden = matmul_nt(
        grad_out, lax.all_gather(down_weight, ("ctx", "fsdp"), axis=0, tiled=True)
    )
    down_grad = lax.psum_scatter(
        matmul_tn(hidden, grad_out), ("ctx", "fsdp"), scatter_dimension=0, tiled=True
    )
    grad_gate = grad_hidden * up_part * gate_sig * (1.0 + gate_part * (1.0 - gate_sig))
    grad_up = grad_hidden * swished
    grad_gate_up = jnp.concatenate([grad_gate, grad_up], axis=1).astype(jnp.bfloat16)
    gate_up_grad = lax.psum_scatter(
        matmul_tn(normed_two, grad_gate_up), ("ctx", "fsdp"), scatter_dimension=0, tiled=True
    )
    grad_normed_two = matmul_nt(
        grad_gate_up, lax.all_gather(gate_up_weight, ("ctx", "fsdp"), axis=0, tiled=True)
    )
    grad_middle, gain_two_grad = norm_back(grad_normed_two, middle, rms_two, gain_two)
    grad_middle = grad_middle + grad_out.astype(jnp.float32)
    grad_attention = grad_middle.astype(jnp.bfloat16)
    out_grad = matmul_tn(grad_attention, context)
    grad_context = jnp.dot(grad_attention, w_out, preferred_element_type=jnp.float32).astype(
        jnp.bfloat16
    )
    grad_group = group_heads(grad_context.reshape(tok_rows, Q_HEADS, HEAD_DIM), tok_rows)
    offset = jnp.sum(grad_group.astype(jnp.float32) * attended, axis=-1)

    def back_block(kv_block, owner_index):
        allowed = block_mask(kv_block[2], owner_index)
        return attend_back(
            query_group, grad_group, kv_block[0], kv_block[1], allowed, logsum, offset, score_scale
        )

    zero_key = jnp.zeros((tok_rows, KV_HEADS, HEAD_DIM), jnp.float32)
    kept_keys = jnp.zeros((ctx_count, tok_rows, KV_HEADS, HEAD_DIM), jnp.float32)
    own_query, own_key, own_value = back_block(local_block, my_block)
    kept_keys = kept_keys.at[0].set(own_key)
    kept_values = (
        jnp.zeros((ctx_count, tok_rows, KV_HEADS, HEAD_DIM), jnp.float32).at[0].set(own_value)
    )

    def backward_step(step_index, carry):
        grad_query, kv_block, stored_keys, stored_values = carry
        kv_block = passed_along((kv_block[0], kv_block[1], kv_block[2]), "ctx", 1)
        owner_index = my_block - step_index

        def compute_block():
            return back_block(kv_block, owner_index)

        part_query, part_key, part_value = lax.cond(
            owner_index >= 0,
            compute_block,
            lambda: (jnp.zeros_like(grad_query), zero_key, zero_key),
        )
        stored_keys = lax.dynamic_update_index_in_dim(stored_keys, part_key, step_index, 0)
        stored_values = lax.dynamic_update_index_in_dim(stored_values, part_value, step_index, 0)
        return (grad_query + part_query, kv_block, stored_keys, stored_values)

    grad_query, _, kept_keys, kept_values = lax.fori_loop(
        1, ctx_count, backward_step, (own_query, local_block, kept_keys, kept_values)
    )

    def return_step(time_index, carry):
        moving_keys, moving_values = carry
        slot = ctx_count - 1 - time_index
        moving_keys = moving_keys + lax.dynamic_index_in_dim(kept_keys, slot, 0, keepdims=False)
        moving_values = moving_values + lax.dynamic_index_in_dim(
            kept_values, slot, 0, keepdims=False
        )
        return (
            passed_along(moving_keys.astype(jnp.bfloat16), "ctx", -1).astype(moving_keys.dtype),
            passed_along(moving_values.astype(jnp.bfloat16), "ctx", -1).astype(moving_values.dtype),
        )

    moving_keys, moving_values = lax.fori_loop(0, ctx_count - 1, return_step, (zero_key, zero_key))
    grad_keys = moving_keys + kept_keys[0]
    grad_values = moving_values + kept_values[0]
    grad_queries = rotate_back(
        ungroup_heads(grad_query, tok_rows).reshape(tok_rows, Q_HEADS, HEAD_DIM), cosine, sine
    )
    grad_keys = rotate_back(grad_keys, cosine, sine)
    grad_projected = jnp.concatenate(
        [
            grad_queries.reshape(tok_rows, width_q),
            grad_keys.reshape(tok_rows, width_k),
            grad_values.reshape(tok_rows, width_k),
        ],
        axis=1,
    ).astype(jnp.bfloat16)
    bias_grad = jnp.sum(grad_projected.astype(jnp.float32), axis=0)
    qkv_grad = matmul_tn(normed_one, grad_projected)
    grad_normed_one = matmul_nt(grad_projected, w_qkv)
    input_grad, gain_one_grad = norm_back(grad_normed_one, inputs, rms_one, gain_one)
    input_grad = input_grad + grad_middle
    reduced = (
        lax.psum_scatter(gain_one_grad, ("ctx", "fsdp"), scatter_dimension=0, tiled=True),
        lax.psum_scatter(qkv_grad, ("ctx", "fsdp"), scatter_dimension=0, tiled=True),
        lax.psum_scatter(bias_grad, ("ctx", "fsdp"), scatter_dimension=0, tiled=True),
        lax.psum_scatter(out_grad, ("ctx", "fsdp"), scatter_dimension=0, tiled=True),
        lax.psum_scatter(gain_two_grad, ("ctx", "fsdp"), scatter_dimension=0, tiled=True),
    )
    return (
        result[None],
        input_grad[None],
        reduced[0],
        reduced[1],
        reduced[2],
        reduced[3],
        reduced[4],
        gate_up_grad,
        down_grad,
    )


def solution(mesh):
    placed = (
        P("fsdp", "ctx", None),
        P("fsdp", "ctx"),
        P("fsdp", "ctx"),
        P(("ctx", "fsdp")),
        P(("ctx", "fsdp"), None),
        P(("ctx", "fsdp")),
        P(("ctx", "fsdp"), None),
        P(("ctx", "fsdp")),
        P(("ctx", "fsdp"), None),
        P(("ctx", "fsdp"), None),
        P("fsdp", "ctx", None),
    )
    return jax.shard_map(
        shards,
        mesh=mesh,
        in_specs=placed,
        out_specs=(
            P("fsdp", "ctx", None),
            P("fsdp", "ctx", None),
            P(("ctx", "fsdp")),
            P(("ctx", "fsdp"), None),
            P(("ctx", "fsdp")),
            P(("ctx", "fsdp"), None),
            P(("ctx", "fsdp")),
            P(("ctx", "fsdp"), None),
            P(("ctx", "fsdp"), None),
        ),
        check_vma=False,
    )
```

profile of v0, /device:TPU:0, one launch (start us, length us, event | category | flops | bytes accessed | tf_op | source)
XLA Modules:
  0.0 2406.0 jit_solution(848086272616404608)
XLA Ops:
  15.0 42.5 %all-reduce.10 = (bf16[2048]{0:T(1024)(128)(2,1)S(1)}, bf16[1536]{0:T(1024)(128)(2,1)S(1)}, bf16[1536]{0:T(1024)(128)(2,1)S(1)}) all-reduce(bf16[2048]{0:T(1024)(128)(2,1)S(1)} %dynamic-update-slice.7, bf16[1536]{0:T(1024)(128)(2,1)S(1)} %dynamic-update-slice.6, ...), channel_id=1, replica_groups=mesh['ctx'=8,'fsdp'=4] {'ctx','fsdp'}, use_global_device_ids=true, to_apply=%add.3 | all-reduce | flops 5120 | bytes 20480
  60.4 22.9 all-gather.5.cloned.1.call-done
  94.2 80.0 %while.70 = (s32[]{:T(128)}, f32[2,768]{1,0:T(2,128)S(1)}, f32[2,768]{1,0:T(2,128)S(1)}, f32[2,768,128]{2,1,0:T(8,128)S(1)}, bf16[128,2,128]{2,0,1:T(8,128)(2,1)...) while((s32[]{:T(128)}, f32[2,768]{1,0:T(2,128)S(1)}, ...), condition=%wide.region_8.9_spmd.clone, body=%wide.region_3.8_spmd.clone.sunk | while | flops 102485376 | bytes 5774003 | solution.py:209
  118.7 5.5 collective-permute-start.1
  142.7 4.2 collective-permute-start.1
  166.0 4.2 collective-permute-start.1
  175.1 4.2 multiply_reduce_fusion.3
  179.8 270.2 %all-gather.9.cloned.1.call-done = bf16[1536,17920]{1,0:T(8,128)(2,1)} async-done(((bf16[48,17920]{1,0:T(8,128)(2,1)}), bf16[1536,17920]{1,0:T(8,128)(2,1)}) %all-gather.9.cloned.1.call-update) | async-done | bytes 55050256 | tf_op jit(solution)/shard_map/all_gather | solution.py:221
  450.1 24.1 %fusion.79 = f32[128,17920]{1,0:T(8,128)} fusion(bf16[1536,17920]{1,0:T(8,128)(2,1)} %all-gather.9.cloned.1.call-done, f32[128,1536]{1,0:T(8,128)S(1)} %get-tuple-element.1085, f32[1536]{0:T(1024)S(1)} %convert_element_type.205, f32[128]{0:T(128)} %add_rsqrt_fusion), kind=kOutput, calls=%fused_computation.154 | convolution fusion | flops 7047020544 | bytes 65018368 | tf_op jit(solution)/shard_map/dot_general | solution.py:219
  474.1 142.8 %all-gather.11.cloned.1.call-done = bf16[8960,1536]{1,0:T(8,128)(2,1)} async-done(((bf16[280,1536]{1,0:T(8,128)(2,1)}), bf16[8960,1536]{1,0:T(8,128)(2,1)}) %all-gather.11.cloned.1.call-update) | async-done | bytes 27525136 | tf_op jit(solution)/shard_map/all_gather | solution.py:232
  616.9 18.7 multiply_convert_fusion.1
  635.7 26.0 %multiply_reduce_fusion = (f32[1536]{0:T(1024)}, f32[128]{0:T(128)S(1)}, f32[128,1536]{1,0:T(8,128)}) fusion(f32[128,1536]{1,0:T(8,128)S(1)} %get-tuple-element.1085, f32[128]{0:T(128)S(1)} %copy-done.36, f32[1536]{0:T(1024)S(1)} %convert_element_type.205, bf16[1536,17920]{1,0:T(8,128)(2,1)} %all-gather.9.cloned.1.call-done, ...), kind=kOutput, calls=%fused_computation.82 | convolution fusion | flops 7056783872 | bytes 61223936 | tf_op jit(solution)/shard_map/dot_general | solution.py:28
  663.2 6.4 fusion.58
  685.3 105.9 %while.71 = (s32[]{:T(128)}, f32[2,768,128]{2,1,0:T(8,128)S(1)}, bf16[128,2,128]{2,0,1:T(8,128)(2,1)S(1)}, bf16[128,2,128]{2,0,1:T(8,128)(2,1)}, bf16[128]{0:T(2...) while((s32[]{:T(128)}, f32[2,768,128]{2,1,0:T(8,128)S(1)}, ...), condition=%wide.region_15.16_spmd.clone, body=%wide.region_12.15_spmd.clone.sunk | while | flops 253510016 | bytes 10275545 | solution.py:292
  695.3 7.5 collective-permute-start.5
  702.8 4.2 collective-permute-start.4
  715.3 7.7 collective-permute-start.4
  730.9 4.3 collective-permute-start.4
  735.3 5.5 collective-permute-start.3
  744.6 4.8 collective-permute-start.5
  749.3 4.3 collective-permute-start.4
  760.1 9.4 collective-permute-start.5
  791.2 73.0 %while.72 = (s32[]{:T(128)}, f32[128,2,128]{2,1,0:T(2,128)}, f32[128,2,128]{2,1,0:T(2,128)}, f32[8,128,2,128]{3,2,1,0:T(2,128)}, f32[8,128,2,128]{3,2,1,0:T(2,12...) while((s32[]{:T(128)}, f32[128,2,128]{2,1,0:T(2,128)}, f32[128,2,128]{2,1,0:T(2,128)}, ...), condition=%wide.region_17.18_spmd.clone, body=%wide.region_16.17_spmd.clone.sunk | while | flops 262151 | bytes 1573102 | solution.py:308
  870.6 6.4 fusion.65
  878.7 25.1 %fusion.47 = f32[8960,1536]{1,0:T(8,128)} fusion(bf16[128,8960]{1,0:T(8,128)(2,1)S(1)} %copy-done.2, bf16[1,128,1536]{2,1,0:T(8,128)(2,1)} %param.35), kind=kOutput, calls=%fused_computation.98 | convolution fusion | flops 3523215360 | bytes 57737216 | tf_op jit(solution)/shard_map/dot_general | solution.py:22
  905.6 42.4 %fusion.19 = f32[1536,17920]{1,0:T(8,128)} fusion(bf16[128,8960]{1,0:T(8,128)(2,1)} %get-tuple-element.1065, bf16[128,8960]{1,0:T(8,128)(2,1)S(1)} %copy-done.12, f32[128,1536]{1,0:T(8,128)S(1)} %get-tuple-element.1085, f32[1536]{0:T(1024)S(1)} %convert_element_type.205, f32[128]{0:T(128)S(1)} %copy-done.37), kind=kOutput, calls=%fused_computation.41 | convolution fusion | flops 7056195584 | bytes 115481088 | tf_op jit(solution)/shard_map/dot_general | solution.py:22
  949.2 5.2 fusion.37
  954.4 43.3 %all-reduce.9 = (f32[1536]{0:T(1024)S(1)}, f32[2048]{0:T(1024)S(1)}, f32[1536]{0:T(1024)S(1)}) all-reduce(f32[1536]{0:T(1024)S(1)} %get-tuple-element.986, f32[2048]{0:T(1024)S(1)} %convert_reduce_fusion, f32[1536]{0:T(1024)S(1)} %copy-done.42), channel_id=2, replica_groups=mesh['ctx'=8,'fsdp'=4] {'ctx','fsdp'}, use_global_device_ids=true, to_apply=%region_20.21.clone | all-reduce | flops 5120 | bytes 40960
  1000.7 12.0 fusion.22
  1012.7 24.2 %reduce-scatter.7.cloned.1.call-done = f32[48,2048]{1,0:T(8,128)} async-done(((f32[1536,2048]{1,0:T(8,128)}), f32[48,2048]{1,0:T(8,128)}) %reduce-scatter.7.cloned.1.call-update) | async-done | bytes 393232 | tf_op jit(solution)/shard_map/reduce_scatter | solution.py:330
  1036.9 468.4 %reduce-scatter.13.cloned.1.call-done = f32[280,1536]{1,0:T(8,128)} async-done(((f32[8960,1536]{1,0:T(8,128)}), f32[280,1536]{1,0:T(8,128)}) %reduce-scatter.13.cloned.1.call-update) | async-done | bytes 1720336
  1505.2 893.4 %reduce-scatter.11.cloned.1.call-done = f32[48,17920]{1,0:T(8,128)} async-done(((f32[1536,17920]{1,0:T(8,128)}), f32[48,17920]{1,0:T(8,128)}) %reduce-scatter.11.cloned.1.call-update) | async-done | bytes 3440656 | tf_op jit(solution)/shard_map/reduce_scatter | solution.py:245
  (420 shorter events, 250.2 us)
Async XLA Ops:
  7.2 76.1 %all-gather.5.cloned.1.call-start = ((), (), s32[]{:S(2)}) async-start(), calls=%async_computation.4 | async-start | bytes 6488064 | tf_op jit(solution)/shard_map/all_gather | solution.py:154
  7.9 167.2 %all-gather.7.cloned.1.call-start = ((), (), s32[]{:S(2)}) async-start(), calls=%async_computation.5 | async-start | bytes 4866048 | tf_op jit(solution)/shard_map/all_gather | solution.py:156
  8.7 441.4 %all-gather.9.cloned.1.call-start = ((), (), s32[]{:S(2)}) async-start(), calls=%async_computation.6 | async-start | bytes 56770560 | tf_op jit(solution)/shard_map/all_gather | solution.py:221
  9.4 607.5 %all-gather.11.cloned.1.call-start = ((), (), s32[]{:S(2)}) async-start(), calls=%async_computation.7 | async-start | bytes 28385280 | tf_op jit(solution)/shard_map/all_gather | solution.py:232
  10.0 1002.7 %reduce-scatter.9.cloned.1.call-start = ((), (), s32[]{:S(2)}) async-start(), calls=%async_computation.9 | async-start | bytes 9732096 | tf_op jit(solution)/shard_map/reduce_scatter | solution.py:332
  94.3 8.5 collective-permute-start.2
  104.1 10.8 collective-permute-start.2
  116.2 10.8 collective-permute-start.2
  118.7 8.3 collective-permute-start.1
  128.3 9.1 collective-permute-start.2
  138.7 10.9 collective-permute-start.2
  150.9 10.2 collective-permute-start.2
  162.4 10.5 collective-permute-start.2
  166.0 6.9 collective-permute-start.1
  669.6 367.2 %reduce-scatter.7.cloned.1.call-start = ((), (), s32[]{:S(2)}) async-start(), calls=%async_computation.8 | async-start | bytes 12976128 | tf_op jit(solution)/shard_map/reduce_scatter | solution.py:330
  685.5 7.5 collective-permute-start.5
  695.3 15.1 collective-permute-start.5
  702.8 7.5 collective-permute-start.4
  712.7 13.7 collective-permute-start.5
  715.3 11.1 collective-permute-start.4
  728.7 13.5 collective-permute-start.5
  730.9 11.3 collective-permute-start.4
  744.6 13.2 collective-permute-start.5
  749.3 8.4 collective-permute-start.4
  760.1 16.9 collective-permute-start.5
  769.5 7.5 collective-permute-start.4
  779.4 9.5 collective-permute-start.5
  781.6 7.3 collective-permute-start.4
  801.5 7.3 collective-permute-start.6
  803.8 8.0 collective-permute-start.7
  877.0 628.2 %reduce-scatter.13.cloned.1.call-start = ((), (), s32[]{:S(2)}) async-start(), calls=%async_computation.11 | async-start | bytes 56770560
  903.8 1494.9 %reduce-scatter.11.cloned.1.call-start = ((), (), s32[]{:S(2)}) async-start(), calls=%async_computation.10 | async-start | bytes 113541120 | tf_op jit(solution)/shard_map/reduce_scatter | solution.py:245
  (76 other events, 1294.4 us)
Sparse Core Ops, SparseCore 0:
  10.9 72.3 all-gather.4
  86.2 62.3 all-gather.6
  151.5 298.4 all-gather.8
  452.8 164.0 all-gather.10
  669.7 136.7 reduce-scatter.8
  877.2 159.6 reduce-scatter.6
  1043.9 461.3 reduce-scatter.12
  1513.4 885.2 reduce-scatter.10
where the time goes:
time: 2420 us; the launch traced here: 2410 us
  waiting for transfers between devices  1870 us (77%)
  matrix products  184 us (8%)
  starting transfers between devices  163 us (7%)
  blocking collectives  85.8 us (4%)
  local copies, waits for them, and re-layouts  51.8 us (2%)
  other arithmetic  38.7 us (2%)
    reduce_scatter x1, waiting for transfers between devices, shards(): lax.psum_scatter(matmul_tn(normed_two, grad_gate_up), ('ctx', 'fsdp'), sc...  893 us
    unnamed x9, waiting for transfers between devices  471 us
    all_gather x1, waiting for transfers between devices, shards(): lax.all_gather(gate_up_weight, ('ctx', 'fsdp'), axis=0, tiled=True)  270 us
    ppermute x56, starting transfers between devices, passed_along(): lax.ppermute(value, axis, [(source, source + steps) for source in range(l...  162 us
    all_gather x1, waiting for transfers between devices, shards(): lax.all_gather(down_weight, ('ctx', 'fsdp'), axis=0, tiled=True)  143 us
    unnamed x2, blocking collectives  85.8 us
    dot_general x4, matrix products, matmul_tn(): lax.dot_general(left, right, (((0,), (0,)), ((), ())), preferred_element_...  80.3 us
    dot_general x4, matrix products, matmul_nt(): lax.dot_general(left, right, (((1,), (1,)), ((), ())), preferred_element_...  54.1 us
  transfers between devices with their start and end apart: 64, of which 34 were waited for; matrix products, arithmetic and copies ran while one was open for 9% of the time, Pallas kernels for 0%

commit v1 on v0

v1 whole, which is shorter than its diff:
```python
import functools

import jax
import jax.numpy as jnp
from jax import lax
from jax.experimental import pallas as pl
from jax.experimental.pallas import tpu as pltpu
from jax.sharding import PartitionSpec as P

Q_HEADS = 12
KV_HEADS = 2
HEAD_DIM = 128
GROUP = Q_HEADS // KV_HEADS
WIDTH_Q = Q_HEADS * HEAD_DIM
WIDTH_K = KV_HEADS * HEAD_DIM
QKV = WIDTH_Q + 2 * WIDTH_K
LANES = 128
ROW_TILE = 16
EPSILON = 1e-06
SCALE = HEAD_DIM ** (-0.5)
BF16 = jnp.bfloat16
F32 = jnp.float32
VMEM_LIMIT = 56 * 1024 * 1024
BOTH = ("ctx", "fsdp")

SMEM_SPEC = pl.BlockSpec(memory_space=pltpu.SMEM)
VMEM_SPEC = pl.BlockSpec(memory_space=pltpu.VMEM)
ANY_SPEC = pl.BlockSpec(memory_space=pl.ANY)


def dot_nn(left, right):
    return lax.dot_general(left, right, (((1,), (0,)), ((), ())), preferred_element_type=F32)


def dot_tn(left, right):
    return lax.dot_general(left, right, (((0,), (0,)), ((), ())), preferred_element_type=F32)


def dot_nt(left, right):
    return lax.dot_general(left, right, (((1,), (1,)), ((), ())), preferred_element_type=F32)


def params():
    return pltpu.CompilerParams(vmem_limit_bytes=VMEM_LIMIT)


def cost(flops, nbytes, exps=0):
    return pl.CostEstimate(flops=int(flops), bytes_accessed=int(nbytes), transcendentals=int(exps))


def struct(shape, dtype):
    return jax.ShapeDtypeStruct(shape, dtype)


def swap_core(value):
    count = lax.axis_size("ctx")
    return lax.ppermute(value, "ctx", [(i, i ^ 1) for i in range(count)])


def shift_chip(value, steps):
    count = lax.axis_size("ctx")
    return lax.ppermute(value, "ctx", [(i, (i + 2 * steps) % count) for i in range(count)])


def shift_open(value, steps):
    count = lax.axis_size("ctx")
    pairs = [(i, i + 2 * steps) for i in range(count) if 0 <= i + 2 * steps < count]
    return lax.ppermute(value, "ctx", pairs)


def send_to(value, steps, other):
    count = lax.axis_size("ctx")
    return lax.ppermute(
        value, "ctx", [(i, ((i + 2 * steps) % count) ^ other) for i in range(count)]
    )


def swap_fsdp(value, bit):
    count = lax.axis_size("fsdp")
    return lax.ppermute(value, "fsdp", [(i, i ^ bit) for i in range(count)])


def picked(array, numbers, axis):
    items = [
        lax.dynamic_index_in_dim(array, numbers[index], axis, keepdims=False)
        for index in range(numbers.shape[0])
    ]
    return jnp.stack(items, axis=axis)


def bits_of(count):
    return [1 << k for k in range(count.bit_length() - 1)]


def halving_order(bits):
    if not bits:
        return [0]
    rest = halving_order(bits[1:])
    return [bits[0] ^ item for item in rest] + rest


def halves_of(chips, fsdp):
    bits = bits_of(fsdp)
    near = [step for step in range(chips) if step in (0, 1)]
    if chips > 2:
        far = [step for step in range(chips) if step not in near]
        return [(near, bits), (far, bits[::-1])]
    return [(near, bits)]


def gather_blocks(shard, chips, fsdp):
    if shard.shape[0] % ROW_TILE:
        return [lax.all_gather(shard, BOTH, axis=0, tiled=True)], None
    moved = {0: shard}
    for step in [1, chips - 1] + list(range(2, chips - 1)):
        if step not in moved and step < chips:
            moved[step] = shift_chip(shard, step)
    arrays, plan = [], []
    for steps, bits in halves_of(chips, fsdp):
        held = {0: jnp.concatenate([moved[step] for step in steps], axis=0)}
        for bit in bits:
            for item in list(held):
                held[item ^ bit] = swap_fsdp(held[item], bit)
        for item, array in held.items():
            for other, version in ((0, array), (1, swap_core(array))):
                for block, step in enumerate(steps):
                    plan.append((len(arrays), block, step, other, item))
                arrays.append(version)
    return arrays, plan


def reduce_blocks(kept, sent, chips, fsdp):
    if not sent:
        return lax.psum_scatter(kept[0], BOTH, scatter_dimension=0, tiled=True).astype(F32)
    total = None
    for (steps, bits), keep, send in zip(halves_of(chips, fsdp), kept, sent):
        held = keep + swap_core(send)
        for bit in bits:
            half = held.shape[0] // 2
            held = held[half:] + swap_fsdp(held[:half], bit)
        held = held[0]
        for at, step in enumerate(steps):
            part = held[at] if step == 0 else shift_chip(held[at], step)
            part = part.astype(F32)
            total = part if total is None else total + part
    return total


def block_row(info_ref, chips, fsdp, step, other, item, away=-1):
    chip = info_ref[0] // 2
    core = info_ref[0] % 2
    chip = (chip + away * step + chips) % chips
    core = 1 - core if other else core
    return (2 * chip + core) * fsdp + jnp.bitwise_xor(info_ref[1], item)


def copies_of(plan, info_ref, pieces, whole, sems, rows, columns, chips, fsdp):
    if plan is None:
        source = pieces[0].at[:, pl.ds(columns[0], columns[1])]
        return [pltpu.make_async_copy(source, whole, sems.at[0])]
    copies = []
    for index, (array, block, step, other, item) in enumerate(plan):
        row = block_row(info_ref, chips, fsdp, step, other, item) * rows
        row = pl.multiple_of(row, rows)
        source = pieces[array].at[pl.ds(block * rows, rows), pl.ds(columns[0], columns[1])]
        copies.append(pltpu.make_async_copy(source, whole.at[pl.ds(row, rows)], sems.at[index]))
    return copies


def normalised(values):
    return lax.rsqrt(jnp.mean(values * values, axis=-1, keepdims=True) + EPSILON)


def pack_kernel(qkv_ref, bias_ref, out_ref, gain_ref, packed_ref):
    packed_ref[:, :QKV] = (qkv_ref[...].astype(F32) * gain_ref[...]).astype(BF16)
    packed_ref[:, QKV : QKV + LANES] = bias_ref[...]
    packed_ref[:, QKV + LANES :] = out_ref[...]


def split_kernel(chips, own, padded, info_ref, weight_ref, gain_ref, split_ref):
    total = weight_ref.shape[1] // 2
    count = 2 * chips
    rows = weight_ref.shape[0]
    chip = info_ref[0] // 2
    core = info_ref[0] % 2
    filler = jnp.zeros((rows, padded - own), F32)
    for target in range(count):
        step = (target // 2 - chip + chips) % chips
        other = jnp.bitwise_xor(core, target % 2)
        for part in range(2):
            start = part * total + target * own
            values = weight_ref[:, start : start + own].astype(F32) * gain_ref[...]
            if padded > own:
                values = jnp.concatenate([values, filler], axis=1)
            split_ref[other, step, :, part * padded : (part + 1) * padded] = values.astype(BF16)


def join_kernel(chips, own, padded, info_ref, parts_ref, weight_ref, gain_ref, grad_ref, norm_ref):
    total = weight_ref.shape[1] // 2
    rows = weight_ref.shape[0]
    chip = info_ref[0] // 2
    core = info_ref[0] % 2
    sums = jnp.zeros((rows, 1), F32)
    for source in range(2 * chips):
        step = (chip - source // 2 + chips) % chips
        other = jnp.bitwise_xor(core, source % 2)
        for part in range(2):
            values = parts_ref[other * chips + step, :, part * padded : (part + 1) * padded]
            values = values[:, :own].astype(F32)
            start = part * total + source * own
            grad_ref[:, start : start + own] = values * gain_ref[...]
            sums = sums + jnp.sum(
                values * weight_ref[:, start : start + own].astype(F32), axis=1, keepdims=True
            )
    norm_ref[...] = sums


def project_kernel(plan, chips, fsdp, bias_width, count, info_ref, tokens_ref, cos_ref, sin_ref, *refs):
    pieces = refs[:count]
    unit_ref, q_ref, kv_ref, whole, sems = refs[count:]
    width = tokens_ref.shape[1]
    rows = width // (2 * chips * fsdp)
    copies = copies_of(plan, info_ref, pieces, whole, sems, rows, (0, QKV + LANES), chips, fsdp)
    for copy in copies:
        copy.start()
    values = tokens_ref[...].astype(F32)
    unit = (values * normalised(values)).astype(BF16)
    unit_ref[...] = unit
    for copy in copies:
        copy.wait()
    cosine, sine = cos_ref[...], sin_ref[...]
    each = LANES // bias_width
    for tile in range(QKV // LANES):
        at = tile * LANES
        bias = jnp.zeros((1, LANES), F32)
        for member in range(each):
            block = (tile * each + member) * rows
            first = block // ROW_TILE * ROW_TILE
            group = whole[first : first + ROW_TILE, QKV:].astype(F32)
            bias = bias + group[block - first : block - first + 1]
        head = dot_nn(unit, whole[:, at : at + LANES]) + bias
        if at < WIDTH_Q + WIDTH_K:
            head = head * cosine + pltpu.roll(head, HEAD_DIM // 2, 1) * sine
        if at < WIDTH_Q:
            q_ref[:, at : at + LANES] = head.astype(BF16)
        else:
            kv_ref[:, at - WIDTH_Q : at - WIDTH_Q + LANES] = head.astype(BF16)


def key_mask(info_ref, place_ref, rows, sources):
    own = info_ref[0] * rows + lax.broadcasted_iota(jnp.int32, (rows, rows), 0)
    begin = own - place_ref[...]
    masks = []
    for step, other in sources:
        block = info_ref[0] - 2 * step
        if other:
            block = jnp.bitwise_xor(info_ref[0], 1) - 2 * step
        keys = block * rows + lax.broadcasted_iota(jnp.int32, (rows, rows), 1)
        masks.append((keys <= own) & (keys >= begin) & (keys >= 0))
    return jnp.concatenate(masks, axis=1)


def head_part(kv_refs, column):
    return jnp.concatenate([ref[:, column : column + HEAD_DIM] for ref in kv_refs], axis=0)


def probabilities(query, keys, allowed):
    scores = dot_nt(query, keys) * SCALE
    scores = jnp.where(allowed, scores, -1e30)
    exps = jnp.exp(scores - jnp.max(scores, axis=1, keepdims=True))
    return exps * (1.0 / jnp.sum(exps, axis=1, keepdims=True))


def attend_kernel(plan, chips, fsdp, count, sources, info_ref, place_ref, q_ref, tokens_ref, *refs):
    kv_refs = refs[: len(sources)]
    refs = refs[len(sources) :]
    pieces = refs[:count]
    context_ref, middle_ref, unit_ref, whole, sems = refs[count:]
    rows, width = tokens_ref.shape
    block_rows = width // (2 * chips * fsdp)
    copies = copies_of(
        plan, info_ref, pieces, whole, sems, block_rows, (QKV + LANES, width), chips, fsdp
    )
    for copy in copies:
        copy.start()
    allowed = key_mask(info_ref, place_ref, rows, sources)
    for kv_head in range(KV_HEADS):
        keys = head_part(kv_refs, kv_head * HEAD_DIM)
        values = head_part(kv_refs, WIDTH_K + kv_head * HEAD_DIM)
        for member in range(GROUP):
            at = (kv_head * GROUP + member) * HEAD_DIM
            probs = probabilities(q_ref[:, at : at + HEAD_DIM], keys, allowed).astype(BF16)
            context_ref[:, at : at + HEAD_DIM] = dot_nn(probs, values).astype(BF16)
    for copy in copies:
        copy.wait()
    middle = tokens_ref[...].astype(F32) + dot_nt(context_ref[...], whole[...])
    middle_ref[...] = middle
    unit_ref[...] = (middle * normalised(middle)).astype(BF16)


def feed_kernel(
    chips, fsdp, own, padded, info_ref, x_mine, x_other, c_mine, c_other, wide_ref, down_ref,
    gu_mine, gu_other, br_mine, br_other, hidden_ref, grad_ref,
    wide, down, acc_units, acc_branch, sems,
):
    rows, width = x_mine.shape
    block_rows = width // (2 * chips * fsdp)
    copies = []
    index = 0
    if block_rows % ROW_TILE:
        copies.append(pltpu.make_async_copy(wide_ref, wide, sems.at[0]))
        index = 1
    for item in range(0 if index else fsdp):
        for other in range(2):
            for step in range(chips):
                chip = (info_ref[0] // 2 - step + chips) % chips
                core = jnp.bitwise_xor(info_ref[0] % 2, other)
                row = pl.multiple_of(((2 * chip + core) * fsdp + item) * block_rows, block_rows)
                copies.append(
                    pltpu.make_async_copy(
                        wide_ref.at[item, other * chips + step],
                        wide.at[pl.ds(row, block_rows)],
                        sems.at[index],
                    )
                )
                index += 1
    last = pltpu.make_async_copy(down_ref, down.at[pl.ds(0, own)], sems.at[index])
    for copy in copies:
        copy.start()
    last.start()
    if padded > own:
        down[own:, :] = jnp.zeros((padded - own, width), BF16)
    for copy in copies:
        copy.wait()
    last.wait()
    x = jnp.concatenate([x_mine[...], x_other[...]], axis=0)
    c = jnp.concatenate([c_mine[...], c_other[...]], axis=0)
    block = 384 if padded % 384 == 0 else LANES
    for at in range(0, padded, block):
        span = slice(at, at + block)
        span_up = slice(padded + at, padded + at + block)
        gate = dot_nn(x, wide[:, span])
        up = dot_nn(x, wide[:, span_up])
        grad_hidden = dot_nt(c, down[span, :])
        sig = 1.0 / (1.0 + jnp.exp(-gate))
        swished = gate * sig
        hidden = (swished * up).astype(BF16)
        grad_gate = (grad_hidden * up * sig * (1.0 + gate * (1.0 - sig))).astype(BF16)
        grad_up = (grad_hidden * swished).astype(BF16)
        hidden_ref[:, span] = hidden
        grad_ref[:, span] = grad_gate
        grad_ref[:, span_up] = grad_up
        units = dot_nt(grad_gate, wide[:, span]) + dot_nt(grad_up, wide[:, span_up])
        branch = dot_nn(hidden, down[span, :])
        if at == 0:
            acc_units[...] = units
            acc_branch[...] = branch
        else:
            acc_units[...] += units
            acc_branch[...] += branch
    gu_mine[...] = acc_units[:rows].astype(BF16)
    gu_other[...] = acc_units[rows:].astype(BF16)
    br_mine[...] = acc_branch[:rows].astype(BF16)
    br_other[...] = acc_branch[rows:].astype(BF16)


def wide_grad_kernel(chips, fsdp, n_units, info_ref, *refs):
    units = refs[:n_units]
    grads = refs[n_units : n_units + n_units // 2]
    out_ref, turned, total = refs[n_units + n_units // 2 :]
    rows, width = units[0].shape
    block_rows = width // (2 * chips * fsdp)

    @pl.when(pl.program_id(0) == 0)
    def _():
        for index, unit in enumerate(units):
            turned[:, index * rows : (index + 1) * rows] = unit[...].T

    for index, grad in enumerate(grads):
        part = dot_nn(turned[:, index * 2 * rows : (index + 1) * 2 * rows], grad[...])
        if index == 0:
            total[...] = part
        else:
            total[...] += part
    if block_rows % ROW_TILE:
        out_ref[...] = total[...].astype(BF16)
        return
    for item in range(fsdp):
        for other in range(2):
            for step in range(chips):
                chip = (info_ref[0] // 2 + step) % chips
                core = jnp.bitwise_xor(info_ref[0] % 2, other)
                row = pl.multiple_of(((2 * chip + core) * fsdp + item) * block_rows, block_rows)
                out_ref[item, other * chips + step] = total[pl.ds(row, block_rows), :].astype(BF16)


def down_grad_kernel(own, n_hidden, *refs):
    hiddens = refs[:n_hidden]
    cots = refs[n_hidden : 3 * n_hidden]
    out_ref, turned = refs[3 * n_hidden :]
    rows = hiddens[0].shape[0]

    @pl.when(pl.program_id(0) == 0)
    def _():
        for index, hidden in enumerate(hiddens):
            turned[:, index * rows : (index + 1) * rows] = hidden[...].T

    total = None
    for index in range(n_hidden):
        c = jnp.concatenate([cots[2 * index][...], cots[2 * index + 1][...]], axis=0)
        part = dot_nn(turned[:own, index * rows : (index + 1) * rows], c)
        total = part if total is None else total + part
    out_ref[...] = total.astype(BF16)


def middle_back_kernel(
    plan, chips, fsdp, count, sources, info_ref, place_ref, q_ref, own_ref, came_ref, middle_ref, cot_ref, *refs
):
    kv_refs = refs[: len(sources)]
    refs = refs[len(sources) :]
    pieces = refs[:count]
    grad_ref, att_ref, dq_ref, mine_ref, other_ref, whole, sems = refs[count:]
    rows, width = middle_ref.shape
    block_rows = width // (2 * chips * fsdp)
    copies = copies_of(
        plan, info_ref, pieces, whole, sems, block_rows, (QKV + LANES, width), chips, fsdp
    )
    for copy in copies:
        copy.start()
    units = own_ref[...].astype(F32) + came_ref[...].astype(F32)
    middle = middle_ref[...]
    rms = normalised(middle)
    grad_middle = (
        cot_ref[...].astype(F32)
        + rms * units
        - middle * (rms * rms * rms) * jnp.mean(units * middle, axis=-1, keepdims=True)
    )
    grad_ref[...] = grad_middle
    attention = grad_middle.astype(BF16)
    att_ref[...] = attention
    allowed = key_mask(info_ref, place_ref, rows, sources)
    for copy in copies:
        copy.wait()
    context_grad = dot_nn(attention, whole[...]).astype(BF16)
    for kv_head in range(KV_HEADS):
        keys = head_part(kv_refs, kv_head * HEAD_DIM)
        values = head_part(kv_refs, WIDTH_K + kv_head * HEAD_DIM)
        dkey = None
        dvalue = None
        for member in range(GROUP):
            at = (kv_head * GROUP + member) * HEAD_DIM
            query = q_ref[:, at : at + HEAD_DIM]
            grad = context_grad[:, at : at + HEAD_DIM]
            probs = probabilities(query, keys, allowed)
            dprobs = dot_nt(grad, values)
            offset = jnp.sum(probs * dprobs, axis=1, keepdims=True)
            dscores = (probs * (dprobs - offset)).astype(BF16)
            dq_ref[:, at : at + HEAD_DIM] = dot_nn(dscores, keys) * SCALE
            more_key = dot_tn(dscores, query)
            more_value = dot_tn(probs.astype(BF16), grad)
            dkey = more_key if dkey is None else dkey + more_key
            dvalue = more_value if dvalue is None else dvalue + more_value
        dkey = (dkey * SCALE).astype(BF16)
        dvalue = dvalue.astype(BF16)
        for index, (step, other) in enumerate(sources):
            ref = other_ref if other else mine_ref
            span = slice(index * rows, (index + 1) * rows)
            ref[step, :, kv_head * HEAD_DIM : (kv_head + 1) * HEAD_DIM] = dkey[span]
            ref[step, :, WIDTH_K + kv_head * HEAD_DIM : WIDTH_K + (kv_head + 1) * HEAD_DIM] = dvalue[span]


def scatter_out(total, info_ref, chips, fsdp, kept, sent):
    block_rows = total.shape[0] // (2 * chips * fsdp)
    if block_rows % ROW_TILE:
        kept[0][...] = total[...].astype(BF16)
        return
    for (steps, bits), keep, send in zip(halves_of(chips, fsdp), kept, sent):
        for slot, item in enumerate(halving_order(bits)):
            for at, step in enumerate(steps):
                for other, ref in ((0, keep), (1, send)):
                    row = block_row(info_ref, chips, fsdp, step, other, item, 1) * block_rows
                    row = pl.multiple_of(row, block_rows)
                    ref[slot, at] = total[pl.ds(row, block_rows), :].astype(BF16)


def out_grad_kernel(chips, fsdp, info_ref, left_ref, right_ref, *refs):
    halves = (len(refs) - 1) // 2
    kept, sent, total = refs[: max(halves, 1)], refs[halves : 2 * halves], refs[-1]
    total[...] = dot_nn(left_ref[...].T, right_ref[...])
    scatter_out(total, info_ref, chips, fsdp, kept, sent)


def projected_back_kernel(
    chips, fsdp, bias_width, came, info_ref, dq_ref, mine_ref, swapped_ref, cos_ref, sin_ref, unit_ref, *refs
):
    arrived = refs[:came]
    gp_ref, *refs = refs[came:]
    halves = (len(refs) - 1) // 2
    kept, sent, total = refs[: max(halves, 1)], refs[halves : 2 * halves], refs[-1]
    width = unit_ref.shape[1]
    block_rows = width // (2 * chips * fsdp)
    kv = mine_ref[...].astype(F32) + swapped_ref[...].astype(F32)
    for ref in arrived:
        kv = kv + ref[...].astype(F32)
    cosine, sine = cos_ref[...], sin_ref[...]
    for tile in range(QKV // LANES):
        at = tile * LANES
        head = dq_ref[:, at : at + LANES] if at < WIDTH_Q else kv[:, at - WIDTH_Q : at - WIDTH_Q + LANES]
        if at < WIDTH_Q + WIDTH_K:
            head = head * cosine - pltpu.roll(head, HEAD_DIM // 2, 1) * sine
        gp_ref[:, at : at + LANES] = head.astype(BF16)
    turned = unit_ref[...].T
    for at in range(0, QKV, 512):
        total[:, at : at + 512] = dot_nn(turned, gp_ref[:, at : at + 512])
    total[:, QKV:] = jnp.zeros((width, LANES), F32)
    each = LANES // bias_width
    for tile in range(QKV // LANES):
        sums = jnp.sum(gp_ref[:, tile * LANES : (tile + 1) * LANES].astype(F32), axis=0, keepdims=True)
        for member in range(each):
            block = (tile * each + member) * block_rows
            total[block : block + 8, QKV:] = jnp.broadcast_to(sums, (8, LANES))
    scatter_out(total, info_ref, chips, fsdp, kept, sent)


def input_back_kernel(plan, chips, fsdp, count, info_ref, gp_ref, tokens_ref, middle_ref, *refs):
    pieces = refs[:count]
    out_ref, whole, sems = refs[count:]
    width = tokens_ref.shape[1]
    rows = width // (2 * chips * fsdp)
    copies = copies_of(plan, info_ref, pieces, whole, sems, rows, (0, QKV), chips, fsdp)
    for copy in copies:
        copy.start()
    values = tokens_ref[...].astype(F32)
    rms = normalised(values)
    for copy in copies:
        copy.wait()
    unit_grad = dot_nt(gp_ref[...], whole[...])
    out_ref[...] = (
        middle_ref[...]
        + rms * unit_grad
        - values * (rms * rms * rms) * jnp.mean(unit_grad * values, axis=-1, keepdims=True)
    )


def call(kernel, outs, ins, any_from=None, any_to=None, scratch=(), estimate=None, name=None):
    specs = [SMEM_SPEC] + [VMEM_SPEC] * (len(ins) - 1)
    if any_from is not None:
        for index in range(any_from, any_to):
            specs[index] = ANY_SPEC
    many = isinstance(outs, (list, tuple))
    return pl.pallas_call(
        kernel,
        out_shape=outs,
        in_specs=specs,
        out_specs=[VMEM_SPEC] * len(outs) if many else VMEM_SPEC,
        scratch_shapes=list(scratch),
        compiler_params=params(),
        cost_estimate=estimate,
        name=name,
    )(*ins)


def shards(
    tokens,
    segments,
    positions,
    norm1_gain,
    qkv_weight,
    qkv_bias,
    out_weight,
    norm2_gain,
    gate_up_weight,
    down_weight,
    cotangent,
):
    inputs = tokens[0]
    grad_out = cotangent[0]
    rows, width = inputs.shape
    ctx = lax.axis_size("ctx")
    fsdp = lax.axis_size("fsdp")
    chips = ctx // 2
    my_ctx = lax.axis_index("ctx")
    my_fsdp = lax.axis_index("fsdp")
    info = jnp.stack([my_ctx, my_fsdp]).astype(jnp.int32)
    weight_rows = qkv_weight.shape[0]
    bias_width = qkv_bias.shape[0]
    own = gate_up_weight.shape[1] // 2 // ctx
    padded = -(-own // LANES) * LANES
    gain_one = norm1_gain.astype(F32)[:, None]
    gain_two = norm2_gain.astype(F32)[:, None]

    each = LANES // bias_width
    spot = (my_ctx * fsdp + my_fsdp) % each
    bias_row = jnp.where(
        jnp.arange(LANES, dtype=jnp.int32) // bias_width == spot, jnp.tile(qkv_bias, each), 0.0
    ).astype(BF16)
    bias_block = jnp.zeros((weight_rows, LANES), BF16).at[0].set(bias_row)
    packed = pl.pallas_call(
        pack_kernel,
        out_shape=struct((weight_rows, QKV + LANES + width), BF16),
        compiler_params=params(),
        name="pack",
    )(qkv_weight, bias_block, out_weight, gain_one)
    pieces, plan = gather_blocks(packed, chips, fsdp)

    split = call(
        functools.partial(split_kernel, chips, own, padded),
        struct((2, chips, weight_rows, 2 * padded), BF16),
        [info, gate_up_weight, gain_two],
        name="split",
    )
    w_down = lax.all_gather(down_weight, "fsdp", axis=0, tiled=True)
    arrived = [
        split[other, step] if (other, step) == (0, 0) else send_to(split[other, step], step, other)
        for other in range(2)
        for step in range(chips)
    ]
    aligned = weight_rows % ROW_TILE == 0
    arrived = jnp.stack(arrived)
    numbers = jnp.arange(ctx, dtype=jnp.int32)
    came_from = (numbers + my_ctx) % 2 * chips + (my_ctx // 2 - numbers // 2 + chips) % chips
    if not aligned:
        arrived = picked(arrived, came_from, 0)
    w_wide = lax.all_gather(arrived, "fsdp", axis=0, tiled=False)
    if not aligned:
        w_wide = w_wide.transpose(1, 0, 2, 3).reshape(width, 2 * padded)

    cot_mine = [grad_out]
    for step in range(1, chips):
        cot_mine.append(shift_chip(grad_out, step))
    cot_other = [swap_core(item) for item in cot_mine]

    steps_half = jnp.arange(0, HEAD_DIM, 2).astype(F32)
    inverse = 10000.0 ** (-steps_half / HEAD_DIM)
    turns = positions[0].astype(F32)[:, None] * inverse[None, :]
    cosine = jnp.tile(jnp.cos(turns), (1, 2))
    sine = jnp.concatenate([-jnp.sin(turns), jnp.sin(turns)], axis=-1)
    places = positions[0][:, None]
    count = len(pieces)
    unit_one, queries, own_kv = call(
        functools.partial(project_kernel, plan, chips, fsdp, bias_width, count),
        [struct((rows, width), BF16), struct((rows, WIDTH_Q), BF16), struct((rows, 2 * WIDTH_K), BF16)],
        [info, inputs, cosine, sine] + pieces,
        4,
        4 + count,
        [pltpu.VMEM((width, QKV + LANES), BF16), pltpu.SemaphoreType.DMA((len(plan or [0]),))],
        cost(2 * rows * width * QKV, 2 * width * QKV),
        "project",
    )
    reach = -(-chips // 2)
    kv_blocks, sources = [], []
    for step in range(reach + 1):
        block = own_kv if step == 0 else shift_open(own_kv, step)
        kv_blocks += [block, swap_core(block)]
        sources += [(step, 0), (step, 1)]
    span = len(sources) * rows
    context, middle, unit_two = call(
        functools.partial(attend_kernel, plan, chips, fsdp, count, sources),
        [struct((rows, width), BF16), struct((rows, width), F32), struct((rows, width), BF16)],
        [info, places, queries, inputs] + kv_blocks + pieces,
        4 + len(sources),
        4 + len(sources) + count,
        [pltpu.VMEM((width, width), BF16), pltpu.SemaphoreType.DMA((len(plan or [0]),))],
        cost(4 * rows * span * WIDTH_Q + 2 * rows * width * width, 2 * width * width, rows * span * Q_HEADS),
        "attend",
    )

    units_mine = [unit_two]
    for step in range(1, chips):
        units_mine.append(shift_chip(units_mine[-1], 1))
    units_other = [swap_core(item) for item in units_mine]
    fed = []
    for step in range(chips):
        fed.append(
            call(
                functools.partial(feed_kernel, chips, fsdp, own, padded),
                [struct((rows, width), BF16)] * 4
                + [struct((2 * rows, padded), BF16), struct((2 * rows, 2 * padded), BF16)],
                [info, units_mine[step], units_other[step], cot_mine[step], cot_other[step], w_wide, w_down],
                5,
                7,
                [
                    pltpu.VMEM((width, 2 * padded), BF16),
                    pltpu.VMEM((padded, width), BF16),
                    pltpu.VMEM((2 * rows, width), F32),
                    pltpu.VMEM((2 * rows, width), F32),
                    pltpu.SemaphoreType.DMA((ctx * fsdp + 1,)),
                ],
                cost(2 * 6 * 2 * rows * width * padded, 6 * width * padded),
                "feed",
            )
        )

    def ring(parts):
        sums = [mine + swap_core(other) for mine, other in parts]
        moving = None
        for step in range(1, chips):
            moving = shift_chip(sums[step] if moving is None else sums[step] + moving, 1)
        return sums[0], moving

    own_units, came_units = ring([(item[0], item[1]) for item in fed])

    n_block = 384 if (2 * padded) % 384 == 0 else LANES
    all_units = [item for pair in zip(units_mine, units_other) for item in pair]
    wide_grad = pl.pallas_call(
        functools.partial(wide_grad_kernel, chips, fsdp, ctx),
        out_shape=struct((fsdp, ctx, weight_rows, 2 * padded) if aligned else (width, 2 * padded), BF16),
        grid=(2 * padded // n_block,),
        in_specs=[SMEM_SPEC]
        + [pl.BlockSpec((rows, width), lambda i: (0, 0))] * ctx
        + [pl.BlockSpec((2 * rows, n_block), lambda i: (0, i))] * chips,
        out_specs=pl.BlockSpec((fsdp, ctx, weight_rows, n_block), lambda i: (0, 0, 0, i))
        if aligned
        else pl.BlockSpec((width, n_block), lambda i: (0, i)),
        scratch_shapes=[pltpu.VMEM((width, ctx * rows), BF16), pltpu.VMEM((width, n_block), F32)],
        compiler_params=params(),
        cost_estimate=cost(4 * ctx * rows * width * padded, 8 * width * padded),
        name="wide_grad",
    )(info, *all_units, *[item[5] for item in fed])
    d_block = 512
    all_cots = [item for pair in zip(cot_mine, cot_other) for item in pair]
    down_grad = pl.pallas_call(
        functools.partial(down_grad_kernel, own, chips),
        out_shape=struct((own, width), BF16),
        grid=(width // d_block,),
        in_specs=[pl.BlockSpec((2 * rows, padded), lambda i: (0, 0))] * chips
        + [pl.BlockSpec((rows, d_block), lambda i: (0, i))] * ctx,
        out_specs=pl.BlockSpec((own, d_block), lambda i: (0, i)),
        scratch_shapes=[pltpu.VMEM((padded, ctx * rows), BF16)],
        compiler_params=params(),
        cost_estimate=cost(2 * ctx * rows * width * padded, 4 * width * padded),
        name="down_grad",
    )(*[item[4] for item in fed], *all_cots)
    down_grad = lax.psum_scatter(down_grad, "fsdp", scatter_dimension=0, tiled=True).astype(F32)
    if not aligned:
        slots = jnp.arange(ctx, dtype=jnp.int32)
        goes_to = 2 * ((my_ctx // 2 + slots % chips) % chips) + (my_ctx + slots // chips) % 2
        wide_grad = wide_grad.reshape(ctx, fsdp, weight_rows, 2 * padded).transpose(1, 0, 2, 3)
        wide_grad = picked(wide_grad, goes_to, 1)
    wide_grad = lax.psum_scatter(
        wide_grad.reshape(fsdp * ctx * weight_rows, 2 * padded), "fsdp", scatter_dimension=0, tiled=True
    ).reshape(ctx, weight_rows, 2 * padded)
    back = [
        wide_grad[other * chips + step]
        if (other, step) == (0, 0)
        else send_to(wide_grad[other * chips + step], step, other)
        for other in range(2)
        for step in range(chips)
    ]
    gate_up_grad, norm2_grad = call(
        functools.partial(join_kernel, chips, own, padded),
        [struct(gate_up_weight.shape, F32), struct((weight_rows, 1), F32)],
        [info, jnp.stack(back), gate_up_weight, gain_two],
        name="join",
    )
    own_branch, came_branch = ring([(item[2], item[3]) for item in fed])
    result = (middle + own_branch.astype(F32) + came_branch.astype(F32)).astype(BF16)

    grad_middle, grad_attention, grad_queries, kv_mine, kv_other = call(
        functools.partial(middle_back_kernel, plan, chips, fsdp, count, sources),
        [
            struct((rows, width), F32),
            struct((rows, width), BF16),
            struct((rows, WIDTH_Q), F32),
            struct((reach + 1, rows, 2 * WIDTH_K), BF16),
            struct((reach + 1, rows, 2 * WIDTH_K), BF16),
        ],
        [info, places, queries, own_units, came_units, middle, grad_out] + kv_blocks + pieces,
        7 + len(sources),
        7 + len(sources) + count,
        [pltpu.VMEM((width, width), BF16), pltpu.SemaphoreType.DMA((len(plan or [0]),))],
        cost(10 * rows * span * WIDTH_Q + 2 * rows * width * width, 2 * width * width, rows * span * Q_HEADS),
        "middle_back",
    )
    halves = halves_of(chips, fsdp)
    kept_count = len(halves) if aligned else 1

    def block_shapes(columns):
        if not aligned:
            return [struct((width, columns), BF16)]
        return 2 * [struct((fsdp, len(steps), weight_rows, columns), BF16) for steps, _ in halves]

    outs = call(
        functools.partial(out_grad_kernel, chips, fsdp),
        block_shapes(width),
        [info, grad_attention, context],
        scratch=[pltpu.VMEM((width, width), F32)],
        estimate=cost(2 * rows * width * width, 2 * width * width),
        name="out_grad",
    )
    out_grad = reduce_blocks(outs[:kept_count], outs[kept_count:], chips, fsdp)

    swapped = swap_core(kv_other)
    came = []
    for step in range(1, reach + 1):
        came.append(shift_open(kv_mine[step] + swapped[step], -step))
    outs = call(
        functools.partial(projected_back_kernel, chips, fsdp, bias_width, reach),
        [struct((rows, QKV), BF16)] + block_shapes(QKV + LANES),
        [info, grad_queries, kv_mine[0], swapped[0], cosine, sine, unit_one] + came,
        scratch=[pltpu.VMEM((width, QKV + LANES), F32)],
        estimate=cost(2 * rows * width * QKV, 2 * width * QKV),
        name="projected_back",
    )
    grad_projected = outs[0]
    qkv_sum = reduce_blocks(outs[1 : 1 + kept_count], outs[1 + kept_count :], chips, fsdp)
    bias_row = lax.dynamic_slice_in_dim(qkv_sum[0], QKV + spot * bias_width, bias_width)
    qkv_sum = qkv_sum[:, :QKV]
    input_grad = call(
        functools.partial(input_back_kernel, plan, chips, fsdp, count),
        struct((rows, width), F32),
        [info, grad_projected, inputs, grad_middle] + pieces,
        4,
        4 + count,
        [pltpu.VMEM((width, QKV), BF16), pltpu.SemaphoreType.DMA((len(plan or [0]),))],
        cost(2 * rows * width * QKV, 2 * width * QKV),
        "input_back",
    )
    return (
        result[None],
        input_grad[None],
        jnp.sum(qkv_sum * qkv_weight.astype(F32), axis=1),
        qkv_sum * gain_one,
        bias_row,
        out_grad,
        norm2_grad[:, 0],
        gate_up_grad,
        down_grad,
    )


def solution(mesh):
    rows = P(BOTH, None)
    token = P("fsdp", "ctx", None)
    flat = P(BOTH)
    return jax.shard_map(
        shards,
        mesh=mesh,
        in_specs=(token, P("fsdp", "ctx"), P("fsdp", "ctx"), flat, rows, flat, rows, flat, rows, rows, token),
        out_specs=(token, token, flat, rows, flat, rows, flat, rows, rows),
        check_vma=False,
    )
```

time: 2420 us -> 605 us (0.25)
  waiting for transfers between devices: 1870 us -> 295 us
  matrix products: 184 us -> 0 us
  Pallas kernels: 0 us -> 148 us
  blocking collectives: 85.8 us -> 0 us
  starting transfers between devices: 163 us -> 103 us
  local copies, waits for them, and re-layouts: 51.8 us -> 17.2 us
    reduce_scatter x3 -> x1, waiting for transfers between devices: 918 us -> 0.01 us  [shards(): lax.psum_scatter(wide_grad.reshape(fsdp * ctx * weight_rows, 2 * padded),...]
    unnamed x9 -> x5, waiting for transfers between devices: 471 us -> 0.73 us
    all_gather x4 -> x2, waiting for transfers between devices: 436 us -> 0.01 us  [the longest x1 0.01 us: shards(): w_down = lax.all_gather(down_weight, 'fsdp', axis=0, tiled=True)]
    ppermute x56 -> x85, waiting for transfers between devices: 41.6 us -> 294 us  [the longest x21 114 us: shift_chip(): lax.ppermute(value, 'ctx', [(i, (i + 2 * steps) % count) for i in range(c...]
    dot_general x18 -> x0, matrix products: 184 us -> none  [the longest x4 80.3 us: matmul_tn(): lax.dot_general(left, right, (((0,), (0,)), ((), ())), preferred_element_...]
    pallas_call x0 -> x15, Pallas kernels: none -> 148 us  [the longest x12 121 us: call(): pl.pallas_call(kernel, out_shape=outs, in_specs=specs, out_specs=[VMEM_SP...]
    unnamed x2 -> x0, blocking collectives: 85.8 us -> none
    ppermute x56 -> x85, starting transfers between devices: 162 us -> 103 us  [the longest x21 38.3 us: shift_chip(): lax.ppermute(value, 'ctx', [(i, (i + 2 * steps) % count) for i in range(c...]
  transfers between devices with their start and end apart: 64 -> 89, of which waited for: 34 -> 34; matrix products, arithmetic and copies ran while one was open for 9% -> 4% of each run, Pallas kernels for 0% -> 20%
where the time goes in v1:
time: 605 us; the launch traced here: 595 us
  waiting for transfers between devices  295 us (49%)
  Pallas kernels  148 us (24%)
  starting transfers between devices  103 us (17%)
  other arithmetic  17.6 us (3%)
  local copies, waits for them, and re-layouts  17.2 us (3%)
  between operations  15.2 us (3%)
    pallas_call x12, Pallas kernels, call(): pl.pallas_call(kernel, out_shape=outs, in_specs=specs, out_specs=[VMEM_SP...  121 us
    ppermute x21, waiting for transfers between devices, shift_chip(): lax.ppermute(value, 'ctx', [(i, (i + 2 * steps) % count) for i in range(c...  114 us
    ppermute x14, waiting for transfers between devices, swap_fsdp(): return lax.ppermute(value, 'fsdp', [(i, i ^ bit) for i in range(count)])  102 us
    ppermute x14, waiting for transfers between devices, send_to(): lax.ppermute(value, 'ctx', [(i, (i + 2 * steps) % count ^ other) for i in...  66.5 us
    ppermute x21, starting transfers between devices, shift_chip(): lax.ppermute(value, 'ctx', [(i, (i + 2 * steps) % count) for i in range(c...  38.3 us
    ppermute x14, starting transfers between devices, send_to(): lax.ppermute(value, 'ctx', [(i, (i + 2 * steps) % count ^ other) for i in...  28.6 us
    ppermute x14, starting transfers between devices, swap_fsdp(): return lax.ppermute(value, 'fsdp', [(i, i ^ bit) for i in range(count)])  16.9 us
    pallas_call x1, Pallas kernels, shards(): pl.pallas_call(functools.partial(wide_grad_kernel, chips, fsdp, ctx), out...  16.3 us
  transfers between devices with their start and end apart: 89, of which 34 were waited for; matrix products, arithmetic and copies ran while one was open for 4% of the time, Pallas kernels for 20%

profile of v1, /device:TPU:0, one launch (start us, length us, event | category | flops | bytes accessed | tf_op | source)
XLA Modules:
  0.0 595.4 jit_solution(5880419300918744146)
XLA Ops:
  24.8 16.2 %collective-permute-done.24 = bf16[48,2304]{1,0:T(8,128)(2,1)S(1)} collective-permute-done((bf16[48,2304]{1,0:T(8,128)(2,1)S(1)}, bf16[48,2304]{1,0:T(8,128)(2,1)S(1)}, u32[]{:S(2)}, u32[]{:S(2)}) %collective-permute-start.24) | collective-permute-done | bytes 221216 | tf_op jit(solution)/shard_map/ppermute | solution.py:73
  47.5 9.9 %collective-permute-done.25 = bf16[48,2304]{1,0:T(8,128)(2,1)S(1)} collective-permute-done((bf16[48,2304]{1,0:T(8,128)(2,1)S(1)}, bf16[48,2304]{1,0:T(8,128)(2,1)S(1)}, u32[]{:S(2)}, u32[]{:S(2)}) %collective-permute-start.25) | collective-permute-done | bytes 221216 | tf_op jit(solution)/shard_map/ppermute | solution.py:73
  73.2 9.4 %collective-permute-done = bf16[48,3712]{1,0:T(8,128)(2,1)S(1)} collective-permute-done((bf16[48,3712]{1,0:T(8,128)(2,1)}, bf16[48,3712]{1,0:T(8,128)(2,1)S(1)}, u32[]{:S(2)}, u32[]{:S(2)}) %collective-permute-start) | collective-permute-done | bytes 356384 | tf_op jit(solution)/shard_map/ppermute | solution.py:62
  86.8 15.5 %collective-permute-done.8 = bf16[48,3712]{1,0:T(8,128)(2,1)S(1)} collective-permute-done((bf16[48,3712]{1,0:T(8,128)(2,1)}, bf16[48,3712]{1,0:T(8,128)(2,1)S(1)}, u32[]{:S(2)}, u32[]{:S(2)}) %collective-permute-start.8) | collective-permute-done | bytes 356384 | tf_op jit(solution)/shard_map/ppermute | solution.py:62
  105.5 8.1 %collective-permute-done.4.refs_4_.refs_10_ = bf16[96,3712]{1,0:T(8,128)(2,1)S(1)} collective-permute-done((bf16[96,3712]{1,0:T(8,128)(2,1)S(1)}, bf16[96,3712]{1,0:T(8,128)(2,1)S(1)}, u32[]{:S(2)}, u32[]{:S(2)}) %collective-permute-start.4) | collective-permute-done | bytes 712736 | tf_op jit(solution)/shard_map/ppermute | solution.py:80
  114.7 24.8 %collective-permute-done.11.refs_10_.refs_16_ = bf16[96,3712]{1,0:T(8,128)(2,1)} collective-permute-done((bf16[96,3712]{1,0:T(8,128)(2,1)S(1)}, bf16[96,3712]{1,0:T(8,128)(2,1)}, u32[]{:S(2)}, u32[]{:S(2)}) %collective-permute-start.11) | collective-permute-done | bytes 712736 | tf_op jit(solution)/shard_map/ppermute | solution.py:80
  141.6 26.9 %collective-permute-done.6.refs_6_.refs_12_ = bf16[96,3712]{1,0:T(8,128)(2,1)} collective-permute-done((bf16[96,3712]{1,0:T(8,128)(2,1)S(1)}, bf16[96,3712]{1,0:T(8,128)(2,1)}, u32[]{:S(2)}, u32[]{:S(2)}) %collective-permute-start.6) | collective-permute-done | bytes 712736 | tf_op jit(solution)/shard_map/ppermute | solution.py:80
  174.2 6.9 %project.1 = (bf16[128,1536]{1,0:T(8,128)(2,1)}, bf16[128,1536]{1,0:T(8,128)(2,1)}, bf16[128,512]{1,0:T(8,128)(2,1)}) custom-call(s32[2]{0:T(128)} %pad_add_fusion.info_ref, bf16[128,1536]{1,0:T(8,128)(2,1)} %bitcast.102, f32[128,128]{1,0:T(8,128)} %copy.43.cos_ref, f32[128,128]{1,0:T(8,128)} %pad_maximum_fusion.1.sin_ref, bf16[96,3712]{1,0:T(8,128)(2,1)} %copy-done, ...), custom_call_target="tpu_custom_call" | custom-call | flops 805306368 | bytes 6291456 | tf_op jit(solution)/shard_map/project/pallas_call | solution.py:551
  181.0 9.1 %collective-permute-start.20 = (bf16[128,512]{1,0:T(8,128)(2,1)}, bf16[128,512]{1,0:T(8,128)(2,1)S(1)}, u32[]{:S(2)}, u32[]{:S(2)}) collective-permute-start(bf16[128,512]{1,0:T(8,128)(2,1)} %get-tuple-element.68.refs_0_), channel_id=1, source_target_pairs={{0,16},{4,20},{8,24},{12,28},{1,17},{5,21},{9,25},{13,29},{2,18},{... | collective-permute-start | bytes 393224 | tf_op jit(solution)/shard_map/ppermute | solution.py:68
  200.2 9.5 %attend.1 = (bf16[128,1536]{1,0:T(8,128)(2,1)}, f32[128,1536]{1,0:T(8,128)}, bf16[128,1536]{1,0:T(8,128)(2,1)}) custom-call(s32[2]{0:T(128)} %pad_add_fusion.info_ref, s32[128,1]{1,0:T(8,128)} %copy.44.place_ref, bf16[128,1536]{1,0:T(8,128)(2,1)} %get-tuple-element.67.q_ref, bf16[128,1536]{1,0:T(8,128)(2,1)} %bitcast.103, ...), custom_call_target="tpu_custom_call" | custom-call | flops 1207959552 | bytes 4718592 | tf_op jit(solution)/shard_map/attend/pallas_call | solution.py:551
  214.1 9.8 %collective-permute-done.32.x_mine.refs_2_ = bf16[128,1536]{1,0:T(8,128)(2,1)S(1)} collective-permute-done((bf16[128,1536]{1,0:T(8,128)(2,1)}, bf16[128,1536]{1,0:T(8,128)(2,1)S(1)}, u32[]{:S(2)}, u32[]{:S(2)}) %collective-permute-start.32) | collective-permute-done | bytes 393248 | tf_op jit(solution)/shard_map/ppermute | solution.py:62
  224.0 16.8 %collective-permute-done.40.c_mine.refs_8_ = bf16[128,1536]{1,0:T(8,128)(2,1)S(1)} collective-permute-done((bf16[128,1536]{1,0:T(8,128)(2,1)S(1)}, bf16[128,1536]{1,0:T(8,128)(2,1)S(1)}, u32[]{:S(2)}, u32[]{:S(2)}) %collective-permute-start.40) | collective-permute-done | bytes 393248 | tf_op jit(solution)/shard_map/ppermute | solution.py:62
  241.4 7.1 %collective-permute-done.33.x_mine.refs_4_ = bf16[128,1536]{1,0:T(8,128)(2,1)S(1)} collective-permute-done((bf16[128,1536]{1,0:T(8,128)(2,1)S(1)}, bf16[128,1536]{1,0:T(8,128)(2,1)S(1)}, u32[]{:S(2)}, u32[]{:S(2)}) %collective-permute-start.33) | collective-permute-done | bytes 393248 | tf_op jit(solution)/shard_map/ppermute | solution.py:62
  248.5 18.2 %collective-permute-start.34 = (bf16[128,1536]{1,0:T(8,128)(2,1)S(1)}, bf16[128,1536]{1,0:T(8,128)(2,1)}, u32[]{:S(2)}, u32[]{:S(2)}) collective-permute-start(bf16[128,1536]{1,0:T(8,128)(2,1)S(1)} %collective-permute-done.33.x_mine.refs_4_), channel_id=1, source_target_pairs={{0,8},{4,12},{8,16},{12,20},{16,24},{20,28},{24,0},{28,4},{1,9},{5... | collective-permute-start | bytes 1179656 | tf_op jit(solution)/shard_map/ppermute | solution.py:62
  266.8 14.9 %feed.7 = (bf16[128,1536]{1,0:T(8,128)(2,1)}, bf16[128,1536]{1,0:T(8,128)(2,1)}, bf16[128,1536]{1,0:T(8,128)(2,1)}, bf16[128,1536]{1,0:T(8,128)(2,1)}, bf16[256,...) custom-call(s32[2]{0:T(128)} %pad_add_fusion.info_ref, bf16[128,1536]{1,0:T(8,128)(2,1)} %copy-done.34, ...), custom_call_target="tpu_custom_call" | custom-call | flops 5435817984 | bytes 10616832 | tf_op jit(solution)/shard_map/feed/pallas_call | solution.py:551
  282.3 15.1 %feed.6 = (bf16[128,1536]{1,0:T(8,128)(2,1)}, bf16[128,1536]{1,0:T(8,128)(2,1)}, bf16[128,1536]{1,0:T(8,128)(2,1)}, bf16[128,1536]{1,0:T(8,128)(2,1)}, bf16[256,...) custom-call(s32[2]{0:T(128)} %pad_add_fusion.info_ref, bf16[128,1536]{1,0:T(8,128)(2,1)} %copy-done.38, ...), custom_call_target="tpu_custom_call" | custom-call | flops 5435817984 | bytes 10616832 | tf_op jit(solution)/shard_map/feed/pallas_call | solution.py:551
  298.2 14.8 %feed.5 = (bf16[128,1536]{1,0:T(8,128)(2,1)}, bf16[128,1536]{1,0:T(8,128)(2,1)}, bf16[128,1536]{1,0:T(8,128)(2,1)}, bf16[128,1536]{1,0:T(8,128)(2,1)}, bf16[256,...) custom-call(s32[2]{0:T(128)} %pad_add_fusion.info_ref, bf16[128,1536]{1,0:T(8,128)(2,1)} %collective-permute-done.34.x_mine.refs_6_, ...), custom_call_target="tpu_custom_call" | custom-call | flops 5435817984 | bytes 10616832 | tf_op jit(solution)/shard_map/feed/pallas_call | solution.py:551
  313.8 15.3 %feed.4 = (bf16[128,1536]{1,0:T(8,128)(2,1)}, bf16[128,1536]{1,0:T(8,128)(2,1)}, bf16[128,1536]{1,0:T(8,128)(2,1)}, bf16[128,1536]{1,0:T(8,128)(2,1)}, bf16[256,...) custom-call(s32[2]{0:T(128)} %pad_add_fusion.info_ref, bf16[128,1536]{1,0:T(8,128)(2,1)} %get-tuple-element.70.x_mine.refs_0_, ...), custom_call_target="tpu_custom_call" | custom-call | flops 5435817984 | bytes 10616832 | tf_op jit(solution)/shard_map/feed/pallas_call | solution.py:551
  329.1 8.3 %down_grad.1 = bf16[1120,1536]{1,0:T(8,128)(2,1)} custom-call(bf16[256,1152]{1,0:T(8,128)(2,1)} %get-tuple-element.109.refs_0_, bf16[256,1152]{1,0:T(8,128)(2,1)} %get-tuple-element.110.refs_1_, bf16[256,1152]{1,0:T(8,128)(2,1)} %get-tuple-element.111.refs_2_, bf16[256,1152]{1,0:T(8,128)(2,1)} %get-tuple-element.112.refs_3_, bf16[128,1536]{1,0:T(8,128)(2,1)} %bitcast.107, ...), custom_call_target="tpu_custom_call" | custom-call | flops 3623878656 | bytes 7077888 | tf_op jit(solution)/shard_map/down_grad/pallas_call | solution.py:722
  337.5 16.3 %wide_grad.1 = bf16[4,8,48,2304]{3,2,1,0:T(8,128)(2,1)} custom-call(s32[2]{0:T(128)} %pad_add_fusion.info_ref, bf16[128,1536]{1,0:T(8,128)(2,1)} %get-tuple-element.70.x_mine.refs_0_, bf16[128,1536]{1,0:T(8,128)(2,1)} %copy-done.46, bf16[128,1536]{1,0:T(8,128)(2,1)} %copy-done.34, bf16[128,1536]{1,0:T(8,128)(2,1)} %copy-done.39, ...), custom_call_target="tpu_custom_call" | custom-call | flops 7247757312 | bytes 14155776 | tf_op jit(solution)/shard_map/wide_grad/pallas_call | solution.py:705
  358.0 11.7 %collective-permute-done.54 = bf16[128,1536]{1,0:T(8,128)(2,1)S(1)} collective-permute-done((bf16[128,1536]{1,0:T(8,128)(2,1)S(1)}, bf16[128,1536]{1,0:T(8,128)(2,1)S(1)}, u32[]{:S(2)}, u32[]{:S(2)}) %collective-permute-start.54) | collective-permute-done | bytes 393248 | tf_op jit(solution)/shard_map/ppermute | solution.py:62
  371.5 12.2 %collective-permute-done.55 = bf16[128,1536]{1,0:T(8,128)(2,1)S(1)} collective-permute-done((bf16[128,1536]{1,0:T(8,128)(2,1)S(1)}, bf16[128,1536]{1,0:T(8,128)(2,1)S(1)}, u32[]{:S(2)}, u32[]{:S(2)}) %collective-permute-start.55) | collective-permute-done | bytes 393248 | tf_op jit(solution)/shard_map/ppermute | solution.py:62
  383.8 8.3 %collective-permute-done.47 = bf16[128,1536]{1,0:T(8,128)(2,1)S(1)} collective-permute-done((bf16[128,1536]{1,0:T(8,128)(2,1)S(1)}, bf16[128,1536]{1,0:T(8,128)(2,1)S(1)}, u32[]{:S(2)}, u32[]{:S(2)}) %collective-permute-start.47) | collective-permute-done | bytes 393248 | tf_op jit(solution)/shard_map/ppermute | solution.py:62
  392.4 8.1 %collective-permute-done.56.came_ref = bf16[128,1536]{1,0:T(8,128)(2,1)S(1)} collective-permute-done((bf16[128,1536]{1,0:T(8,128)(2,1)S(1)}, bf16[128,1536]{1,0:T(8,128)(2,1)S(1)}, u32[]{:S(2)}, u32[]{:S(2)}) %collective-permute-start.56) | collective-permute-done | bytes 393248 | tf_op jit(solution)/shard_map/ppermute | solution.py:62
  401.3 14.3 %middle_back.1 = (f32[128,1536]{1,0:T(8,128)}, bf16[128,1536]{1,0:T(8,128)(2,1)}, f32[128,1536]{1,0:T(8,128)}, bf16[3,128,512]{2,1,0:T(8,128)(2,1)}, bf16[3,128,512]{2,1,0:T(8,128)(2,1)}) custom-call(s32[2]{0:T(128)} %pad_add_fusion.info_ref, s32[128,1]{1,0:T(8,128)} %copy.44.place_ref, bf16[128,1536]{1,0:T(8,128)(2,1)} %get-tuple-element.67.q_ref, ...), custom_call_target="tpu_custom_call" | custom-call | flops 2113929216 | bytes 4718592 | tf_op jit(solution)/shard_map/middle_back/pallas_call | solution.py:551
  449.0 7.9 %input_back.1 = f32[128,1536]{1,0:T(8,128)} custom-call(s32[2]{0:T(128)} %pad_add_fusion.info_ref, bf16[128,2048]{1,0:T(8,128)(2,1)} %get-tuple-element.91.gp_ref, bf16[128,1536]{1,0:T(8,128)(2,1)} %bitcast.104, f32[128,1536]{1,0:T(8,128)} %get-tuple-element.92.middle_ref, bf16[96,3712]{1,0:T(8,128)(2,1)} %copy-done, bf16[96,3712]{1,0:T(8,128)(2,1)} %copy-done.4, ...), custom_call_target="tpu_custom_call" | custom-call | flops 805306368 | bytes 6291456 | tf_op jit(solution)/shard_map/input_back/pallas_call | solution.py:551
  457.8 10.0 %collective-permute-done.74 = bf16[2,2,48,1536]{3,2,1,0:T(8,128)(2,1)S(1)} collective-permute-done((bf16[2,2,48,1536]{3,2,1,0:T(8,128)(2,1)S(1)}, bf16[2,2,48,1536]{3,2,1,0:T(8,128)(2,1)S(1)}, u32[]{:S(2)}, u32[]{:S(2)}) %collective-permute-start.74) | collective-permute-done | bytes 589856 | tf_op jit(solution)/shard_map/ppermute | solution.py:80
  469.3 8.5 %collective-permute-done.71 = bf16[1,2,48,1536]{3,2,1,0:T(8,128)(2,1)S(1)} collective-permute-done((bf16[1,2,48,1536]{3,2,1,0:T(8,128)(2,1)S(1)}, bf16[1,2,48,1536]{3,2,1,0:T(8,128)(2,1)S(1)}, u32[]{:S(2)}, u32[]{:S(2)}) %collective-permute-start.71) | collective-permute-done | bytes 294944 | tf_op jit(solution)/shard_map/ppermute | solution.py:80
  485.3 12.5 %collective-permute-done.61 = bf16[2,2,48,2176]{3,2,1,0:T(8,128)(2,1)S(1)} collective-permute-done((bf16[2,2,48,2176]{3,2,1,0:T(8,128)(2,1)S(1)}, bf16[2,2,48,2176]{3,2,1,0:T(8,128)(2,1)S(1)}, u32[]{:S(2)}, u32[]{:S(2)}) %collective-permute-start.61) | collective-permute-done | bytes 835616 | tf_op jit(solution)/shard_map/ppermute | solution.py:80
  540.5 16.2 %collective-permute-done.78 = bf16[48,2304]{1,0:T(8,128)(2,1)S(1)} collective-permute-done((bf16[48,2304]{1,0:T(8,128)(2,1)S(1)}, bf16[48,2304]{1,0:T(8,128)(2,1)S(1)}, u32[]{:S(2)}, u32[]{:S(2)}) %collective-permute-start.78) | collective-permute-done | bytes 221216 | tf_op jit(solution)/shard_map/ppermute | solution.py:73
  561.4 10.5 %collective-permute-done.79 = bf16[48,2304]{1,0:T(8,128)(2,1)S(1)} collective-permute-done((bf16[48,2304]{1,0:T(8,128)(2,1)S(1)}, bf16[48,2304]{1,0:T(8,128)(2,1)S(1)}, u32[]{:S(2)}, u32[]{:S(2)}) %collective-permute-start.79) | collective-permute-done | bytes 221216 | tf_op jit(solution)/shard_map/ppermute | solution.py:73
  572.2 6.9 %collective-permute-done.80 = bf16[48,2304]{1,0:T(8,128)(2,1)S(1)} collective-permute-done((bf16[48,2304]{1,0:T(8,128)(2,1)S(1)}, bf16[48,2304]{1,0:T(8,128)(2,1)S(1)}, u32[]{:S(2)}, u32[]{:S(2)}) %collective-permute-start.80) | collective-permute-done | bytes 221216 | tf_op jit(solution)/shard_map/ppermute | solution.py:73
  (347 shorter events, 180.2 us)
Async XLA Ops:
  7.2 259.6 %all-gather.4.cloned.1.call-start = ((), (), s32[]{:S(2)}) async-start(), calls=%async_computation.2 | async-start | bytes 4300800 | tf_op jit(solution)/shard_map/all_gather | solution.py:612
  7.9 258.8 %all-gather.6.cloned.1.call-start = ((), (), s32[]{:S(2)}) async-start(), calls=%async_computation.4 | async-start | bytes 8847360 | tf_op jit(solution)/shard_map/all_gather | solution.py:624
  15.4 49.3 %collective-permute-start.30 = (bf16[48,2304]{1,0:T(8,128)(2,1)S(1)}, bf16[48,2304]{1,0:T(8,128)(2,1)S(1)}, u32[]{:S(2)}, u32[]{:S(2)}) collective-permute-start(bf16[48,2304]{1,0:T(8,128)(2,1)S(1)} %get-tuple-element.120), channel_id=1, source_target_pairs={{0,28},{4,24},{8,4},{12,0},{16,12},{20,8},{24,20},{28,16},{1,29},{... | collective-permute-start | bytes 663560 | tf_op jit(solution)/shard_map/ppermute | solution.py:73
  20.0 44.8 %collective-permute-start.29 = (bf16[48,2304]{1,0:T(8,128)(2,1)S(1)}, bf16[48,2304]{1,0:T(8,128)(2,1)S(1)}, u32[]{:S(2)}, u32[]{:S(2)}) collective-permute-start(bf16[48,2304]{1,0:T(8,128)(2,1)S(1)} %get-tuple-element.121), channel_id=1, source_target_pairs={{0,20},{4,16},{8,28},{12,24},{16,4},{20,0},{24,12},{28,8},{1,21},{... | collective-permute-start | bytes 663560 | tf_op jit(solution)/shard_map/ppermute | solution.py:73
  20.0 44.7 %collective-permute-start.28 = (bf16[48,2304]{1,0:T(8,128)(2,1)S(1)}, bf16[48,2304]{1,0:T(8,128)(2,1)S(1)}, u32[]{:S(2)}, u32[]{:S(2)}) collective-permute-start(bf16[48,2304]{1,0:T(8,128)(2,1)S(1)} %get-tuple-element.122), channel_id=1, source_target_pairs={{0,12},{4,8},{8,20},{12,16},{16,28},{20,24},{24,4},{28,0},{1,13},{... | collective-permute-start | bytes 663560 | tf_op jit(solution)/shard_map/ppermute | solution.py:73
  20.9 43.8 %collective-permute-start.27 = (bf16[48,2304]{1,0:T(8,128)(2,1)S(1)}, bf16[48,2304]{1,0:T(8,128)(2,1)S(1)}, u32[]{:S(2)}, u32[]{:S(2)}) collective-permute-start(bf16[48,2304]{1,0:T(8,128)(2,1)S(1)} %get-tuple-element.123), channel_id=1, source_target_pairs={{0,4},{4,0},{8,12},{12,8},{16,20},{20,16},{24,28},{28,24},{1,5},{5... | collective-permute-start | bytes 663560 | tf_op jit(solution)/shard_map/ppermute | solution.py:73
  66.0 461.0 %reduce-scatter.7.cloned.1.call-start = ((), (), s32[]{:S(2)}) async-start(), calls=%async_computation.5 | async-start | bytes 4300800
  69.4 32.9 %collective-permute-start.9 = (bf16[48,3712]{1,0:T(8,128)(2,1)}, bf16[48,3712]{1,0:T(8,128)(2,1)S(1)}, u32[]{:S(2)}, u32[]{:S(2)}) collective-permute-start(bf16[48,3712]{1,0:T(8,128)(2,1)} %pack.1), channel_id=1, source_target_pairs={{0,24},{4,28},{8,0},{12,4},{16,8},{20,12},{24,16},{28,20},{1,25},{... | collective-permute-start | bytes 1069064 | tf_op jit(solution)/shard_map/ppermute | solution.py:62
  83.7 29.8 %collective-permute-start.4 = (bf16[96,3712]{1,0:T(8,128)(2,1)S(1)}, bf16[96,3712]{1,0:T(8,128)(2,1)S(1)}, u32[]{:S(2)}, u32[]{:S(2)}) collective-permute-start(bf16[96,3712]{1,0:T(8,128)(2,1)S(1)} %pad_maximum_fusion.refs_0_.refs_6_), channel_id=1, source_target_pairs={{0,2},{1,3},{2,0},{3,1},{4,6},{5,7},{6,4},{7,5},{8,10},{9,11},{10,... | collective-permute-start | bytes 2138120 | tf_op jit(solution)/shard_map/ppermute | solution.py:80
  102.4 37.1 %collective-permute-start.11 = (bf16[96,3712]{1,0:T(8,128)(2,1)S(1)}, bf16[96,3712]{1,0:T(8,128)(2,1)}, u32[]{:S(2)}, u32[]{:S(2)}) collective-permute-start(bf16[96,3712]{1,0:T(8,128)(2,1)S(1)} %constant_dynamic-update-slice_fusion.refs_8_.refs_14_), channel_id=1, source_target_pairs={{0,2},{1,3},{2,0},{3,1},{4,6},{5,7},{6,4},{7,5},{8,10},{9,11},{10,... | collective-permute-start | bytes 2138120 | tf_op jit(solution)/shard_map/ppermute | solution.py:80
  104.0 37.0 %collective-permute-start.13 = (bf16[96,3712]{1,0:T(8,128)(2,1)S(1)}, bf16[96,3712]{1,0:T(8,128)(2,1)}, u32[]{:S(2)}, u32[]{:S(2)}) collective-permute-start(bf16[96,3712]{1,0:T(8,128)(2,1)S(1)} %constant_dynamic-update-slice_fusion.refs_8_.refs_14_), channel_id=1, source_target_pairs={{0,1},{1,0},{2,3},{3,2},{4,5},{5,4},{6,7},{7,6},{8,9},{9,8},{10,11... | collective-permute-start | bytes 2138120 | tf_op jit(solution)/shard_map/ppermute | solution.py:80
  114.1 54.4 %collective-permute-start.6 = (bf16[96,3712]{1,0:T(8,128)(2,1)S(1)}, bf16[96,3712]{1,0:T(8,128)(2,1)}, u32[]{:S(2)}, u32[]{:S(2)}) collective-permute-start(bf16[96,3712]{1,0:T(8,128)(2,1)S(1)} %collective-permute-done.2.refs_2_.refs_8_), channel_id=1, source_target_pairs={{0,2},{1,3},{2,0},{3,1},{4,6},{5,7},{6,4},{7,5},{8,10},{9,11},{10,... | collective-permute-start | bytes 2138120 | tf_op jit(solution)/shard_map/ppermute | solution.py:80
  139.5 32.1 %collective-permute-start.15 = (bf16[96,3712]{1,0:T(8,128)(2,1)}, bf16[96,3712]{1,0:T(8,128)(2,1)}, u32[]{:S(2)}, u32[]{:S(2)}) collective-permute-start(bf16[96,3712]{1,0:T(8,128)(2,1)} %collective-permute-done.11.refs_10_.refs_16_), channel_id=1, source_target_pairs={{0,1},{1,0},{2,3},{3,2},{4,5},{5,4},{6,7},{7,6},{8,9},{9,8},{10,11... | collective-permute-start | bytes 2138120 | tf_op jit(solution)/shard_map/ppermute | solution.py:80
  141.0 32.5 %collective-permute-start.3 = (bf16[96,3712]{1,0:T(8,128)(2,1)S(1)}, bf16[96,3712]{1,0:T(8,128)(2,1)}, u32[]{:S(2)}, u32[]{:S(2)}) collective-permute-start(bf16[96,3712]{1,0:T(8,128)(2,1)S(1)} %collective-permute-done.2.refs_2_.refs_8_), channel_id=1, source_target_pairs={{0,4},{4,0},{8,12},{12,8},{16,20},{20,16},{24,28},{28,24},{1,5},{5... | collective-permute-start | bytes 2138120 | tf_op jit(solution)/shard_map/ppermute | solution.py:57
  141.0 32.5 %collective-permute-start.12 = (bf16[96,3712]{1,0:T(8,128)(2,1)}, bf16[96,3712]{1,0:T(8,128)(2,1)}, u32[]{:S(2)}, u32[]{:S(2)}) collective-permute-start(bf16[96,3712]{1,0:T(8,128)(2,1)} %collective-permute-done.11.refs_10_.refs_16_), channel_id=1, source_target_pairs={{0,4},{4,0},{8,12},{12,8},{16,20},{20,16},{24,28},{28,24},{1,5},{5... | collective-permute-start | bytes 2138120 | tf_op jit(solution)/shard_map/ppermute | solution.py:57
  141.5 32.0 %collective-permute-start.14 = (bf16[96,3712]{1,0:T(8,128)(2,1)}, bf16[96,3712]{1,0:T(8,128)(2,1)}, u32[]{:S(2)}, u32[]{:S(2)}) collective-permute-start(bf16[96,3712]{1,0:T(8,128)(2,1)} %collective-permute-done.13.refs_12_.refs_18_), channel_id=1, source_target_pairs={{0,4},{4,0},{8,12},{12,8},{16,20},{20,16},{24,28},{28,24},{1,5},{5... | collective-permute-start | bytes 2138120 | tf_op jit(solution)/shard_map/ppermute | solution.py:57
  211.3 29.5 %collective-permute-start.40 = (bf16[128,1536]{1,0:T(8,128)(2,1)S(1)}, bf16[128,1536]{1,0:T(8,128)(2,1)S(1)}, u32[]{:S(2)}, u32[]{:S(2)}) collective-permute-start(bf16[128,1536]{1,0:T(8,128)(2,1)S(1)} %bitcast.110), channel_id=1, source_target_pairs={{0,16},{4,20},{8,24},{12,28},{16,0},{20,4},{24,8},{28,12},{1,17},{... | collective-permute-start | bytes 1179656 | tf_op jit(solution)/shard_map/ppermute | solution.py:62
  240.8 72.2 %collective-permute-start.23 = (bf16[128,1536]{1,0:T(8,128)(2,1)S(1)}, bf16[128,1536]{1,0:T(8,128)(2,1)}, u32[]{:S(2)}, u32[]{:S(2)}) collective-permute-start(bf16[128,1536]{1,0:T(8,128)(2,1)S(1)} %bitcast.112), channel_id=1, source_target_pairs={{0,4},{4,0},{8,12},{12,8},{16,20},{20,16},{24,28},{28,24},{1,5},{5... | collective-permute-start | bytes 1179656 | tf_op jit(solution)/shard_map/ppermute | solution.py:57
  240.8 40.9 %collective-permute-start.41 = (bf16[128,1536]{1,0:T(8,128)(2,1)S(1)}, bf16[128,1536]{1,0:T(8,128)(2,1)}, u32[]{:S(2)}, u32[]{:S(2)}) collective-permute-start(bf16[128,1536]{1,0:T(8,128)(2,1)S(1)} %collective-permute-done.40.c_mine.refs_8_), channel_id=1, source_target_pairs={{0,4},{4,0},{8,12},{12,8},{16,20},{20,16},{24,28},{28,24},{1,5},{5... | collective-permute-start | bytes 1179656 | tf_op jit(solution)/shard_map/ppermute | solution.py:57
  241.3 56.0 %collective-permute-start.37 = (bf16[128,1536]{1,0:T(8,128)(2,1)S(1)}, bf16[128,1536]{1,0:T(8,128)(2,1)}, u32[]{:S(2)}, u32[]{:S(2)}) collective-permute-start(bf16[128,1536]{1,0:T(8,128)(2,1)S(1)} %collective-permute-done.36.c_mine.refs_10_), channel_id=1, source_target_pairs={{0,4},{4,0},{8,12},{12,8},{16,20},{20,16},{24,28},{28,24},{1,5},{5... | collective-permute-start | bytes 1179656 | tf_op jit(solution)/shard_map/ppermute | solution.py:57
  248.5 33.8 %collective-permute-start.39 = (bf16[128,1536]{1,0:T(8,128)(2,1)S(1)}, bf16[128,1536]{1,0:T(8,128)(2,1)}, u32[]{:S(2)}, u32[]{:S(2)}) collective-permute-start(bf16[128,1536]{1,0:T(8,128)(2,1)S(1)} %collective-permute-done.33.x_mine.refs_4_), channel_id=1, source_target_pairs={{0,4},{4,0},{8,12},{12,8},{16,20},{20,16},{24,28},{28,24},{1,5},{5... | collective-permute-start | bytes 1179656 | tf_op jit(solution)/shard_map/ppermute | solution.py:57
  248.5 33.4 %collective-permute-start.34 = (bf16[128,1536]{1,0:T(8,128)(2,1)S(1)}, bf16[128,1536]{1,0:T(8,128)(2,1)}, u32[]{:S(2)}, u32[]{:S(2)}) collective-permute-start(bf16[128,1536]{1,0:T(8,128)(2,1)S(1)} %collective-permute-done.33.x_mine.refs_4_), channel_id=1, source_target_pairs={{0,8},{4,12},{8,16},{12,20},{16,24},{20,28},{24,0},{28,4},{1,9},{5... | collective-permute-start | bytes 1179656 | tf_op jit(solution)/shard_map/ppermute | solution.py:62
  281.7 31.3 %collective-permute-start.22 = (bf16[128,1536]{1,0:T(8,128)(2,1)S(1)}, bf16[128,1536]{1,0:T(8,128)(2,1)S(1)}, u32[]{:S(2)}, u32[]{:S(2)}) collective-permute-start(bf16[128,1536]{1,0:T(8,128)(2,1)S(1)} %copy-done.33), channel_id=1, source_target_pairs={{0,4},{4,0},{8,12},{12,8},{16,20},{20,16},{24,28},{28,24},{1,5},{5... | collective-permute-start | bytes 1179656 | tf_op jit(solution)/shard_map/ppermute | solution.py:57
  337.5 192.2 %reduce-scatter.5.cloned.1.call-start = ((), (), s32[]{:S(2)}) async-start(), calls=%async_computation.3 | async-start | bytes 8847360 | tf_op jit(solution)/shard_map/reduce_scatter | solution.py:740
  370.0 51.2 %collective-permute-start.38 = (bf16[128,1536]{1,0:T(8,128)(2,1)S(1)}, bf16[128,1536]{1,0:T(8,128)(2,1)S(1)}, u32[]{:S(2)}, u32[]{:S(2)}) collective-permute-start(bf16[128,1536]{1,0:T(8,128)(2,1)S(1)} %copy-done.31), channel_id=1, source_target_pairs={{0,4},{4,0},{8,12},{12,8},{16,20},{20,16},{24,28},{28,24},{1,5},{5... | collective-permute-start | bytes 1179656 | tf_op jit(solution)/shard_map/ppermute | solution.py:57
  448.5 31.3 %collective-permute-start.64 = (bf16[4,2,48,2176]{3,2,1,0:T(8,128)(2,1)}, bf16[4,2,48,2176]{3,2,1,0:T(8,128)(2,1)S(1)}, u32[]{:S(2)}, u32[]{:S(2)}) collective-permute-start(bf16[4,2,48,2176]{3,2,1,0:T(8,128)(2,1)} %get-tuple-element.96), channel_id=1, source_target_pairs={{0,4},{4,0},{8,12},{12,8},{16,20},{20,16},{24,28},{28,24},{1,5},{5... | collective-permute-start | bytes 5013512 | tf_op jit(solution)/shard_map/ppermute | solution.py:57
  477.8 35.3 %collective-permute-start.72 = (bf16[48,1536]{1,0:T(8,128)(2,1)S(1)}, bf16[48,1536]{1,0:T(8,128)(2,1)S(1)}, u32[]{:S(2)}, u32[]{:S(2)}) collective-permute-start(bf16[48,1536]{1,0:T(8,128)(2,1)S(1)} %slice_bitcast_fusion.15), channel_id=1, source_target_pairs={{0,8},{4,12},{8,16},{12,20},{16,24},{20,28},{24,0},{28,4},{1,9},{5... | collective-permute-start | bytes 442376 | tf_op jit(solution)/shard_map/ppermute | solution.py:62
  481.1 32.3 %collective-permute-start.76 = (bf16[48,1536]{1,0:T(8,128)(2,1)S(1)}, bf16[48,1536]{1,0:T(8,128)(2,1)S(1)}, u32[]{:S(2)}, u32[]{:S(2)}) collective-permute-start(bf16[48,1536]{1,0:T(8,128)(2,1)S(1)} %get-tuple-element.135), channel_id=1, source_target_pairs={{0,16},{4,20},{8,24},{12,28},{16,0},{20,4},{24,8},{28,12},{1,17},{... | collective-permute-start | bytes 442376 | tf_op jit(solution)/shard_map/ppermute | solution.py:62
  531.2 48.0 %collective-permute-start.84 = (bf16[48,2304]{1,0:T(8,128)(2,1)S(1)}, bf16[48,2304]{1,0:T(8,128)(2,1)S(1)}, u32[]{:S(2)}, u32[]{:S(2)}) collective-permute-start(bf16[48,2304]{1,0:T(8,128)(2,1)S(1)} %get-tuple-element.113), channel_id=1, source_target_pairs={{0,28},{4,24},{8,4},{12,0},{16,12},{20,8},{24,20},{28,16},{1,29},{... | collective-permute-start | bytes 663560 | tf_op jit(solution)/shard_map/ppermute | solution.py:73
  533.1 46.1 %collective-permute-start.83 = (bf16[48,2304]{1,0:T(8,128)(2,1)S(1)}, bf16[48,2304]{1,0:T(8,128)(2,1)S(1)}, u32[]{:S(2)}, u32[]{:S(2)}) collective-permute-start(bf16[48,2304]{1,0:T(8,128)(2,1)S(1)} %get-tuple-element.114), channel_id=1, source_target_pairs={{0,20},{4,16},{8,28},{12,24},{16,4},{20,0},{24,12},{28,8},{1,21},{... | collective-permute-start | bytes 663560 | tf_op jit(solution)/shard_map/ppermute | solution.py:73
  537.4 41.8 %collective-permute-start.82 = (bf16[48,2304]{1,0:T(8,128)(2,1)S(1)}, bf16[48,2304]{1,0:T(8,128)(2,1)S(1)}, u32[]{:S(2)}, u32[]{:S(2)}) collective-permute-start(bf16[48,2304]{1,0:T(8,128)(2,1)S(1)} %get-tuple-element.115), channel_id=1, source_target_pairs={{0,12},{4,8},{8,20},{12,16},{16,28},{20,24},{24,4},{28,0},{1,13},{... | collective-permute-start | bytes 663560 | tf_op jit(solution)/shard_map/ppermute | solution.py:73
  537.4 41.7 %collective-permute-start.81 = (bf16[48,2304]{1,0:T(8,128)(2,1)S(1)}, bf16[48,2304]{1,0:T(8,128)(2,1)S(1)}, u32[]{:S(2)}, u32[]{:S(2)}) collective-permute-start(bf16[48,2304]{1,0:T(8,128)(2,1)S(1)} %get-tuple-element.116), channel_id=1, source_target_pairs={{0,4},{4,0},{8,12},{12,8},{16,20},{20,16},{24,28},{28,24},{1,5},{5... | collective-permute-start | bytes 663560 | tf_op jit(solution)/shard_map/ppermute | solution.py:73
  (109 other events, 1906.7 us)
Sparse Core Ops, SparseCore 0:
  9.9 49.1 all-gather.3
  66.2 114.6 all-gather.5
  337.6 43.6 reduce-scatter.6
  384.2 94.5 reduce-scatter.4

commit v2 on v1

--- a/solution.py
+++ b/solution.py
@@ -45,7 +45,7 @@
 
 
 def cost(flops, nbytes, exps=0):
-    return pl.CostEstimate(flops=int(flops), bytes_accessed=int(nbytes), transcendentals=int(exps))
+    return pl.CostEstimate(flops=1, bytes_accessed=1, transcendentals=0)
 
 
 def struct(shape, dtype):
@@ -68,24 +68,17 @@
     return lax.ppermute(value, "ctx", pairs)
 
 
-def send_to(value, steps, other):
-    count = lax.axis_size("ctx")
-    return lax.ppermute(
-        value, "ctx", [(i, ((i + 2 * steps) % count) ^ other) for i in range(count)]
-    )
-
-
 def swap_fsdp(value, bit):
     count = lax.axis_size("fsdp")
     return lax.ppermute(value, "fsdp", [(i, i ^ bit) for i in range(count)])
 
 
-def picked(array, numbers, axis):
-    items = [
-        lax.dynamic_index_in_dim(array, numbers[index], axis, keepdims=False)
-        for index in range(numbers.shape[0])
-    ]
-    return jnp.stack(items, axis=axis)
+def after(value, *others):
+    return lax.optimization_barrier((value,) + others)[0]
+
+
+def is_aligned(rows, fsdp):
+    return rows % ROW_TILE == 0 and fsdp == 4
 
 
 def bits_of(count):
@@ -108,39 +101,59 @@
     return [(near, bits)]
 
 
-def gather_blocks(shard, chips, fsdp):
-    if shard.shape[0] % ROW_TILE:
-        return [lax.all_gather(shard, BOTH, axis=0, tiled=True)], None
-    moved = {0: shard}
-    for step in [1, chips - 1] + list(range(2, chips - 1)):
-        if step not in moved and step < chips:
-            moved[step] = shift_chip(shard, step)
-    arrays, plan = [], []
-    for steps, bits in halves_of(chips, fsdp):
-        held = {0: jnp.concatenate([moved[step] for step in steps], axis=0)}
-        for bit in bits:
-            for item in list(held):
-                held[item ^ bit] = swap_fsdp(held[item], bit)
-        for item, array in held.items():
+def spread(array, bits, waits=()):
+    held = {0: array}
+    for bit in bits:
+        for item in list(held):
+            held[item ^ bit] = swap_fsdp(held[item], bit)
+    return held
+
+
+def gather_head(packed, down, split, tables, chips):
+    half = down.shape[1] // 2
+    first, second = 1, 2
+    left, right = after(down[:, :half], packed), after(down[:, half:], packed)
+    moved = {0: packed, 1: shift_chip(packed, 1)}
+    lefts, rights = {0: left, first: swap_fsdp(left, first)}, {0: right, second: swap_fsdp(right, second)}
+    if chips > 2:
+        moved[chips - 1] = shift_chip(packed, -1)
+    lefts[second], rights[first] = swap_fsdp(left, second), swap_fsdp(right, first)
+    done = [lefts[first], lefts[second], rights[first], rights[second], split] + list(moved.values())[1:]
+    for step in range(2, chips - 1):
+        moved[step] = shift_chip(after(moved[step - 1], *done), 1)
+    lefts[3] = swap_fsdp(after(lefts[first], *done), second)
+    rights[3] = swap_fsdp(after(rights[second], *done), first)
+    done = [lefts[3], rights[3]] + [moved[step] for step in range(2, chips - 1)] + tables
+    groups = [
+        (steps, bits)
+        for steps, bits in (
+            ([step for step in range(chips) if step < 2], (first, second)),
+            ([step for step in range(chips) if step >= 2], (second, first)),
+        )
+        if steps
+    ]
+    arrays, plan, held = [], [], []
+    for steps, bits in groups:
+        own = after(jnp.concatenate([moved[step] for step in steps], axis=0), *done)
+        held.append({0: own, bits[0]: swap_fsdp(own, bits[0]), bits[1]: swap_fsdp(own, bits[1])})
+    wide_part = lax.all_to_all(after(split, *done), "ctx", 0, 0)
+    middle = [group[item] for group in held for item in (first, second)] + [wide_part]
+    for group, (steps, bits) in zip(held, groups):
+        group[3] = swap_fsdp(after(group[bits[0]], *middle), bits[1])
+        for item, array in group.items():
             for other, version in ((0, array), (1, swap_core(array))):
                 for block, step in enumerate(steps):
                     plan.append((len(arrays), block, step, other, item))
                 arrays.append(version)
-    return arrays, plan
-
-
-def reduce_blocks(kept, sent, chips, fsdp):
-    if not sent:
-        return lax.psum_scatter(kept[0], BOTH, scatter_dimension=0, tiled=True).astype(F32)
+    downs = [lefts[item] for item in range(4)] + [rights[item] for item in range(4)]
+    return arrays, plan, downs, wide_part, [wide_part] + [group[3] for group in held]
+
+
+def reduce_chips(held, chips, fsdp):
     total = None
-    for (steps, bits), keep, send in zip(halves_of(chips, fsdp), kept, sent):
-        held = keep + swap_core(send)
-        for bit in bits:
-            half = held.shape[0] // 2
-            held = held[half:] + swap_fsdp(held[:half], bit)
-        held = held[0]
+    for (steps, _), part_of in zip(halves_of(chips, fsdp), held):
         for at, step in enumerate(steps):
-            part = held[at] if step == 0 else shift_chip(held[at], step)
+            part = part_of[at] if step == 0 else shift_chip(part_of[at], step)
             part = part.astype(F32)
             total = part if total is None else total + part
     return total
@@ -177,42 +190,43 @@
     packed_ref[:, QKV + LANES :] = out_ref[...]
 
 
-def split_kernel(chips, own, padded, info_ref, weight_ref, gain_ref, split_ref):
+def split_kernel(own, weight_ref, gain_ref, split_ref):
     total = weight_ref.shape[1] // 2
-    count = 2 * chips
-    rows = weight_ref.shape[0]
-    chip = info_ref[0] // 2
-    core = info_ref[0] % 2
+    count, rows, padded = split_ref.shape
+    padded = padded // 2
     filler = jnp.zeros((rows, padded - own), F32)
     for target in range(count):
-        step = (target // 2 - chip + chips) % chips
-        other = jnp.bitwise_xor(core, target % 2)
         for part in range(2):
             start = part * total + target * own
             values = weight_ref[:, start : start + own].astype(F32) * gain_ref[...]
             if padded > own:
                 values = jnp.concatenate([values, filler], axis=1)
-            split_ref[other, step, :, part * padded : (part + 1) * padded] = values.astype(BF16)
-
-
-def join_kernel(chips, own, padded, info_ref, parts_ref, weight_ref, gain_ref, grad_ref, norm_ref):
+            split_ref[target, :, part * padded : (part + 1) * padded] = values.astype(BF16)
+
+
+def join_kernel(own, gate_ref, up_ref, weight_ref, gain_ref, grad_ref, norm_ref):
     total = weight_ref.shape[1] // 2
     rows = weight_ref.shape[0]
-    chip = info_ref[0] // 2
-    core = info_ref[0] % 2
     sums = jnp.zeros((rows, 1), F32)
-    for source in range(2 * chips):
-        step = (chip - source // 2 + chips) % chips
-        other = jnp.bitwise_xor(core, source % 2)
-        for part in range(2):
-            values = parts_ref[other * chips + step, :, part * padded : (part + 1) * padded]
-            values = values[:, :own].astype(F32)
+    for source in range(gate_ref.shape[0]):
+        for part, ref in enumerate((gate_ref, up_ref)):
+            values = ref[source].astype(F32)[:, :own]
             start = part * total + source * own
             grad_ref[:, start : start + own] = values * gain_ref[...]
             sums = sums + jnp.sum(
                 values * weight_ref[:, start : start + own].astype(F32), axis=1, keepdims=True
             )
     norm_ref[...] = sums
+
+
+def stack_kernel(fsdp, info_ref, *refs):
+    pieces, out_ref, whole = refs[:-2], refs[-2], refs[-1]
+    rows, columns = pieces[0].shape
+    for half in range(2):
+        for item in range(fsdp):
+            row = pl.multiple_of(jnp.bitwise_xor(info_ref[1], item) * rows, 8)
+            whole[pl.ds(row, rows), half * columns : (half + 1) * columns] = pieces[half * fsdp + item][...].astype(F32)
+    out_ref[...] = whole[...].astype(BF16)
 
 
 def project_kernel(plan, chips, fsdp, bias_width, count, info_ref, tokens_ref, cos_ref, sin_ref, *refs):
@@ -298,124 +312,148 @@
     unit_ref[...] = (middle * normalised(middle)).astype(BF16)
 
 
+def tokens_of(info_ref, step, chips, rows):
+    chip = (info_ref[0] // 2 - step + chips) % chips
+    return pl.ds(pl.multiple_of(chip * 2 * rows, 2 * rows), 2 * rows)
+
+
 def feed_kernel(
-    chips, fsdp, own, padded, info_ref, x_mine, x_other, c_mine, c_other, wide_ref, down_ref,
-    gu_mine, gu_other, br_mine, br_other, hidden_ref, grad_ref,
-    wide, down, acc_units, acc_branch, sems,
+    steps, first, plan, chips, fsdp, own, padded, count, info_ref, units_ref, cots_ref, *refs
 ):
-    rows, width = x_mine.shape
+    pieces, down_ref = refs[: 2 * count], refs[2 * count]
+    refs = refs[2 * count + (1 if first else 2) :]
+    branch_ref, mine_ref, other_ref, hidden_ref, grad_ref = refs[:5]
+    x, c, gate_w, up_w, down, acc_units, acc_branch, branch, gate_sems, up_sems, sems = refs[5:]
+    _, rows, width = mine_ref.shape
     block_rows = width // (2 * chips * fsdp)
-    copies = []
-    index = 0
-    if block_rows % ROW_TILE:
-        copies.append(pltpu.make_async_copy(wide_ref, wide, sems.at[0]))
-        index = 1
-    for item in range(0 if index else fsdp):
-        for other in range(2):
-            for step in range(chips):
-                chip = (info_ref[0] // 2 - step + chips) % chips
-                core = jnp.bitwise_xor(info_ref[0] % 2, other)
-                row = pl.multiple_of(((2 * chip + core) * fsdp + item) * block_rows, block_rows)
-                copies.append(
-                    pltpu.make_async_copy(
-                        wide_ref.at[item, other * chips + step],
-                        wide.at[pl.ds(row, block_rows)],
-                        sems.at[index],
-                    )
-                )
-                index += 1
-    last = pltpu.make_async_copy(down_ref, down.at[pl.ds(0, own)], sems.at[index])
-    for copy in copies:
+    spans = [tokens_of(info_ref, step, chips, rows) for step in steps]
+    places = [pl.ds(index * 2 * rows, 2 * rows) for index in range(len(steps))]
+
+    def loads(parts, whole, part_sems):
+        if plan is None:
+            return [pltpu.make_async_copy(parts[0], whole, part_sems.at[0])]
+        copies = []
+        for index, (array, block, item) in enumerate(plan):
+            row = (block * fsdp + jnp.bitwise_xor(info_ref[1], item)) * block_rows
+            row = pl.multiple_of(row, block_rows)
+            source = parts[array].at[block]
+            copies.append(
+                pltpu.make_async_copy(source, whole.at[pl.ds(row, block_rows)], part_sems.at[index])
+            )
+        return copies
+
+    x_loads = [
+        pltpu.make_async_copy(units_ref.at[span], x.at[place], sems.at[index])
+        for index, (span, place) in enumerate(zip(spans, places))
+    ]
+    c_loads = [
+        pltpu.make_async_copy(cots_ref.at[span], c.at[place], sems.at[len(steps) + index])
+        for index, (span, place) in enumerate(zip(spans, places))
+    ]
+    c_loads.append(pltpu.make_async_copy(down_ref, down.at[pl.ds(0, own)], sems.at[2 * len(steps)]))
+    gate_loads = loads(pieces[:count], gate_w, gate_sems)
+    up_loads = loads(pieces[count:], up_w, up_sems)
+    for copy in x_loads + gate_loads + up_loads + c_loads:
         copy.start()
-    last.start()
     if padded > own:
         down[own:, :] = jnp.zeros((padded - own, width), BF16)
-    for copy in copies:
+    block = 384 if padded % 384 == 0 else LANES
+    for copy in x_loads + gate_loads:
         copy.wait()
-    last.wait()
-    x = jnp.concatenate([x_mine[...], x_other[...]], axis=0)
-    c = jnp.concatenate([c_mine[...], c_other[...]], axis=0)
-    block = 384 if padded % 384 == 0 else LANES
     for at in range(0, padded, block):
-        span = slice(at, at + block)
-        span_up = slice(padded + at, padded + at + block)
-        gate = dot_nn(x, wide[:, span])
-        up = dot_nn(x, wide[:, span_up])
-        grad_hidden = dot_nt(c, down[span, :])
+        cols = slice(at, at + block)
+        cols_up = slice(padded + at, padded + at + block)
+        gate = dot_nn(x[...], gate_w[:, cols])
+        if at == 0:
+            for copy in up_loads:
+                copy.wait()
+        up = dot_nn(x[...], up_w[:, cols])
+        if at == 0:
+            for copy in c_loads:
+                copy.wait()
+        grad_hidden = dot_nt(c[...], down[cols, :])
         sig = 1.0 / (1.0 + jnp.exp(-gate))
         swished = gate * sig
         hidden = (swished * up).astype(BF16)
         grad_gate = (grad_hidden * up * sig * (1.0 + gate * (1.0 - sig))).astype(BF16)
         grad_up = (grad_hidden * swished).astype(BF16)
-        hidden_ref[:, span] = hidden
-        grad_ref[:, span] = grad_gate
-        grad_ref[:, span_up] = grad_up
-        units = dot_nt(grad_gate, wide[:, span]) + dot_nt(grad_up, wide[:, span_up])
-        branch = dot_nn(hidden, down[span, :])
+        hidden_ref[cols, :] = hidden.T
+        grad_ref[:, cols] = grad_gate
+        grad_ref[:, cols_up] = grad_up
+        units = dot_nt(grad_gate, gate_w[:, cols]) + dot_nt(grad_up, up_w[:, cols])
+        more = dot_nn(hidden, down[cols, :])
         if at == 0:
             acc_units[...] = units
-            acc_branch[...] = branch
+            acc_branch[...] = more
         else:
             acc_units[...] += units
-            acc_branch[...] += branch
-    gu_mine[...] = acc_units[:rows].astype(BF16)
-    gu_other[...] = acc_units[rows:].astype(BF16)
-    br_mine[...] = acc_branch[:rows].astype(BF16)
-    br_other[...] = acc_branch[rows:].astype(BF16)
-
-
-def wide_grad_kernel(chips, fsdp, n_units, info_ref, *refs):
-    units = refs[:n_units]
-    grads = refs[n_units : n_units + n_units // 2]
-    out_ref, turned, total = refs[n_units + n_units // 2 :]
-    rows, width = units[0].shape
-    block_rows = width // (2 * chips * fsdp)
-
-    @pl.when(pl.program_id(0) == 0)
-    def _():
-        for index, unit in enumerate(units):
-            turned[:, index * rows : (index + 1) * rows] = unit[...].T
-
-    for index, grad in enumerate(grads):
-        part = dot_nn(turned[:, index * 2 * rows : (index + 1) * 2 * rows], grad[...])
-        if index == 0:
-            total[...] = part
-        else:
-            total[...] += part
-    if block_rows % ROW_TILE:
-        out_ref[...] = total[...].astype(BF16)
+            acc_branch[...] += more
+    branch[...] = acc_branch[...].astype(BF16)
+    stores = [
+        pltpu.make_async_copy(branch.at[place], branch_ref.at[span], sems.at[index])
+        for index, (span, place) in enumerate(zip(spans, places))
+    ]
+    for copy in stores:
+        copy.start()
+    core = info_ref[0] % 2
+    for index in range(len(steps)):
+        start = index * 2 * rows
+        mine = pl.ds(pl.multiple_of(start + core * rows, rows), rows)
+        other = pl.ds(pl.multiple_of(start + (1 - core) * rows, rows), rows)
+        mine_ref[index] = acc_units[mine, :].astype(BF16)
+        other_ref[index] = acc_units[other, :].astype(BF16)
+    for copy in stores:
+        copy.wait()
+
+
+def turn_kernel(steps, chips, rows, info_ref, units_ref, out_ref):
+    for index, step in enumerate(steps):
+        span = tokens_of(info_ref, step, chips, rows)
+        out_ref[:, index * 2 * rows : (index + 1) * 2 * rows] = units_ref[span, :].T
+
+
+def wide_grad_kernel(orders, info_ref, turned, *refs):
+    outs = 1 if orders is None else 4
+    grads, out_refs, total = refs[: -1 - outs], refs[-1 - outs : -1], refs[-1]
+    total[...] = dot_nn(turned[...], jnp.concatenate([grad[...] for grad in grads], axis=0))
+    each, count, block_rows, _ = out_refs[0].shape
+    if orders is None:
+        for slot in range(each):
+            for block in range(count):
+                row = (block * each + slot) * block_rows
+                out_refs[0][slot, block] = total[row : row + block_rows, :].astype(BF16)
         return
-    for item in range(fsdp):
-        for other in range(2):
-            for step in range(chips):
-                chip = (info_ref[0] // 2 + step) % chips
-                core = jnp.bitwise_xor(info_ref[0] % 2, other)
-                row = pl.multiple_of(((2 * chip + core) * fsdp + item) * block_rows, block_rows)
-                out_ref[item, other * chips + step] = total[pl.ds(row, block_rows), :].astype(BF16)
-
-
-def down_grad_kernel(own, n_hidden, *refs):
-    hiddens = refs[:n_hidden]
-    cots = refs[n_hidden : 3 * n_hidden]
-    out_ref, turned = refs[3 * n_hidden :]
-    rows = hiddens[0].shape[0]
-
-    @pl.when(pl.program_id(0) == 0)
-    def _():
-        for index, hidden in enumerate(hiddens):
-            turned[:, index * rows : (index + 1) * rows] = hidden[...].T
-
-    total = None
-    for index in range(n_hidden):
-        c = jnp.concatenate([cots[2 * index][...], cots[2 * index + 1][...]], axis=0)
-        part = dot_nn(turned[:own, index * rows : (index + 1) * rows], c)
-        total = part if total is None else total + part
-    out_ref[...] = total.astype(BF16)
+    fsdp = 2 * each
+    for half, items in enumerate(orders):
+        for slot, item in enumerate(items):
+            for block in range(count):
+                row = ((half * count + block) * fsdp + jnp.bitwise_xor(info_ref[1], item)) * block_rows
+                row = pl.multiple_of(row, block_rows)
+                out_refs[2 * half + slot // each][slot % each, block] = total[pl.ds(row, block_rows), :].astype(BF16)
+
+
+def down_grad_kernel(orders, steps, chips, rows, info_ref, cots_ref, *refs):
+    outs = 1 if orders is None else 4
+    hiddens, out_refs, total = refs[: -1 - outs], refs[-1 - outs : -1], refs[-1]
+    own, half = total.shape
+    turned = jnp.concatenate([hidden[:own, :] for hidden in hiddens], axis=1)
+    cots = jnp.concatenate([cots_ref[tokens_of(info_ref, step, chips, rows), :] for step in steps], axis=0)
+    for index in range(cots.shape[1] // half):
+        total[...] = dot_nn(turned, cots[:, index * half : (index + 1) * half])
+        if orders is None:
+            out_refs[0][:, index * half : (index + 1) * half] = total[...].astype(BF16)
+            continue
+        each = len(orders[0]) // 2
+        part = own // len(orders[0])
+        for slot, item in enumerate(orders[index]):
+            row = pl.multiple_of(jnp.bitwise_xor(info_ref[1], item) * part, 8)
+            out_refs[2 * index + slot // each][slot % each] = total[pl.ds(row, part), :].astype(BF16)
 
 
 def middle_back_kernel(
-    plan, chips, fsdp, count, sources, info_ref, place_ref, q_ref, own_ref, came_ref, middle_ref, cot_ref, *refs
+    plan, chips, fsdp, count, sources, info_ref, place_ref, q_ref, middle_ref, cot_ref, *refs
 ):
+    unit_refs, refs = refs[:chips], refs[chips:]
     kv_refs = refs[: len(sources)]
     refs = refs[len(sources) :]
     pieces = refs[:count]
@@ -427,7 +465,9 @@
     )
     for copy in copies:
         copy.start()
-    units = own_ref[...].astype(F32) + came_ref[...].astype(F32)
+    units = unit_refs[0][...].astype(F32)
+    for ref in unit_refs[1:]:
+        units = units + ref[...].astype(F32)
     middle = middle_ref[...]
     rms = normalised(middle)
     grad_middle = (
@@ -471,7 +511,7 @@
 
 def scatter_out(total, info_ref, chips, fsdp, kept, sent):
     block_rows = total.shape[0] // (2 * chips * fsdp)
-    if block_rows % ROW_TILE:
+    if not is_aligned(block_rows, fsdp):
         kept[0][...] = total[...].astype(BF16)
         return
     for (steps, bits), keep, send in zip(halves_of(chips, fsdp), kept, sent):
@@ -601,41 +641,55 @@
         compiler_params=params(),
         name="pack",
     )(qkv_weight, bias_block, out_weight, gain_one)
-    pieces, plan = gather_blocks(packed, chips, fsdp)
-
-    split = call(
-        functools.partial(split_kernel, chips, own, padded),
-        struct((2, chips, weight_rows, 2 * padded), BF16),
-        [info, gate_up_weight, gain_two],
+    own_down = down_weight.shape[0]
+    aligned = is_aligned(weight_rows, fsdp) and own_down % 8 == 0
+    split = pl.pallas_call(
+        functools.partial(split_kernel, own),
+        out_shape=struct((ctx, weight_rows, 2 * padded), BF16),
+        compiler_params=params(),
         name="split",
-    )
-    w_down = lax.all_gather(down_weight, "fsdp", axis=0, tiled=True)
-    arrived = [
-        split[other, step] if (other, step) == (0, 0) else send_to(split[other, step], step, other)
-        for other in range(2)
-        for step in range(chips)
-    ]
-    aligned = weight_rows % ROW_TILE == 0
-    arrived = jnp.stack(arrived)
-    numbers = jnp.arange(ctx, dtype=jnp.int32)
-    came_from = (numbers + my_ctx) % 2 * chips + (my_ctx // 2 - numbers // 2 + chips) % chips
-    if not aligned:
-        arrived = picked(arrived, came_from, 0)
-    w_wide = lax.all_gather(arrived, "fsdp", axis=0, tiled=False)
-    if not aligned:
-        w_wide = w_wide.transpose(1, 0, 2, 3).reshape(width, 2 * padded)
-
-    cot_mine = [grad_out]
-    for step in range(1, chips):
-        cot_mine.append(shift_chip(grad_out, step))
-    cot_other = [swap_core(item) for item in cot_mine]
-
+    )(gate_up_weight, after(gain_two, packed))
+    bits = bits_of(fsdp)
+    d_half = width // 2
     steps_half = jnp.arange(0, HEAD_DIM, 2).astype(F32)
     inverse = 10000.0 ** (-steps_half / HEAD_DIM)
-    turns = positions[0].astype(F32)[:, None] * inverse[None, :]
-    cosine = jnp.tile(jnp.cos(turns), (1, 2))
-    sine = jnp.concatenate([-jnp.sin(turns), jnp.sin(turns)], axis=-1)
+    angles = positions[0].astype(F32)[:, None] * inverse[None, :]
+    cosine = jnp.tile(jnp.cos(angles), (1, 2))
+    sine = jnp.concatenate([-jnp.sin(angles), jnp.sin(angles)], axis=-1)
     places = positions[0][:, None]
+    if aligned:
+        pieces, plan, down_held, wide_part, last = gather_head(
+            packed, down_weight, split, [cosine, sine, places], chips
+        )
+        w_down = call(
+            functools.partial(stack_kernel, fsdp),
+            struct((own, width), BF16),
+            [info] + down_held,
+            scratch=[pltpu.VMEM((own, width), F32)],
+            estimate=cost(0, 0),
+            name="stack",
+        )
+    else:
+        pieces, plan, last = [lax.all_gather(packed, BOTH, axis=0, tiled=True)], None, []
+        wide_part = lax.all_to_all(split, "ctx", 0, 0)
+        w_down = lax.all_gather(down_weight, "fsdp", axis=0, tiled=True)
+    gate_part, up_part = wide_part[:, :, :padded], wide_part[:, :, padded:]
+    if aligned:
+        gate_held, up_held = spread(gate_part, bits), spread(up_part, bits[::-1])
+        items = sorted(gate_held)
+        near_wide = [gate_held[bits[0]], up_held[bits[-1]]]
+        wide_plan = [(index, block, item) for index, item in enumerate(items) for block in range(ctx)]
+        wide_pieces = [gate_held[item] for item in items] + [up_held[item] for item in items]
+    else:
+        wide_plan = None
+        near_wide = []
+        wide_pieces = [
+            lax.all_gather(part, "fsdp", axis=1, tiled=False).reshape(width, padded)
+            for part in (gate_part, up_part)
+        ]
+    wide_count = len(wide_pieces) // 2
+    all_cots = lax.all_gather(after(grad_out, *last), "ctx", axis=0, tiled=True)
+
     count = len(pieces)
     unit_one, queries, own_kv = call(
         functools.partial(project_kernel, plan, chips, fsdp, bias_width, count),
@@ -657,7 +711,7 @@
     context, middle, unit_two = call(
         functools.partial(attend_kernel, plan, chips, fsdp, count, sources),
         [struct((rows, width), BF16), struct((rows, width), F32), struct((rows, width), BF16)],
-        [info, places, queries, inputs] + kv_blocks + pieces,
+        [after(info, *near_wide), places, queries, inputs] + kv_blocks + pieces,
         4 + len(sources),
         4 + len(sources) + count,
         [pltpu.VMEM((width, width), BF16), pltpu.SemaphoreType.DMA((len(plan or [0]),))],
@@ -665,96 +719,103 @@
         "attend",
     )
 
-    units_mine = [unit_two]
-    for step in range(1, chips):
-        units_mine.append(shift_chip(units_mine[-1], 1))
-    units_other = [swap_core(item) for item in units_mine]
-    fed = []
-    for step in range(chips):
-        fed.append(
-            call(
-                functools.partial(feed_kernel, chips, fsdp, own, padded),
-                [struct((rows, width), BF16)] * 4
-                + [struct((2 * rows, padded), BF16), struct((2 * rows, 2 * padded), BF16)],
-                [info, units_mine[step], units_other[step], cot_mine[step], cot_other[step], w_wide, w_down],
-                5,
-                7,
-                [
-                    pltpu.VMEM((width, 2 * padded), BF16),
-                    pltpu.VMEM((padded, width), BF16),
-                    pltpu.VMEM((2 * rows, width), F32),
-                    pltpu.VMEM((2 * rows, width), F32),
-                    pltpu.SemaphoreType.DMA((ctx * fsdp + 1,)),
-                ],
-                cost(2 * 6 * 2 * rows * width * padded, 6 * width * padded),
-                "feed",
-            )
+    all_units = lax.all_gather(after(unit_two, all_cots), "ctx", axis=0, tiled=True)
+    order = list(range(2, chips - 1)) + [1, chips - 1, 0] if chips > 2 else list(range(chips))[::-1]
+    turned = call(
+        functools.partial(turn_kernel, order, chips, rows),
+        struct((width, ctx * rows), BF16),
+        [after(info, w_down, *wide_pieces), all_units],
+        estimate=cost(0, 4 * ctx * rows * width),
+        name="turn",
+    )
+    half = len(order) // 2
+    fed, unit_parts, branch, when = [], {}, [], turned
+    for steps in (order[:half], order[half:]):
+        tokens_now = 2 * rows * len(steps)
+        plan_count = len(wide_plan or [0])
+        operands = [after(info, when), all_units, all_cots] + wide_pieces + [w_down] + branch
+        branch_now, mine, other, hidden, grads = pl.pallas_call(
+            functools.partial(
+                feed_kernel, steps, not branch, wide_plan, chips, fsdp, own, padded, wide_count
+            ),
+            out_shape=[
+                struct((ctx * rows, width), BF16),
+                struct((len(steps), rows, width), BF16),
+                struct((len(steps), rows, width), BF16),
+                struct((padded, tokens_now), BF16),
+                struct((tokens_now, 2 * padded), BF16),
+            ],
+            in_specs=[SMEM_SPEC] + [ANY_SPEC] * (len(operands) - 1),
+            out_specs=[ANY_SPEC] + [VMEM_SPEC] * 4,
+            input_output_aliases={len(operands) - 1: 0} if branch else {},
+            scratch_shapes=[
+                pltpu.VMEM((tokens_now, width), BF16),
+                pltpu.VMEM((tokens_now, width), BF16),
+                pltpu.VMEM((width, padded), BF16),
+                pltpu.VMEM((width, padded), BF16),
+                pltpu.VMEM((padded, width), BF16),
+                pltpu.VMEM((tokens_now, width), F32),
+                pltpu.VMEM((tokens_now, width), F32),
+                pltpu.VMEM((tokens_now, width), BF16),
+                pltpu.SemaphoreType.DMA((plan_count,)),
+                pltpu.SemaphoreType.DMA((plan_count,)),
+                pltpu.SemaphoreType.DMA((2 * len(steps) + 1,)),
+            ],
+            compiler_params=params(),
+            cost_estimate=cost(0, 0),
+            name="feed",
+        )(*operands)
+        branch = [branch_now]
+        fed.append((hidden, grads))
+        early = list(unit_parts.values())
+        swapped = swap_core(after(other, *early))
+        for index, step in enumerate(steps):
+            part = mine[index] + swapped[index]
+            unit_parts[step] = shift_chip(part, -step) if step else part
+        when = swapped
+    n_block = 384 if padded % 384 == 0 else LANES
+
+    def wide_grad(start, items, when):
+        outs = 4 if items else 1
+        shape = (fsdp // 2, chips, weight_rows, padded) if items else (fsdp, ctx, weight_rows, padded)
+        return pl.pallas_call(
+            functools.partial(wide_grad_kernel, items),
+            out_shape=[struct(shape, BF16)] * outs,
+            grid=(padded // n_block,),
+            in_specs=[SMEM_SPEC, pl.BlockSpec((width, ctx * rows), lambda i: (0, 0))]
+            + [
+                pl.BlockSpec((grads.shape[0], n_block), lambda i: (0, start // n_block + i))
+                for _, grads in fed
+            ],
+            out_specs=[pl.BlockSpec(shape[:3] + (n_block,), lambda i: (0, 0, 0, i))] * outs,
+            scratch_shapes=[pltpu.VMEM((width, n_block), F32)],
+            compiler_params=params(),
+            cost_estimate=cost(2 * ctx * rows * width * padded, 4 * width * padded),
+            name="wide_grad",
+        )(when, turned, *[grads for _, grads in fed])
+
+    turns = (bits, bits[::-1])
+    wide_orders = [halving_order(items) for items in turns] if aligned else None
+    gate_parts = wide_grad(0, wide_orders, after(info, *early))
+    up_parts = wide_grad(padded, wide_orders, after(info, gate_parts[0]))
+
+    def wide_first(parts, *waits):
+        return [swap_fsdp(after(part, *waits), items[0]) for part, items in zip(parts[::2], turns)]
+
+    def wide_second(parts, came, *waits):
+        pairs = []
+        for keep, more, items in zip(parts[1::2], came, turns):
+            away = swap_fsdp(after(keep[0] + more[0], *waits), items[1])
+            pairs.append((keep[1] + more[1], away))
+        return pairs
+
+    def wide_across(pairs, *waits):
+        return lax.all_to_all(
+            after(jnp.concatenate([mine + away for mine, away in pairs], axis=0), *waits), "ctx", 0, 0
         )
 
-    def ring(parts):
-        sums = [mine + swap_core(other) for mine, other in parts]
-        moving = None
-        for step in range(1, chips):
-            moving = shift_chip(sums[step] if moving is None else sums[step] + moving, 1)
-        return sums[0], moving
-
-    own_units, came_units = ring([(item[0], item[1]) for item in fed])
-
-    n_block = 384 if (2 * padded) % 384 == 0 else LANES
-    all_units = [item for pair in zip(units_mine, units_other) for item in pair]
-    wide_grad = pl.pallas_call(
-        functools.partial(wide_grad_kernel, chips, fsdp, ctx),
-        out_shape=struct((fsdp, ctx, weight_rows, 2 * padded) if aligned else (width, 2 * padded), BF16),
-        grid=(2 * padded // n_block,),
-        in_specs=[SMEM_SPEC]
-        + [pl.BlockSpec((rows, width), lambda i: (0, 0))] * ctx
-        + [pl.BlockSpec((2 * rows, n_block), lambda i: (0, i))] * chips,
-        out_specs=pl.BlockSpec((fsdp, ctx, weight_rows, n_block), lambda i: (0, 0, 0, i))
-        if aligned
-        else pl.BlockSpec((width, n_block), lambda i: (0, i)),
-        scratch_shapes=[pltpu.VMEM((width, ctx * rows), BF16), pltpu.VMEM((width, n_block), F32)],
-        compiler_params=params(),
-        cost_estimate=cost(4 * ctx * rows * width * padded, 8 * width * padded),
-        name="wide_grad",
-    )(info, *all_units, *[item[5] for item in fed])
-    d_block = 512
-    all_cots = [item for pair in zip(cot_mine, cot_other) for item in pair]
-    down_grad = pl.pallas_call(
-        functools.partial(down_grad_kernel, own, chips),
-        out_shape=struct((own, width), BF16),
-        grid=(width // d_block,),
-        in_specs=[pl.BlockSpec((2 * rows, padded), lambda i: (0, 0))] * chips
-        + [pl.BlockSpec((rows, d_block), lambda i: (0, i))] * ctx,
-        out_specs=pl.BlockSpec((own, d_block), lambda i: (0, i)),
-        scratch_shapes=[pltpu.VMEM((padded, ctx * rows), BF16)],
-        compiler_params=params(),
-        cost_estimate=cost(2 * ctx * rows * width * padded, 4 * width * padded),
-        name="down_grad",
-    )(*[item[4] for item in fed], *all_cots)
-    down_grad = lax.psum_scatter(down_grad, "fsdp", scatter_dimension=0, tiled=True).astype(F32)
-    if not aligned:
-        slots = jnp.arange(ctx, dtype=jnp.int32)
-        goes_to = 2 * ((my_ctx // 2 + slots % chips) % chips) + (my_ctx + slots // chips) % 2
-        wide_grad = wide_grad.reshape(ctx, fsdp, weight_rows, 2 * padded).transpose(1, 0, 2, 3)
-        wide_grad = picked(wide_grad, goes_to, 1)
-    wide_grad = lax.psum_scatter(
-        wide_grad.reshape(fsdp * ctx * weight_rows, 2 * padded), "fsdp", scatter_dimension=0, tiled=True
-    ).reshape(ctx, weight_rows, 2 * padded)
-    back = [
-        wide_grad[other * chips + step]
-        if (other, step) == (0, 0)
-        else send_to(wide_grad[other * chips + step], step, other)
-        for other in range(2)
-        for step in range(chips)
-    ]
-    gate_up_grad, norm2_grad = call(
-        functools.partial(join_kernel, chips, own, padded),
-        [struct(gate_up_weight.shape, F32), struct((weight_rows, 1), F32)],
-        [info, jnp.stack(back), gate_up_weight, gain_two],
-        name="join",
-    )
-    own_branch, came_branch = ring([(item[2], item[3]) for item in fed])
-    result = (middle + own_branch.astype(F32) + came_branch.astype(F32)).astype(BF16)
+    gate_came = wide_first(gate_parts) if aligned else []
+    up_came = wide_first(up_parts) if aligned else []
 
     grad_middle, grad_attention, grad_queries, kv_mine, kv_other = call(
         functools.partial(middle_back_kernel, plan, chips, fsdp, count, sources),
@@ -765,22 +826,24 @@
             struct((reach + 1, rows, 2 * WIDTH_K), BF16),
             struct((reach + 1, rows, 2 * WIDTH_K), BF16),
         ],
-        [info, places, queries, own_units, came_units, middle, grad_out] + kv_blocks + pieces,
-        7 + len(sources),
-        7 + len(sources) + count,
+        [after(info, up_parts[0], *gate_came), places, queries, middle, grad_out]
+        + [unit_parts[step] for step in range(chips)]
+        + kv_blocks
+        + pieces,
+        5 + chips + len(sources),
+        5 + chips + len(sources) + count,
         [pltpu.VMEM((width, width), BF16), pltpu.SemaphoreType.DMA((len(plan or [0]),))],
         cost(10 * rows * span * WIDTH_Q + 2 * rows * width * width, 2 * width * width, rows * span * Q_HEADS),
         "middle_back",
     )
     halves = halves_of(chips, fsdp)
-    kept_count = len(halves) if aligned else 1
 
     def block_shapes(columns):
         if not aligned:
             return [struct((width, columns), BF16)]
         return 2 * [struct((fsdp, len(steps), weight_rows, columns), BF16) for steps, _ in halves]
 
-    outs = call(
+    out_parts = call(
         functools.partial(out_grad_kernel, chips, fsdp),
         block_shapes(width),
         [info, grad_attention, context],
@@ -788,34 +851,117 @@
         estimate=cost(2 * rows * width * width, 2 * width * width),
         name="out_grad",
     )
-    out_grad = reduce_blocks(outs[:kept_count], outs[kept_count:], chips, fsdp)
-
-    swapped = swap_core(kv_other)
+    swapped = swap_core(after(kv_other, out_parts[0], *up_came))
+    gate_pairs = wide_second(gate_parts, gate_came, out_parts[0], *up_came) if aligned else []
+    if aligned:
+        down_orders = [halving_order(bits), halving_order(bits[::-1])]
+        down_shapes = [struct((fsdp // 2, own_down, d_half), BF16)] * 4
+    else:
+        down_orders = None
+        down_shapes = [struct((own, width), BF16)]
+    down_parts = call(
+        functools.partial(down_grad_kernel, down_orders, order, chips, rows),
+        down_shapes,
+        [after(info, swapped), all_cots] + [hidden for hidden, _ in fed],
+        scratch=[pltpu.VMEM((own, d_half), F32)],
+        estimate=cost(2 * ctx * rows * width * padded, 4 * width * padded),
+        name="down_grad",
+    )
     came = []
     for step in range(1, reach + 1):
         came.append(shift_open(kv_mine[step] + swapped[step], -step))
     outs = call(
         functools.partial(projected_back_kernel, chips, fsdp, bias_width, reach),
         [struct((rows, QKV), BF16)] + block_shapes(QKV + LANES),
-        [info, grad_queries, kv_mine[0], swapped[0], cosine, sine, unit_one] + came,
+        [after(info, down_parts[0], *[away for _, away in gate_pairs]), grad_queries, kv_mine[0], swapped[0], cosine, sine, unit_one] + came,
         scratch=[pltpu.VMEM((width, QKV + LANES), F32)],
         estimate=cost(2 * rows * width * QKV, 2 * width * QKV),
         name="projected_back",
     )
-    grad_projected = outs[0]
-    qkv_sum = reduce_blocks(outs[1 : 1 + kept_count], outs[1 + kept_count :], chips, fsdp)
+    grad_projected, qkv_parts = outs[0], outs[1:]
+    def back_to_input(waits):
+        return call(
+            functools.partial(input_back_kernel, plan, chips, fsdp, count),
+            struct((rows, width), F32),
+            [after(info, *waits), grad_projected, inputs, grad_middle] + pieces,
+            4,
+            4 + count,
+            [pltpu.VMEM((width, QKV), BF16), pltpu.SemaphoreType.DMA((len(plan or [0]),))],
+            cost(2 * rows * width * QKV, 2 * width * QKV),
+            "input_back",
+        )
+
+    if aligned:
+        sides = [items for _, items in halves]
+
+        def swapped_of(parts, *waits):
+            return [(keep, swap_core(after(send, *waits))) for keep, send in zip(parts[:2], parts[2:])]
+
+        def first_exchange(pairs, *waits):
+            half = fsdp // 2
+            return [
+                swap_fsdp(after(keep[:half] + got[:half], *waits), items[0])
+                for (keep, got), items in zip(pairs, sides)
+            ]
+
+        def second_exchange(pairs, came_back):
+            sums = []
+            for (keep, got), more, items in zip(pairs, came_back, sides):
+                away = swap_fsdp(keep[2] + got[2] + more[0], items[1])
+                sums.append((keep[3] + got[3] + more[1], away))
+            return [mine + away for mine, away in sums]
+
+        up_pairs = wide_second(up_parts, up_came, *[away for _, away in gate_pairs])
+        gate_back = wide_across(gate_pairs, grad_projected)
+        qkv_pairs = swapped_of(qkv_parts)
+        input_grad = back_to_input([])
+        out_pairs = swapped_of(out_parts)
+        out_came = first_exchange(out_pairs, *[away for _, away in gate_pairs])
+        down_came = [
+            swap_fsdp(after(part, *[away for _, away in gate_pairs]), items[0])
+            for part, items in zip(down_parts[::2], (bits, bits[::-1]))
+        ]
+        qkv_came = first_exchange(qkv_pairs, input_grad, *[away for _, away in up_pairs], *out_came)
+        up_back = wide_across(up_pairs, gate_back)
+        qkv_far = second_exchange(qkv_pairs, [after(item, *down_came) for item in qkv_came])
+        qkv_sum = reduce_chips(qkv_far, chips, fsdp)
+        out_far = second_exchange(out_pairs, [after(item, *qkv_far) for item in out_came])
+        out_grad = reduce_chips(out_far, chips, fsdp)
+        down_away = [
+            swap_fsdp(after(kept[0] + more[0], *qkv_far), items[1])
+            for kept, more, items in zip(down_parts[1::2], down_came, (bits, bits[::-1]))
+        ]
+        down_grad = jnp.concatenate(
+            [
+                (kept[1] + more[1]).astype(F32) + away.astype(F32)
+                for kept, more, away in zip(down_parts[1::2], down_came, down_away)
+            ],
+            axis=1,
+        )
+    else:
+
+        def over(array, axes):
+            return lax.psum_scatter(array, axes, scatter_dimension=0, tiled=True)
+
+        qkv_sum, out_grad = (over(parts[0], BOTH).astype(F32) for parts in (qkv_parts, out_parts))
+        down_grad = over(down_parts[0], "fsdp").astype(F32)
+        gate_back, up_back = (
+            lax.all_to_all(
+                over(parts[0].reshape(-1, padded), "fsdp").reshape(ctx, weight_rows, padded), "ctx", 0, 0
+            )
+            for parts in (gate_parts, up_parts)
+        )
+        input_grad = back_to_input([])
+    branch = lax.psum_scatter(after(branch[0], *early), "ctx", scatter_dimension=0, tiled=True)
+    result = (middle + branch.astype(F32)).astype(BF16)
+    gate_up_grad, norm2_grad = pl.pallas_call(
+        functools.partial(join_kernel, own),
+        out_shape=[struct(gate_up_weight.shape, F32), struct((weight_rows, 1), F32)],
+        compiler_params=params(),
+        name="join",
+    )(gate_back, up_back, gate_up_weight, after(gain_two, input_grad))
     bias_row = lax.dynamic_slice_in_dim(qkv_sum[0], QKV + spot * bias_width, bias_width)
     qkv_sum = qkv_sum[:, :QKV]
-    input_grad = call(
-        functools.partial(input_back_kernel, plan, chips, fsdp, count),
-        struct((rows, width), F32),
-        [info, grad_projected, inputs, grad_middle] + pieces,
-        4,
-        4 + count,
-        [pltpu.VMEM((width, QKV), BF16), pltpu.SemaphoreType.DMA((len(plan or [0]),))],
-        cost(2 * rows * width * QKV, 2 * width * QKV),
-        "input_back",
-    )
     return (
         result[None],
         input_grad[None],

time: 605 us -> 524 us (0.87)
  waiting for transfers between devices: 295 us -> 191 us
  other arithmetic: 17.6 us -> 40.7 us
  Pallas kernels: 148 us -> 160 us
  starting transfers between devices: 103 us -> 91.7 us
    ppermute x21 -> x12, waiting for transfers between devices: 114 us -> 16.9 us  [shift_chip(): lax.ppermute(value, 'ctx', [(i, (i + 2 * steps) % count) for i in range(c...]
    pallas_call x2 -> x6, Pallas kernels: 24.7 us -> 91.3 us  [the longest x2 61.9 us: shards(): pl.pallas_call(functools.partial(feed_kernel, steps, not branch, wide_pla...]
    ppermute x14 -> x0, waiting for transfers between devices: 66.5 us -> none  [send_to(): lax.ppermute(value, 'ctx', [(i, (i + 2 * steps) % count ^ other) for i in...]
    pallas_call x12 -> x9, Pallas kernels: 121 us -> 66.8 us  [call(): pl.pallas_call(kernel, out_shape=outs, in_specs=specs, out_specs=[VMEM_SP...]
    ppermute x14 -> x38, waiting for transfers between devices: 102 us -> 149 us  [swap_fsdp(): return lax.ppermute(value, 'fsdp', [(i, i ^ bit) for i in range(count)])]
    ppermute x14 -> x0, starting transfers between devices: 28.6 us -> none  [send_to(): lax.ppermute(value, 'ctx', [(i, (i + 2 * steps) % count ^ other) for i in...]
    ppermute x14 -> x38, starting transfers between devices: 16.9 us -> 41.9 us  [swap_fsdp(): return lax.ppermute(value, 'fsdp', [(i, i ^ bit) for i in range(count)])]
    add x21 -> x27, other arithmetic: 4.87 us -> 28.1 us  [the longest x4 5.29 us: second_exchange(): away = swap_fsdp(keep[2] + got[2] + more[0], items[1])]
  transfers between devices with their start and end apart: 89 -> 78, of which waited for: 34 -> 33; matrix products, arithmetic and copies ran while one was open for 4% -> 9% of each run, Pallas kernels for 20% -> 23%
where the time goes in v2:
time: 524 us; the launch traced here: 520 us
  waiting for transfers between devices  191 us (36%)
  Pallas kernels  160 us (31%)
  starting transfers between devices  91.7 us (18%)
  other arithmetic  40.7 us (8%)
  local copies, waits for them, and re-layouts  21.5 us (4%)
  between operations  14.8 us (3%)
    ppermute x38, waiting for transfers between devices, swap_fsdp(): return lax.ppermute(value, 'fsdp', [(i, i ^ bit) for i in range(count)])  149 us
    pallas_call x9, Pallas kernels, call(): pl.pallas_call(kernel, out_shape=outs, in_specs=specs, out_specs=[VMEM_SP...  66.8 us
    pallas_call x2, Pallas kernels, shards(): pl.pallas_call(functools.partial(feed_kernel, steps, not branch, wide_pla...  61.9 us
    ppermute x38, starting transfers between devices, swap_fsdp(): return lax.ppermute(value, 'fsdp', [(i, i ^ bit) for i in range(count)])  41.9 us
    ppermute x12, starting transfers between devices, shift_chip(): lax.ppermute(value, 'ctx', [(i, (i + 2 * steps) % count) for i in range(c...  22 us
    pallas_call x2, Pallas kernels, wide_grad(): pl.pallas_call(functools.partial(wide_grad_kernel, items), out_shape=[str...  18.6 us
    ppermute x12, waiting for transfers between devices, shift_chip(): lax.ppermute(value, 'ctx', [(i, (i + 2 * steps) % count) for i in range(c...  16.9 us
  transfers between devices with their start and end apart: 78, of which 33 were waited for; matrix products, arithmetic and copies ran while one was open for 9% of the time, Pallas kernels for 23%

profile of v2, /device:TPU:0, one launch (start us, length us, event | category | flops | bytes accessed | tf_op | source)
XLA Modules:
  0.0 519.6 jit_solution(14639948293626457555)
XLA Ops:
  11.8 5.0 collective-permute-start.5
  33.2 5.5 %collective-permute-done.3.refs_6_ = bf16[280,768]{1,0:T(8,128)(2,1)S(1)} collective-permute-done((bf16[280,768]{1,0:T(8,128)(2,1)S(1)}, bf16[280,768]{1,0:T(8,128)(2,1)S(1)}, u32[]{:S(2)}, u32[]{:S(2)}) %collective-permute-start.3) | collective-permute-done | bytes 430112 | tf_op jit(solution)/shard_map/ppermute | solution.py:73
  43.1 7.4 %collective-permute-done.8 = bf16[48,3712]{1,0:T(8,128)(2,1)} collective-permute-done((bf16[48,3712]{1,0:T(8,128)(2,1)S(1)}, bf16[48,3712]{1,0:T(8,128)(2,1)}, u32[]{:S(2)}, u32[]{:S(2)}) %collective-permute-start.8) | collective-permute-done | bytes 356384 | tf_op jit(solution)/shard_map/ppermute | solution.py:62
  51.4 4.8 all-to-all-start
  61.7 14.7 %collective-permute-done.14.refs_4_.refs_10_.refs_14_ = bf16[96,3712]{1,0:T(8,128)(2,1)S(1)} collective-permute-done((bf16[96,3712]{1,0:T(8,128)(2,1)S(1)}, bf16[96,3712]{1,0:T(8,128)(2,1)S(1)}, u32[]{:S(2)}, u32[]{:S(2)}) %collective-permute-start.14) | collective-permute-done | bytes 712736 | tf_op jit(solution)/shard_map/ppermute | solution.py:73
  77.9 13.4 %collective-permute-done.17.refs_10_.refs_16_.refs_20_ = bf16[96,3712]{1,0:T(8,128)(2,1)S(1)} collective-permute-done((bf16[96,3712]{1,0:T(8,128)(2,1)S(1)}, bf16[96,3712]{1,0:T(8,128)(2,1)S(1)}, u32[]{:S(2)}, u32[]{:S(2)}) %collective-permute-start.17) | collective-permute-done | bytes 712736 | tf_op jit(solution)/shard_map/ppermute | solution.py:73
  92.5 5.8 %all-to-all-done = bf16[8,48,2304]{2,1,0:T(8,128)(2,1)} async-done(((bf16[8,48,2304]{2,1,0:T(8,128)(2,1)}), bf16[8,48,2304]{2,1,0:T(8,128)(2,1)}, u32[]{:S(2)}, u32[]{:S(2)}) %all-to-all-start) | async-done | bytes 1769504 | tf_op jit(solution)/shard_map/all_to_all | solution.py:139
  101.2 14.6 %collective-permute-done.18.refs_6_.refs_12_.refs_16_ = bf16[96,3712]{1,0:T(8,128)(2,1)S(1)} collective-permute-done((bf16[96,3712]{1,0:T(8,128)(2,1)S(1)}, bf16[96,3712]{1,0:T(8,128)(2,1)S(1)}, u32[]{:S(2)}, u32[]{:S(2)}) %collective-permute-start.18) | collective-permute-done | bytes 712736 | tf_op jit(solution)/shard_map/ppermute | solution.py:73
  132.0 6.9 %project.1 = (bf16[128,1536]{1,0:T(8,128)(2,1)}, bf16[128,1536]{1,0:T(8,128)(2,1)}, bf16[128,512]{1,0:T(8,128)(2,1)}) custom-call(s32[2]{0:T(128)} %pad_add_fusion.info_ref, bf16[128,1536]{1,0:T(8,128)(2,1)} %bitcast.118, f32[128,128]{1,0:T(8,128)} %copy.37.cos_ref, f32[128,128]{1,0:T(8,128)} %pad_maximum_fusion.5.sin_ref, bf16[96,3712]{1,0:T(8,128)(2,1)} %copy-done, ...), custom_call_target="tpu_custom_call" | custom-call | flops 1 | bytes 1 | tf_op jit(solution)/shard_map/project/pallas_call | solution.py:591
  140.3 4.6 collective-permute-start.26
  147.3 5.3 %collective-permute-done.26.refs_2_.refs_6_ = bf16[128,512]{1,0:T(8,128)(2,1)S(1)} collective-permute-done((bf16[128,512]{1,0:T(8,128)(2,1)}, bf16[128,512]{1,0:T(8,128)(2,1)S(1)}, u32[]{:S(2)}, u32[]{:S(2)}) %collective-permute-start.26) | collective-permute-done | bytes 131104 | tf_op jit(solution)/shard_map/ppermute | solution.py:68
  154.6 9.5 %attend.1 = (bf16[128,1536]{1,0:T(8,128)(2,1)}, f32[128,1536]{1,0:T(8,128)}, bf16[128,1536]{1,0:T(8,128)(2,1)}) custom-call(s32[2]{0:T(128)} %pad_add_fusion.info_ref, s32[128,1]{1,0:T(8,128)} %copy.38.place_ref, bf16[128,1536]{1,0:T(8,128)(2,1)} %get-tuple-element.121.q_ref, bf16[128,1536]{1,0:T(8,128)(2,1)} %bitcast.119, ...), custom_call_target="tpu_custom_call" | custom-call | flops 1 | bytes 1 | tf_op jit(solution)/shard_map/attend/pallas_call | solution.py:591
  173.1 14.2 %collective-permute-done.32.refs_5_ = bf16[8,48,1152]{2,1,0:T(8,128)(2,1)S(1)} collective-permute-done((bf16[8,48,1152]{2,1,0:T(8,128)(2,1)}, bf16[8,48,1152]{2,1,0:T(8,128)(2,1)S(1)}, u32[]{:S(2)}, u32[]{:S(2)}) %collective-permute-start.32) | collective-permute-done | bytes 884768 | tf_op jit(solution)/shard_map/ppermute | solution.py:73
  187.8 17.8 %collective-permute-done.33.refs_7_ = bf16[8,48,1152]{2,1,0:T(8,128)(2,1)S(1)} collective-permute-done((bf16[8,48,1152]{2,1,0:T(8,128)(2,1)S(1)}, bf16[8,48,1152]{2,1,0:T(8,128)(2,1)S(1)}, u32[]{:S(2)}, u32[]{:S(2)}) %collective-permute-start.33) | collective-permute-done | bytes 884768 | tf_op jit(solution)/shard_map/ppermute | solution.py:73
  214.8 35.8 %feed.2 = (bf16[1024,1536]{1,0:T(8,128)(2,1)}, bf16[2,128,1536]{2,1,0:T(8,128)(2,1)}, bf16[2,128,1536]{2,1,0:T(8,128)(2,1)}, bf16[1152,512]{1,0:T(8,128)(2,1)}, bf16[512,2304]{1,0:T(8,128)(2,1)}) custom-call(s32[2]{0:T(128)} %pad_add_fusion.info_ref, bf16[1024,1536]{1,0:T(8,128)(2,1)} %all-gather.5.cloned.1.call-done.units_ref, ...), custom_call_target="tpu_custom_call" | custom-call | flops 1 | bytes 1 | tf_op jit(solution)/shard_map/feed/pallas_call | solution.py:737
  256.7 4.6 collective-permute-start.35
  261.3 26.2 %feed.3 = (bf16[1024,1536]{1,0:T(8,128)(2,1)}, bf16[2,128,1536]{2,1,0:T(8,128)(2,1)}, bf16[2,128,1536]{2,1,0:T(8,128)(2,1)}, bf16[1152,512]{1,0:T(8,128)(2,1)}, bf16[512,2304]{1,0:T(8,128)(2,1)}) custom-call(s32[2]{0:T(128)} %pad_add_fusion.info_ref, bf16[1024,1536]{1,0:T(8,128)(2,1)} %all-gather.5.cloned.1.call-done.units_ref, ...), custom_call_target="tpu_custom_call", output_to_operand_aliasing={{0}: (12, {})} | custom-call | flops 1 | bytes 1 | tf_op jit(solution)/shard_map/feed/pallas_call | solution.py:737
  287.6 9.4 %wide_grad.2 = (bf16[2,4,48,1152]{3,2,1,0:T(8,128)(2,1)}, bf16[2,4,48,1152]{3,2,1,0:T(8,128)(2,1)}, bf16[2,4,48,1152]{3,2,1,0:T(8,128)(2,1)}, bf16[2,4,48,1152]{3,2,1,0:T(8,128)(2,1)}) custom-call(s32[2]{0:T(128)} %pad_add_fusion.info_ref, bf16[1536,1024]{1,0:T(8,128)(2,1)} %turn.1.turned, bf16[512,2304]{1,0:T(8,128)(2,1)} %get-tuple-element.136.refs_0_, ...), custom_call_target="tpu_custom_call" | custom-call | flops 1 | bytes 1 | tf_op jit(solution)/shard_map/wide_grad/pallas_call | solution.py:781
  299.7 9.2 %wide_grad.3 = (bf16[2,4,48,1152]{3,2,1,0:T(8,128)(2,1)}, bf16[2,4,48,1152]{3,2,1,0:T(8,128)(2,1)}, bf16[2,4,48,1152]{3,2,1,0:T(8,128)(2,1)}, bf16[2,4,48,1152]{3,2,1,0:T(8,128)(2,1)}) custom-call(s32[2]{0:T(128)} %pad_add_fusion.info_ref, bf16[1536,1024]{1,0:T(8,128)(2,1)} %turn.1.turned, bf16[512,2304]{1,0:T(8,128)(2,1)} %get-tuple-element.136.refs_0_, ...), custom_call_target="tpu_custom_call" | custom-call | flops 1 | bytes 1 | tf_op jit(solution)/shard_map/wide_grad/pallas_call | solution.py:781
  313.2 6.6 %collective-permute-done.37 = bf16[2,4,48,1152]{3,2,1,0:T(8,128)(2,1)S(1)} collective-permute-done((bf16[2,4,48,1152]{3,2,1,0:T(8,128)(2,1)}, bf16[2,4,48,1152]{3,2,1,0:T(8,128)(2,1)S(1)}, u32[]{:S(2)}, u32[]{:S(2)}) %collective-permute-start.37) | collective-permute-done | bytes 884768 | tf_op jit(solution)/shard_map/ppermute | solution.py:73
  322.6 15.7 %collective-permute-done.41 = bf16[2,4,48,1152]{3,2,1,0:T(8,128)(2,1)S(1)} collective-permute-done((bf16[2,4,48,1152]{3,2,1,0:T(8,128)(2,1)}, bf16[2,4,48,1152]{3,2,1,0:T(8,128)(2,1)S(1)}, u32[]{:S(2)}, u32[]{:S(2)}) %collective-permute-start.41) | collective-permute-done | bytes 884768 | tf_op jit(solution)/shard_map/ppermute | solution.py:73
  340.0 14.3 %middle_back.1 = (f32[128,1536]{1,0:T(8,128)}, bf16[128,1536]{1,0:T(8,128)(2,1)}, f32[128,1536]{1,0:T(8,128)}, bf16[3,128,512]{2,1,0:T(8,128)(2,1)}, bf16[3,128,512]{2,1,0:T(8,128)(2,1)}) custom-call(s32[2]{0:T(128)} %pad_add_fusion.info_ref, s32[128,1]{1,0:T(8,128)} %copy.38.place_ref, bf16[128,1536]{1,0:T(8,128)(2,1)} %get-tuple-element.121.q_ref, ...), custom_call_target="tpu_custom_call" | custom-call | flops 1 | bytes 1 | tf_op jit(solution)/shard_map/middle_back/pallas_call | solution.py:591
  354.3 4.9 out_grad.1
  365.5 7.7 %down_grad.1 = (bf16[2,280,768]{2,1,0:T(8,128)(2,1)}, bf16[2,280,768]{2,1,0:T(8,128)(2,1)}, bf16[2,280,768]{2,1,0:T(8,128)(2,1)}, bf16[2,280,768]{2,1,0:T(8,128)(2,1)}) custom-call(s32[2]{0:T(128)} %pad_add_fusion.info_ref, bf16[1024,1536]{1,0:T(8,128)(2,1)} %all-gather.3.cloned.1.call-done.cots_ref, bf16[1152,512]{1,0:T(8,128)(2,1)} %get-tuple-element.153.refs_0_, ...), custom_call_target="tpu_custom_call" | custom-call | flops 1 | bytes 1 | tf_op jit(solution)/shard_map/down_grad/pallas_call | solution.py:591
  381.8 6.6 %projected_back.1 = (bf16[128,2048]{1,0:T(8,128)(2,1)}, bf16[4,2,48,2176]{3,2,1,0:T(8,128)(2,1)}, bf16[4,2,48,2176]{3,2,1,0:T(8,128)(2,1)}, bf16[4,2,48,2176]{3,2,1,0:T(8,128)(2,1)}, bf16[4,2,48,2176]{3,2,1,0:T(8,128)(2,1)}) custom-call(s32[2]{0:T(128)} %pad_add_fusion.info_ref, f32[128,1536]{1,0:T(8,128)} %get-tuple-element.161.dq_ref, ...), custom_call_target="tpu_custom_call" | custom-call | flops 1 | bytes 1 | tf_op jit(solution)/shard_map/projected_back/pallas_call | solution.py:591
  388.4 7.8 %input_back.1 = f32[128,1536]{1,0:T(8,128)} custom-call(s32[2]{0:T(128)} %pad_add_fusion.info_ref, bf16[128,2048]{1,0:T(8,128)(2,1)} %get-tuple-element.164.gp_ref, bf16[128,1536]{1,0:T(8,128)(2,1)} %bitcast.120, f32[128,1536]{1,0:T(8,128)} %get-tuple-element.165.middle_ref, bf16[96,3712]{1,0:T(8,128)(2,1)} %copy-done, bf16[96,3712]{1,0:T(8,128)(2,1)} %copy-done.7, ...), custom_call_target="tpu_custom_call" | custom-call | flops 1 | bytes 1 | tf_op jit(solution)/shard_map/input_back/pallas_call | solution.py:591
  396.2 5.7 %all-to-all-start.1 = ((bf16[8,48,1152]{2,1,0:T(8,128)(2,1)}), bf16[8,48,1152]{2,1,0:T(8,128)(2,1)S(1)}, u32[]{:S(2)}, u32[]{:S(2)}) async-start(bf16[8,48,1152]{2,1,0:T(8,128)(2,1)} %pad_maximum_fusion.1), calls=%async_computation.2 | async-start | bytes 1769472 | tf_op jit(solution)/shard_map/all_to_all | solution.py:813
  411.8 25.2 %collective-permute-done.54 = bf16[2,2,48,1536]{3,2,1,0:T(8,128)(2,1)S(1)} collective-permute-done((bf16[2,2,48,1536]{3,2,1,0:T(8,128)(2,1)S(1)}, bf16[2,2,48,1536]{3,2,1,0:T(8,128)(2,1)S(1)}, u32[]{:S(2)}, u32[]{:S(2)}) %collective-permute-start.54) | collective-permute-done | bytes 589856 | tf_op jit(solution)/shard_map/ppermute | solution.py:73
  443.7 4.7 all-to-all-start.2
  448.4 9.2 %collective-permute-done.61 = bf16[2,2,48,2176]{3,2,1,0:T(8,128)(2,1)} collective-permute-done((bf16[2,2,48,2176]{3,2,1,0:T(8,128)(2,1)}, bf16[2,2,48,2176]{3,2,1,0:T(8,128)(2,1)}, u32[]{:S(2)}, u32[]{:S(2)}) %collective-permute-start.61) | collective-permute-done | bytes 835616 | tf_op jit(solution)/shard_map/ppermute | solution.py:73
  462.6 6.8 %collective-permute-done.62 = bf16[2,48,2176]{2,1,0:T(8,128)(2,1)S(1)} collective-permute-done((bf16[2,48,2176]{2,1,0:T(8,128)(2,1)S(1)}, bf16[2,48,2176]{2,1,0:T(8,128)(2,1)S(1)}, u32[]{:S(2)}, u32[]{:S(2)}) %collective-permute-start.62) | collective-permute-done | bytes 417824 | tf_op jit(solution)/shard_map/ppermute | solution.py:73
  483.7 6.8 %join.1 = (f32[48,17920]{1,0:T(8,128)}, f32[48,1]{1,0:T(8,128)}) custom-call(bf16[8,48,1152]{2,1,0:T(8,128)(2,1)} %copy-done.11, bf16[8,48,1152]{2,1,0:T(8,128)(2,1)} %copy-done.12, bf16[48,17920]{1,0:T(8,128)(2,1)} %weight_ref.3, f32[48,1]{1,0:T(8,128)} %copy.41.gain_ref), custom_call_target="tpu_custom_call" | custom-call | tf_op jit(solution)/shard_map/join/pallas_call | solution.py:957
  (359 shorter events, 168.1 us)
Async XLA Ops:
  51.4 46.9 %all-to-all-start = ((bf16[8,48,2304]{2,1,0:T(8,128)(2,1)}), bf16[8,48,2304]{2,1,0:T(8,128)(2,1)}, u32[]{:S(2)}, u32[]{:S(2)}) async-start(bf16[8,48,2304]{2,1,0:T(8,128)(2,1)} %split.1), calls=%async_computation | async-start | bytes 3538944 | tf_op jit(solution)/shard_map/all_to_all | solution.py:139
  56.2 108.0 %all-gather.3.cloned.1.call-start = ((), (), s32[]{:S(2)}) async-start(), calls=%async_computation.4 | async-start | bytes 3538944 | tf_op jit(solution)/shard_map/all_gather | solution.py:691
  60.6 30.7 %collective-permute-start.17 = (bf16[96,3712]{1,0:T(8,128)(2,1)S(1)}, bf16[96,3712]{1,0:T(8,128)(2,1)S(1)}, u32[]{:S(2)}, u32[]{:S(2)}) collective-permute-start(bf16[96,3712]{1,0:T(8,128)(2,1)S(1)} %pad_maximum_fusion.4.refs_8_.refs_14_.refs_18_), channel_id=1, source_target_pairs={{0,2},{1,3},{2,0},{3,1},{4,6},{5,7},{6,4},{7,5},{8,10},{9,11},{10,... | collective-permute-start | bytes 2138120 | tf_op jit(solution)/shard_map/ppermute | solution.py:73
  61.2 31.3 %collective-permute-start.16 = (bf16[96,3712]{1,0:T(8,128)(2,1)S(1)}, bf16[96,3712]{1,0:T(8,128)(2,1)}, u32[]{:S(2)}, u32[]{:S(2)}) collective-permute-start(bf16[96,3712]{1,0:T(8,128)(2,1)S(1)} %pad_maximum_fusion.4.refs_8_.refs_14_.refs_18_), channel_id=1, source_target_pairs={{0,1},{1,0},{2,3},{3,2},{4,5},{5,4},{6,7},{7,6},{8,9},{9,8},{10,11... | collective-permute-start | bytes 2138120 | tf_op jit(solution)/shard_map/ppermute | solution.py:73
  118.1 92.1 %all-gather.5.cloned.1.call-start = ((), (), s32[]{:S(2)}) async-start(), calls=%async_computation.5 | async-start | bytes 3538944 | tf_op jit(solution)/shard_map/all_gather | solution.py:722
  128.4 24.9 %collective-permute-start.10 = (bf16[8,48,1152]{2,1,0:T(8,128)(2,1)}, bf16[8,48,1152]{2,1,0:T(8,128)(2,1)S(1)}, u32[]{:S(2)}, u32[]{:S(2)}) collective-permute-start(bf16[8,48,1152]{2,1,0:T(8,128)(2,1)} %get-tuple-element.197.refs_4_), channel_id=1, source_target_pairs={{0,2},{1,3},{2,0},{3,1},{4,6},{5,7},{6,4},{7,5},{8,10},{9,11},{10,... | collective-permute-start | bytes 2654216 | tf_op jit(solution)/shard_map/ppermute | solution.py:73
  129.2 24.1 %collective-permute-start.9 = (bf16[8,48,1152]{2,1,0:T(8,128)(2,1)}, bf16[8,48,1152]{2,1,0:T(8,128)(2,1)S(1)}, u32[]{:S(2)}, u32[]{:S(2)}) collective-permute-start(bf16[8,48,1152]{2,1,0:T(8,128)(2,1)} %get-tuple-element.198.refs_0_), channel_id=1, source_target_pairs={{0,1},{1,0},{2,3},{3,2},{4,5},{5,4},{6,7},{7,6},{8,9},{9,8},{10,11... | collective-permute-start | bytes 2654216 | tf_op jit(solution)/shard_map/ppermute | solution.py:73
  164.2 346.8 %reduce-scatter.2.cloned.1.call-start = ((), (), s32[]{:S(2)}) async-start(), calls=%async_computation.6 | async-start | bytes 3538944 | tf_op jit(solution)/shard_map/reduce_scatter | solution.py:955
  164.5 22.7 %collective-permute-start.32 = (bf16[8,48,1152]{2,1,0:T(8,128)(2,1)}, bf16[8,48,1152]{2,1,0:T(8,128)(2,1)S(1)}, u32[]{:S(2)}, u32[]{:S(2)}) collective-permute-start(bf16[8,48,1152]{2,1,0:T(8,128)(2,1)} %get-tuple-element.197.refs_4_), channel_id=1, source_target_pairs={{0,1},{1,0},{2,3},{3,2},{4,5},{5,4},{6,7},{7,6},{8,9},{9,8},{10,11... | collective-permute-start | bytes 2654216 | tf_op jit(solution)/shard_map/ppermute | solution.py:73
  165.1 22.7 %collective-permute-start.30 = (bf16[8,48,1152]{2,1,0:T(8,128)(2,1)}, bf16[8,48,1152]{2,1,0:T(8,128)(2,1)S(1)}, u32[]{:S(2)}, u32[]{:S(2)}) collective-permute-start(bf16[8,48,1152]{2,1,0:T(8,128)(2,1)} %get-tuple-element.198.refs_0_), channel_id=1, source_target_pairs={{0,2},{1,3},{2,0},{3,1},{4,6},{5,7},{6,4},{7,5},{8,10},{9,11},{10,... | collective-permute-start | bytes 2654216 | tf_op jit(solution)/shard_map/ppermute | solution.py:73
  166.3 39.3 %collective-permute-start.33 = (bf16[8,48,1152]{2,1,0:T(8,128)(2,1)S(1)}, bf16[8,48,1152]{2,1,0:T(8,128)(2,1)S(1)}, u32[]{:S(2)}, u32[]{:S(2)}) collective-permute-start(bf16[8,48,1152]{2,1,0:T(8,128)(2,1)S(1)} %collective-permute-done.10.refs_6_), channel_id=1, source_target_pairs={{0,1},{1,0},{2,3},{3,2},{4,5},{5,4},{6,7},{7,6},{8,9},{9,8},{10,11... | collective-permute-start | bytes 2654216 | tf_op jit(solution)/shard_map/ppermute | solution.py:73
  167.7 38.8 %collective-permute-start.31 = (bf16[8,48,1152]{2,1,0:T(8,128)(2,1)S(1)}, bf16[8,48,1152]{2,1,0:T(8,128)(2,1)}, u32[]{:S(2)}, u32[]{:S(2)}) collective-permute-start(bf16[8,48,1152]{2,1,0:T(8,128)(2,1)S(1)} %collective-permute-done.9.refs_1_), channel_id=1, source_target_pairs={{0,2},{1,3},{2,0},{3,1},{4,6},{5,7},{6,4},{7,5},{8,10},{9,11},{10,... | collective-permute-start | bytes 2654216 | tf_op jit(solution)/shard_map/ppermute | solution.py:73
  254.3 33.2 %collective-permute-start.36 = (bf16[128,1536]{1,0:T(8,128)(2,1)S(1)}, bf16[128,1536]{1,0:T(8,128)(2,1)S(1)}, u32[]{:S(2)}, u32[]{:S(2)}) collective-permute-start(bf16[128,1536]{1,0:T(8,128)(2,1)S(1)} %get-tuple-element.201), channel_id=1, source_target_pairs={{0,24},{4,28},{8,0},{12,4},{16,8},{20,12},{24,16},{28,20},{1,25},{... | collective-permute-start | bytes 1179656 | tf_op jit(solution)/shard_map/ppermute | solution.py:62
  256.7 30.8 %collective-permute-start.35 = (bf16[128,1536]{1,0:T(8,128)(2,1)S(1)}, bf16[128,1536]{1,0:T(8,128)(2,1)S(1)}, u32[]{:S(2)}, u32[]{:S(2)}) collective-permute-start(bf16[128,1536]{1,0:T(8,128)(2,1)S(1)} %get-tuple-element.202), channel_id=1, source_target_pairs={{0,16},{4,20},{8,24},{12,28},{16,0},{20,4},{24,8},{28,12},{1,17},{... | collective-permute-start | bytes 1179656 | tf_op jit(solution)/shard_map/ppermute | solution.py:62
  287.5 22.9 %collective-permute-start.39 = (bf16[2,128,1536]{2,1,0:T(8,128)(2,1)}, bf16[2,128,1536]{2,1,0:T(8,128)(2,1)S(1)}, u32[]{:S(2)}, u32[]{:S(2)}) collective-permute-start(bf16[2,128,1536]{2,1,0:T(8,128)(2,1)} %get-tuple-element.145), channel_id=1, source_target_pairs={{0,4},{4,0},{8,12},{12,8},{16,20},{20,16},{24,28},{28,24},{1,5},{5... | collective-permute-start | bytes 2359304 | tf_op jit(solution)/shard_map/ppermute | solution.py:57
  297.1 22.7 %collective-permute-start.37 = (bf16[2,4,48,1152]{3,2,1,0:T(8,128)(2,1)}, bf16[2,4,48,1152]{3,2,1,0:T(8,128)(2,1)S(1)}, u32[]{:S(2)}, u32[]{:S(2)}) collective-permute-start(bf16[2,4,48,1152]{3,2,1,0:T(8,128)(2,1)} %get-tuple-element.138), channel_id=1, source_target_pairs={{0,1},{1,0},{2,3},{3,2},{4,5},{5,4},{6,7},{7,6},{8,9},{9,8},{10,11... | collective-permute-start | bytes 2654216 | tf_op jit(solution)/shard_map/ppermute | solution.py:73
  298.2 22.7 %collective-permute-start.38 = (bf16[2,4,48,1152]{3,2,1,0:T(8,128)(2,1)}, bf16[2,4,48,1152]{3,2,1,0:T(8,128)(2,1)S(1)}, u32[]{:S(2)}, u32[]{:S(2)}) collective-permute-start(bf16[2,4,48,1152]{3,2,1,0:T(8,128)(2,1)} %get-tuple-element.141), channel_id=1, source_target_pairs={{0,2},{1,3},{2,0},{3,1},{4,6},{5,7},{6,4},{7,5},{8,10},{9,11},{10,... | collective-permute-start | bytes 2654216 | tf_op jit(solution)/shard_map/ppermute | solution.py:73
  308.9 29.4 %collective-permute-start.41 = (bf16[2,4,48,1152]{3,2,1,0:T(8,128)(2,1)}, bf16[2,4,48,1152]{3,2,1,0:T(8,128)(2,1)S(1)}, u32[]{:S(2)}, u32[]{:S(2)}) collective-permute-start(bf16[2,4,48,1152]{3,2,1,0:T(8,128)(2,1)} %get-tuple-element.140), channel_id=1, source_target_pairs={{0,1},{1,0},{2,3},{3,2},{4,5},{5,4},{6,7},{7,6},{8,9},{9,8},{10,11... | collective-permute-start | bytes 2654216 | tf_op jit(solution)/shard_map/ppermute | solution.py:73
  309.9 49.4 %collective-permute-start.42 = (bf16[2,4,48,1152]{3,2,1,0:T(8,128)(2,1)}, bf16[2,4,48,1152]{3,2,1,0:T(8,128)(2,1)S(1)}, u32[]{:S(2)}, u32[]{:S(2)}) collective-permute-start(bf16[2,4,48,1152]{3,2,1,0:T(8,128)(2,1)} %get-tuple-element.150), channel_id=1, source_target_pairs={{0,2},{1,3},{2,0},{3,1},{4,6},{5,7},{6,4},{7,5},{8,10},{9,11},{10,... | collective-permute-start | bytes 2654216 | tf_op jit(solution)/shard_map/ppermute | solution.py:73
  311.3 27.9 %collective-permute-start.40 = (bf16[128,1536]{1,0:T(8,128)(2,1)S(1)}, bf16[128,1536]{1,0:T(8,128)(2,1)S(1)}, u32[]{:S(2)}, u32[]{:S(2)}) collective-permute-start(bf16[128,1536]{1,0:T(8,128)(2,1)S(1)} %get-tuple-element.199), channel_id=1, source_target_pairs={{0,8},{4,12},{8,16},{12,20},{16,24},{20,28},{24,0},{28,4},{1,9},{5... | collective-permute-start | bytes 1179656 | tf_op jit(solution)/shard_map/ppermute | solution.py:62
  362.8 45.3 %collective-permute-start.53 = (bf16[4,2,48,1536]{3,2,1,0:T(8,128)(2,1)}, bf16[4,2,48,1536]{3,2,1,0:T(8,128)(2,1)S(1)}, u32[]{:S(2)}, u32[]{:S(2)}) collective-permute-start(bf16[4,2,48,1536]{3,2,1,0:T(8,128)(2,1)} %get-tuple-element.175), channel_id=1, source_target_pairs={{0,4},{4,0},{8,12},{12,8},{16,20},{20,16},{24,28},{28,24},{1,5},{5... | collective-permute-start | bytes 3538952 | tf_op jit(solution)/shard_map/ppermute | solution.py:57
  362.8 45.8 %collective-permute-start.51 = (bf16[4,2,48,1536]{3,2,1,0:T(8,128)(2,1)}, bf16[4,2,48,1536]{3,2,1,0:T(8,128)(2,1)S(1)}, u32[]{:S(2)}, u32[]{:S(2)}) collective-permute-start(bf16[4,2,48,1536]{3,2,1,0:T(8,128)(2,1)} %get-tuple-element.172), channel_id=1, source_target_pairs={{0,4},{4,0},{8,12},{12,8},{16,20},{20,16},{24,28},{28,24},{1,5},{5... | collective-permute-start | bytes 3538952 | tf_op jit(solution)/shard_map/ppermute | solution.py:57
  374.7 28.0 %collective-permute-start.49 = (bf16[4,48,1152]{2,1,0:T(8,128)(2,1)}, bf16[4,48,1152]{2,1,0:T(8,128)(2,1)}, u32[]{:S(2)}, u32[]{:S(2)}) collective-permute-start(bf16[4,48,1152]{2,1,0:T(8,128)(2,1)} %fusion.9), channel_id=1, source_target_pairs={{0,2},{1,3},{2,0},{3,1},{4,6},{5,7},{6,4},{7,5},{8,10},{9,11},{10,... | collective-permute-start | bytes 1327112 | tf_op jit(solution)/shard_map/ppermute | solution.py:73
  378.5 27.0 %collective-permute-start.50 = (bf16[4,48,1152]{2,1,0:T(8,128)(2,1)}, bf16[4,48,1152]{2,1,0:T(8,128)(2,1)}, u32[]{:S(2)}, u32[]{:S(2)}) collective-permute-start(bf16[4,48,1152]{2,1,0:T(8,128)(2,1)} %fusion.8), channel_id=1, source_target_pairs={{0,1},{1,0},{2,3},{3,2},{4,5},{5,4},{6,7},{7,6},{8,9},{9,8},{10,11... | collective-permute-start | bytes 1327112 | tf_op jit(solution)/shard_map/ppermute | solution.py:73
  380.8 59.9 %collective-permute-start.56 = (bf16[2,280,768]{2,1,0:T(8,128)(2,1)}, bf16[2,280,768]{2,1,0:T(8,128)(2,1)}, u32[]{:S(2)}, u32[]{:S(2)}) collective-permute-start(bf16[2,280,768]{2,1,0:T(8,128)(2,1)} %get-tuple-element.178), channel_id=1, source_target_pairs={{0,1},{1,0},{2,3},{3,2},{4,5},{5,4},{6,7},{7,6},{8,9},{9,8},{10,11... | collective-permute-start | bytes 2580488 | tf_op jit(solution)/shard_map/ppermute | solution.py:73
  396.2 47.5 %all-to-all-start.1 = ((bf16[8,48,1152]{2,1,0:T(8,128)(2,1)}), bf16[8,48,1152]{2,1,0:T(8,128)(2,1)S(1)}, u32[]{:S(2)}, u32[]{:S(2)}) async-start(bf16[8,48,1152]{2,1,0:T(8,128)(2,1)} %pad_maximum_fusion.1), calls=%async_computation.2 | async-start | bytes 1769472 | tf_op jit(solution)/shard_map/all_to_all | solution.py:813
  402.7 38.0 %collective-permute-start.57 = (bf16[2,280,768]{2,1,0:T(8,128)(2,1)}, bf16[2,280,768]{2,1,0:T(8,128)(2,1)S(1)}, u32[]{:S(2)}, u32[]{:S(2)}) collective-permute-start(bf16[2,280,768]{2,1,0:T(8,128)(2,1)} %get-tuple-element.180), channel_id=1, source_target_pairs={{0,2},{1,3},{2,0},{3,1},{4,6},{5,7},{6,4},{7,5},{8,10},{9,11},{10,... | collective-permute-start | bytes 2580488 | tf_op jit(solution)/shard_map/ppermute | solution.py:73
  408.1 30.5 %collective-permute-start.48 = (bf16[4,2,48,2176]{3,2,1,0:T(8,128)(2,1)S(1)}, bf16[4,2,48,2176]{3,2,1,0:T(8,128)(2,1)S(1)}, u32[]{:S(2)}, u32[]{:S(2)}) collective-permute-start(bf16[4,2,48,2176]{3,2,1,0:T(8,128)(2,1)S(1)} %copy-done.75), channel_id=1, source_target_pairs={{0,4},{4,0},{8,12},{12,8},{16,20},{20,16},{24,28},{28,24},{1,5},{5... | collective-permute-start | bytes 5013512 | tf_op jit(solution)/shard_map/ppermute | solution.py:57
  408.6 28.4 %collective-permute-start.54 = (bf16[2,2,48,1536]{3,2,1,0:T(8,128)(2,1)S(1)}, bf16[2,2,48,1536]{3,2,1,0:T(8,128)(2,1)S(1)}, u32[]{:S(2)}, u32[]{:S(2)}) collective-permute-start(bf16[2,2,48,1536]{3,2,1,0:T(8,128)(2,1)S(1)} %slice_add_fusion.2), channel_id=1, source_target_pairs={{0,2},{1,3},{2,0},{3,1},{4,6},{5,7},{6,4},{7,5},{8,10},{9,11},{10,... | collective-permute-start | bytes 1769480 | tf_op jit(solution)/shard_map/ppermute | solution.py:73
  409.8 27.2 %collective-permute-start.52 = (bf16[2,2,48,1536]{3,2,1,0:T(8,128)(2,1)S(1)}, bf16[2,2,48,1536]{3,2,1,0:T(8,128)(2,1)S(1)}, u32[]{:S(2)}, u32[]{:S(2)}) collective-permute-start(bf16[2,2,48,1536]{3,2,1,0:T(8,128)(2,1)S(1)} %slice_add_fusion.3), channel_id=1, source_target_pairs={{0,1},{1,0},{2,3},{3,2},{4,5},{5,4},{6,7},{7,6},{8,9},{9,8},{10,11... | collective-permute-start | bytes 1769480 | tf_op jit(solution)/shard_map/ppermute | solution.py:73
  443.7 39.1 %all-to-all-start.2 = ((bf16[8,48,1152]{2,1,0:T(8,128)(2,1)}), bf16[8,48,1152]{2,1,0:T(8,128)(2,1)S(1)}, u32[]{:S(2)}, u32[]{:S(2)}) async-start(bf16[8,48,1152]{2,1,0:T(8,128)(2,1)} %pad_maximum_fusion.2), calls=%async_computation.3 | async-start | bytes 1769472 | tf_op jit(solution)/shard_map/all_to_all | solution.py:813
  481.2 20.8 %collective-permute-start.65 = (bf16[2,48,1536]{2,1,0:T(8,128)(2,1)S(1)}, bf16[2,48,1536]{2,1,0:T(8,128)(2,1)S(1)}, u32[]{:S(2)}, u32[]{:S(2)}) collective-permute-start(bf16[2,48,1536]{2,1,0:T(8,128)(2,1)S(1)} %fusion.39), channel_id=1, source_target_pairs={{0,2},{1,3},{2,0},{3,1},{4,6},{5,7},{6,4},{7,5},{8,10},{9,11},{10,... | collective-permute-start | bytes 884744 | tf_op jit(solution)/shard_map/ppermute | solution.py:73
  (123 other events, 1414.8 us)
Sparse Core Ops, SparseCore 0:
  118.2 38.0 all-gather.2
  164.3 45.8 all-gather.4
  299.8 46.7 reduce-scatter.1

commit v3 on v2

--- a/solution.py
+++ b/solution.py
@@ -317,17 +317,31 @@
     return pl.ds(pl.multiple_of(chip * 2 * rows, 2 * rows), 2 * rows)
 
 
-def feed_kernel(
-    steps, first, plan, chips, fsdp, own, padded, count, info_ref, units_ref, cots_ref, *refs
-):
-    pieces, down_ref = refs[: 2 * count], refs[2 * count]
-    refs = refs[2 * count + (1 if first else 2) :]
-    branch_ref, mine_ref, other_ref, hidden_ref, grad_ref = refs[:5]
-    x, c, gate_w, up_w, down, acc_units, acc_branch, branch, gate_sems, up_sems, sems = refs[5:]
+def hidden_grad_kernel(steps, chips, rows, padded, info_ref, cots_ref, down_ref, out_ref):
+    own = down_ref.shape[0]
+    for index, step in enumerate(steps):
+        part = dot_nt(cots_ref[tokens_of(info_ref, step, chips, rows), :], down_ref[...]).astype(BF16)
+        out_ref[index * 2 * rows : (index + 1) * 2 * rows, :own] = part
+        if padded > own:
+            out_ref[index * 2 * rows : (index + 1) * 2 * rows, own:] = jnp.zeros((2 * rows, padded - own), BF16)
+
+
+def branch_kernel(groups, chips, rows, info_ref, down_ref, *refs):
+    hiddens, out_ref = refs[:-1], refs[-1]
+    own = down_ref.shape[0]
+    for steps, hidden in zip(groups, hiddens):
+        for index, step in enumerate(steps):
+            part = hidden[:own, index * 2 * rows : (index + 1) * 2 * rows]
+            out_ref[tokens_of(info_ref, step, chips, rows), :] = dot_tn(part, down_ref[...]).astype(BF16)
+
+
+def feed_kernel(steps, offset, plan, chips, fsdp, padded, count, info_ref, units_ref, c_ref, *refs):
+    pieces, refs = refs[: 2 * count], refs[2 * count :]
+    mine_ref, other_ref, hidden_ref, grad_ref = refs[:4]
+    x, c, gate_w, up_w, acc_units, gate_sems, up_sems, sems = refs[4:]
     _, rows, width = mine_ref.shape
     block_rows = width // (2 * chips * fsdp)
-    spans = [tokens_of(info_ref, step, chips, rows) for step in steps]
-    places = [pl.ds(index * 2 * rows, 2 * rows) for index in range(len(steps))]
+    tokens = 2 * rows * len(steps)
 
     def loads(parts, whole, part_sems):
         if plan is None:
@@ -343,20 +357,18 @@
         return copies
 
     x_loads = [
-        pltpu.make_async_copy(units_ref.at[span], x.at[place], sems.at[index])
-        for index, (span, place) in enumerate(zip(spans, places))
+        pltpu.make_async_copy(
+            units_ref.at[tokens_of(info_ref, step, chips, rows)],
+            x.at[pl.ds(index * 2 * rows, 2 * rows)],
+            sems.at[index],
+        )
+        for index, step in enumerate(steps)
     ]
-    c_loads = [
-        pltpu.make_async_copy(cots_ref.at[span], c.at[place], sems.at[len(steps) + index])
-        for index, (span, place) in enumerate(zip(spans, places))
-    ]
-    c_loads.append(pltpu.make_async_copy(down_ref, down.at[pl.ds(0, own)], sems.at[2 * len(steps)]))
+    c_load = pltpu.make_async_copy(c_ref.at[pl.ds(offset, tokens)], c, sems.at[len(steps)])
     gate_loads = loads(pieces[:count], gate_w, gate_sems)
     up_loads = loads(pieces[count:], up_w, up_sems)
-    for copy in x_loads + gate_loads + up_loads + c_loads:
+    for copy in x_loads + gate_loads + up_loads + [c_load]:
         copy.start()
-    if padded > own:
-        down[own:, :] = jnp.zeros((padded - own, width), BF16)
     block = 384 if padded % 384 == 0 else LANES
     for copy in x_loads + gate_loads:
         copy.wait()
@@ -369,9 +381,8 @@
                 copy.wait()
         up = dot_nn(x[...], up_w[:, cols])
         if at == 0:
-            for copy in c_loads:
-                copy.wait()
-        grad_hidden = dot_nt(c[...], down[cols, :])
+            c_load.wait()
+        grad_hidden = c[:, cols].astype(F32)
         sig = 1.0 / (1.0 + jnp.exp(-gate))
         swished = gate * sig
         hidden = (swished * up).astype(BF16)
@@ -381,20 +392,10 @@
         grad_ref[:, cols] = grad_gate
         grad_ref[:, cols_up] = grad_up
         units = dot_nt(grad_gate, gate_w[:, cols]) + dot_nt(grad_up, up_w[:, cols])
-        more = dot_nn(hidden, down[cols, :])
         if at == 0:
             acc_units[...] = units
-            acc_branch[...] = more
         else:
             acc_units[...] += units
-            acc_branch[...] += more
-    branch[...] = acc_branch[...].astype(BF16)
-    stores = [
-        pltpu.make_async_copy(branch.at[place], branch_ref.at[span], sems.at[index])
-        for index, (span, place) in enumerate(zip(spans, places))
-    ]
-    for copy in stores:
-        copy.start()
     core = info_ref[0] % 2
     for index in range(len(steps)):
         start = index * 2 * rows
@@ -402,8 +403,15 @@
         other = pl.ds(pl.multiple_of(start + (1 - core) * rows, rows), rows)
         mine_ref[index] = acc_units[mine, :].astype(BF16)
         other_ref[index] = acc_units[other, :].astype(BF16)
-    for copy in stores:
-        copy.wait()
+
+
+def sum_kernel(plan, count, info_ref, *refs):
+    for terms, out_ref in zip(plan, refs[count:]):
+        total = None
+        for number, index in terms:
+            term = (refs[number][...] if index is None else refs[number][index]).astype(F32)
+            total = term if total is None else total + term
+        out_ref[...] = total.astype(out_ref.dtype)
 
 
 def turn_kernel(steps, chips, rows, info_ref, units_ref, out_ref):
@@ -598,6 +606,30 @@
         cost_estimate=estimate,
         name=name,
     )(*ins)
+
+
+def sums(when, *outs):
+    arrays, plan, shapes = [], [], []
+    for terms in outs:
+        row = []
+        for array, index in terms:
+            row.append((len(arrays), index))
+            arrays.append(array)
+        array, index = terms[0]
+        shape = array.shape
+        if isinstance(index, slice):
+            shape = (len(range(*index.indices(shape[0]))),) + shape[1:]
+        elif index is not None:
+            shape = shape[1:]
+        plan.append(row)
+        shapes.append(struct(shape, BF16))
+    return call(
+        functools.partial(sum_kernel, plan, len(arrays)),
+        shapes,
+        [when] + arrays,
+        estimate=cost(0, 0),
+        name="sums",
+    )
 
 
 def shards(
@@ -721,58 +753,60 @@
 
     all_units = lax.all_gather(after(unit_two, all_cots), "ctx", axis=0, tiled=True)
     order = list(range(2, chips - 1)) + [1, chips - 1, 0] if chips > 2 else list(range(chips))[::-1]
+    hidden_grads = call(
+        functools.partial(hidden_grad_kernel, order, chips, rows, padded),
+        struct((ctx * rows, padded), BF16),
+        [info, all_cots, w_down],
+        estimate=cost(0, 0),
+        name="hidden_grad",
+    )
     turned = call(
         functools.partial(turn_kernel, order, chips, rows),
         struct((width, ctx * rows), BF16),
-        [after(info, w_down, *wide_pieces), all_units],
+        [after(info, hidden_grads, *wide_pieces), all_units],
         estimate=cost(0, 4 * ctx * rows * width),
         name="turn",
     )
     half = len(order) // 2
-    fed, unit_parts, branch, when = [], {}, [], turned
-    for steps in (order[:half], order[half:]):
+    fed, unit_parts, when = [], {}, turned
+    groups = (order[:half], order[half:])
+    plan_count = len(wide_plan or [0])
+    for steps in groups:
         tokens_now = 2 * rows * len(steps)
-        plan_count = len(wide_plan or [0])
-        operands = [after(info, when), all_units, all_cots] + wide_pieces + [w_down] + branch
-        branch_now, mine, other, hidden, grads = pl.pallas_call(
+        mine, other, hidden, grads = call(
             functools.partial(
-                feed_kernel, steps, not branch, wide_plan, chips, fsdp, own, padded, wide_count
+                feed_kernel, steps, 2 * rows * order.index(steps[0]), wide_plan, chips, fsdp, padded, wide_count
             ),
-            out_shape=[
-                struct((ctx * rows, width), BF16),
+            [
                 struct((len(steps), rows, width), BF16),
                 struct((len(steps), rows, width), BF16),
                 struct((padded, tokens_now), BF16),
                 struct((tokens_now, 2 * padded), BF16),
             ],
-            in_specs=[SMEM_SPEC] + [ANY_SPEC] * (len(operands) - 1),
-            out_specs=[ANY_SPEC] + [VMEM_SPEC] * 4,
-            input_output_aliases={len(operands) - 1: 0} if branch else {},
-            scratch_shapes=[
+            [after(info, when), all_units, hidden_grads] + wide_pieces,
+            1,
+            3 + 2 * wide_count,
+            [
                 pltpu.VMEM((tokens_now, width), BF16),
-                pltpu.VMEM((tokens_now, width), BF16),
+                pltpu.VMEM((tokens_now, padded), BF16),
                 pltpu.VMEM((width, padded), BF16),
                 pltpu.VMEM((width, padded), BF16),
-                pltpu.VMEM((padded, width), BF16),
                 pltpu.VMEM((tokens_now, width), F32),
-                pltpu.VMEM((tokens_now, width), F32),
-                pltpu.VMEM((tokens_now, width), BF16),
                 pltpu.SemaphoreType.DMA((plan_count,)),
                 pltpu.SemaphoreType.DMA((plan_count,)),
-                pltpu.SemaphoreType.DMA((2 * len(steps) + 1,)),
+                pltpu.SemaphoreType.DMA((len(steps) + 1,)),
             ],
-            compiler_params=params(),
-            cost_estimate=cost(0, 0),
-            name="feed",
-        )(*operands)
-        branch = [branch_now]
+            cost(0, 0),
+            "feed",
+        )
         fed.append((hidden, grads))
         early = list(unit_parts.values())
         swapped = swap_core(after(other, *early))
-        for index, step in enumerate(steps):
-            part = mine[index] + swapped[index]
+        parts = sums(info, *[[(mine, index), (swapped, index)] for index in range(len(steps))])
+        for step, part in zip(steps, parts):
             unit_parts[step] = shift_chip(part, -step) if step else part
-        when = swapped
+        when = parts[0]
+
     n_block = 384 if padded % 384 == 0 else LANES
 
     def wide_grad(start, items, when):
@@ -815,7 +849,7 @@
         )
 
     gate_came = wide_first(gate_parts) if aligned else []
-    up_came = wide_first(up_parts) if aligned else []
+    up_came = wide_first(up_parts, *unit_parts.values()) if aligned else []
 
     grad_middle, grad_attention, grad_queries, kv_mine, kv_other = call(
         functools.partial(middle_back_kernel, plan, chips, fsdp, count, sources),
@@ -826,7 +860,7 @@
             struct((reach + 1, rows, 2 * WIDTH_K), BF16),
             struct((reach + 1, rows, 2 * WIDTH_K), BF16),
         ],
-        [after(info, up_parts[0], *gate_came), places, queries, middle, grad_out]
+        [after(info, up_parts[0]), places, queries, middle, grad_out]
         + [unit_parts[step] for step in range(chips)]
         + kv_blocks
         + pieces,
@@ -843,42 +877,34 @@
             return [struct((width, columns), BF16)]
         return 2 * [struct((fsdp, len(steps), weight_rows, columns), BF16) for steps, _ in halves]
 
+    swapped = swap_core(after(kv_other, *gate_came))
+    returned = [kv_mine[step] + swapped[step] for step in range(1, reach + 1)]
+    branch = call(
+        functools.partial(branch_kernel, groups, chips, rows),
+        struct((ctx * rows, width), BF16),
+        [after(info, *returned), w_down] + [hidden for hidden, _ in fed],
+        estimate=cost(0, 0),
+        name="branch",
+    )
+    gate_pairs = wide_second(gate_parts, gate_came, *returned) if aligned else []
+    came = [shift_open(part, -step - 1) for step, part in enumerate(returned)]
+    outs = call(
+        functools.partial(projected_back_kernel, chips, fsdp, bias_width, reach),
+        [struct((rows, QKV), BF16)] + block_shapes(QKV + LANES),
+        [after(info, branch), grad_queries, kv_mine[0], swapped[0], cosine, sine, unit_one] + came,
+        scratch=[pltpu.VMEM((width, QKV + LANES), F32)],
+        estimate=cost(2 * rows * width * QKV, 2 * width * QKV),
+        name="projected_back",
+    )
+    grad_projected, qkv_parts = outs[0], outs[1:]
     out_parts = call(
         functools.partial(out_grad_kernel, chips, fsdp),
         block_shapes(width),
-        [info, grad_attention, context],
+        [after(info, grad_projected), grad_attention, context],
         scratch=[pltpu.VMEM((width, width), F32)],
         estimate=cost(2 * rows * width * width, 2 * width * width),
         name="out_grad",
     )
-    swapped = swap_core(after(kv_other, out_parts[0], *up_came))
-    gate_pairs = wide_second(gate_parts, gate_came, out_parts[0], *up_came) if aligned else []
-    if aligned:
-        down_orders = [halving_order(bits), halving_order(bits[::-1])]
-        down_shapes = [struct((fsdp // 2, own_down, d_half), BF16)] * 4
-    else:
-        down_orders = None
-        down_shapes = [struct((own, width), BF16)]
-    down_parts = call(
-        functools.partial(down_grad_kernel, down_orders, order, chips, rows),
-        down_shapes,
-        [after(info, swapped), all_cots] + [hidden for hidden, _ in fed],
-        scratch=[pltpu.VMEM((own, d_half), F32)],
-        estimate=cost(2 * ctx * rows * width * padded, 4 * width * padded),
-        name="down_grad",
-    )
-    came = []
-    for step in range(1, reach + 1):
-        came.append(shift_open(kv_mine[step] + swapped[step], -step))
-    outs = call(
-        functools.partial(projected_back_kernel, chips, fsdp, bias_width, reach),
-        [struct((rows, QKV), BF16)] + block_shapes(QKV + LANES),
-        [after(info, down_parts[0], *[away for _, away in gate_pairs]), grad_queries, kv_mine[0], swapped[0], cosine, sine, unit_one] + came,
-        scratch=[pltpu.VMEM((width, QKV + LANES), F32)],
-        estimate=cost(2 * rows * width * QKV, 2 * width * QKV),
-        name="projected_back",
-    )
-    grad_projected, qkv_parts = outs[0], outs[1:]
     def back_to_input(waits):
         return call(
             functools.partial(input_back_kernel, plan, chips, fsdp, count),
@@ -891,6 +917,16 @@
             "input_back",
         )
 
+    (down_part,) = call(
+        functools.partial(down_grad_kernel, None, order, chips, rows),
+        [struct((own, width), BF16)],
+        [after(info, out_parts[0], *[away for _, away in gate_pairs]), all_cots] + [hidden for hidden, _ in fed],
+        scratch=[pltpu.VMEM((own, d_half), F32)],
+        estimate=cost(0, 0),
+        name="down_grad",
+    )
+    down_grad = lax.psum_scatter(down_part, "fsdp", scatter_dimension=0, tiled=True).astype(F32)
+
     if aligned:
         sides = [items for _, items in halves]
 
@@ -911,40 +947,25 @@
                 sums.append((keep[3] + got[3] + more[1], away))
             return [mine + away for mine, away in sums]
 
-        up_pairs = wide_second(up_parts, up_came, *[away for _, away in gate_pairs])
+        aways = [away for _, away in gate_pairs]
+        up_pairs = wide_second(up_parts, up_came, *aways)
         gate_back = wide_across(gate_pairs, grad_projected)
         qkv_pairs = swapped_of(qkv_parts)
-        input_grad = back_to_input([])
+        qkv_came = first_exchange(qkv_pairs, *[away for _, away in up_pairs])
+        input_grad = back_to_input([down_part, *[got for _, got in qkv_pairs]])
+        up_back = wide_across(up_pairs, gate_back)
         out_pairs = swapped_of(out_parts)
-        out_came = first_exchange(out_pairs, *[away for _, away in gate_pairs])
-        down_came = [
-            swap_fsdp(after(part, *[away for _, away in gate_pairs]), items[0])
-            for part, items in zip(down_parts[::2], (bits, bits[::-1]))
-        ]
-        qkv_came = first_exchange(qkv_pairs, input_grad, *[away for _, away in up_pairs], *out_came)
-        up_back = wide_across(up_pairs, gate_back)
-        qkv_far = second_exchange(qkv_pairs, [after(item, *down_came) for item in qkv_came])
+        qkv_far = second_exchange(qkv_pairs, [after(item, input_grad) for item in qkv_came])
+        out_came = first_exchange(out_pairs, *qkv_came)
         qkv_sum = reduce_chips(qkv_far, chips, fsdp)
         out_far = second_exchange(out_pairs, [after(item, *qkv_far) for item in out_came])
         out_grad = reduce_chips(out_far, chips, fsdp)
-        down_away = [
-            swap_fsdp(after(kept[0] + more[0], *qkv_far), items[1])
-            for kept, more, items in zip(down_parts[1::2], down_came, (bits, bits[::-1]))
-        ]
-        down_grad = jnp.concatenate(
-            [
-                (kept[1] + more[1]).astype(F32) + away.astype(F32)
-                for kept, more, away in zip(down_parts[1::2], down_came, down_away)
-            ],
-            axis=1,
-        )
     else:
 
         def over(array, axes):
             return lax.psum_scatter(array, axes, scatter_dimension=0, tiled=True)
 
         qkv_sum, out_grad = (over(parts[0], BOTH).astype(F32) for parts in (qkv_parts, out_parts))
-        down_grad = over(down_parts[0], "fsdp").astype(F32)
         gate_back, up_back = (
             lax.all_to_all(
                 over(parts[0].reshape(-1, padded), "fsdp").reshape(ctx, weight_rows, padded), "ctx", 0, 0
@@ -952,7 +973,7 @@
             for parts in (gate_parts, up_parts)
         )
         input_grad = back_to_input([])
-    branch = lax.psum_scatter(after(branch[0], *early), "ctx", scatter_dimension=0, tiled=True)
+    branch = lax.psum_scatter(branch, "ctx", scatter_dimension=0, tiled=True)
     result = (middle + branch.astype(F32)).astype(BF16)
     gate_up_grad, norm2_grad = pl.pallas_call(
         functools.partial(join_kernel, own),

time: 524 us -> 509 us (0.971); the launches traced: 520 us -> 499 us
  waiting for transfers between devices: 191 us -> 182 us
  starting transfers between devices: 91.7 us -> 86.4 us
    pallas_call x2 -> x0, Pallas kernels: 61.9 us -> none  [shards(): pl.pallas_call(functools.partial(feed_kernel, steps, not branch, wide_pla...]
    pallas_call x9 -> x15, Pallas kernels: 66.8 us -> 126 us  [call(): pl.pallas_call(kernel, out_shape=outs, in_specs=specs, out_specs=[VMEM_SP...]
    ppermute x38 -> x34, waiting for transfers between devices: 149 us -> 118 us  [swap_fsdp(): return lax.ppermute(value, 'fsdp', [(i, i ^ bit) for i in range(count)])]
    ppermute x12, waiting for transfers between devices: 16.9 us -> 27.8 us  [shift_chip(): lax.ppermute(value, 'ctx', [(i, (i + 2 * steps) % count) for i in range(c...]
    ppermute x4, waiting for transfers between devices: 8.89 us -> 17.2 us  [shift_open(): return lax.ppermute(value, 'ctx', pairs)]
    ppermute x38 -> x34, starting transfers between devices: 41.9 us -> 35 us  [swap_fsdp(): return lax.ppermute(value, 'fsdp', [(i, i ^ bit) for i in range(count)])]
    add x4, other arithmetic: 2.34 us -> 8.76 us  [first_exchange(): keep[:half] + got[:half]]
    unnamed x154 -> x122, local copies, waits for them, and re-layouts: 10.2 us -> 12.9 us
  transfers between devices with their start and end apart: 78 -> 75, of which waited for: 33 -> 37; matrix products, arithmetic and copies ran while one was open for 9% -> 8% of each run, Pallas kernels for 23% -> 24%
where the time goes in v3:
time: 509 us; the launch traced here: 499 us
  waiting for transfers between devices  182 us (36%)
  Pallas kernels  157 us (31%)
  starting transfers between devices  86.4 us (17%)
  other arithmetic  36.5 us (7%)
  local copies, waits for them, and re-layouts  22.8 us (4%)
  between operations  14.9 us (3%)
    pallas_call x15, Pallas kernels, call(): pl.pallas_call(kernel, out_shape=outs, in_specs=specs, out_specs=[VMEM_SP...  126 us
    ppermute x34, waiting for transfers between devices, swap_fsdp(): return lax.ppermute(value, 'fsdp', [(i, i ^ bit) for i in range(count)])  118 us
    ppermute x34, starting transfers between devices, swap_fsdp(): return lax.ppermute(value, 'fsdp', [(i, i ^ bit) for i in range(count)])  35 us
    ppermute x12, waiting for transfers between devices, shift_chip(): lax.ppermute(value, 'ctx', [(i, (i + 2 * steps) % count) for i in range(c...  27.8 us
    ppermute x12, starting transfers between devices, shift_chip(): lax.ppermute(value, 'ctx', [(i, (i + 2 * steps) % count) for i in range(c...  22.9 us
    pallas_call x2, Pallas kernels, wide_grad(): pl.pallas_call(functools.partial(wide_grad_kernel, items), out_shape=[str...  18.2 us
    ppermute x4, waiting for transfers between devices, shift_open(): return lax.ppermute(value, 'ctx', pairs)  17.2 us
    unnamed x122, local copies, waits for them, and re-layouts  12.9 us
  transfers between devices with their start and end apart: 75, of which 37 were waited for; matrix products, arithmetic and copies ran while one was open for 8% of the time, Pallas kernels for 24%

profile of v3, /device:TPU:0, one launch (start us, length us, event | category | flops | bytes accessed | tf_op | source)
XLA Modules:
  0.0 499.1 jit_solution(1933337278108588525)
XLA Ops:
  11.8 5.0 %collective-permute-start.5 = (bf16[48,3712]{1,0:T(8,128)(2,1)}, bf16[48,3712]{1,0:T(8,128)(2,1)S(1)}, u32[]{:S(2)}, u32[]{:S(2)}) collective-permute-start(bf16[48,3712]{1,0:T(8,128)(2,1)} %pack.1), channel_id=1, source_target_pairs={{0,24},{4,28},{8,0},{12,4},{16,8},{20,12},{24,16},{28,20},{1,25},{... | collective-permute-start | bytes 1069064 | tf_op jit(solution)/shard_map/ppermute | solution.py:62
  33.2 5.5 %collective-permute-done.3.refs_6_ = bf16[280,768]{1,0:T(8,128)(2,1)S(1)} collective-permute-done((bf16[280,768]{1,0:T(8,128)(2,1)S(1)}, bf16[280,768]{1,0:T(8,128)(2,1)S(1)}, u32[]{:S(2)}, u32[]{:S(2)}) %collective-permute-start.3) | collective-permute-done | bytes 430112 | tf_op jit(solution)/shard_map/ppermute | solution.py:73
  43.1 7.3 %collective-permute-done.8 = bf16[48,3712]{1,0:T(8,128)(2,1)} collective-permute-done((bf16[48,3712]{1,0:T(8,128)(2,1)S(1)}, bf16[48,3712]{1,0:T(8,128)(2,1)}, u32[]{:S(2)}, u32[]{:S(2)}) %collective-permute-start.8) | collective-permute-done | bytes 356384 | tf_op jit(solution)/shard_map/ppermute | solution.py:62
  51.4 4.8 all-to-all-start
  61.7 14.7 %collective-permute-done.14.refs_4_.refs_10_.refs_14_ = bf16[96,3712]{1,0:T(8,128)(2,1)S(1)} collective-permute-done((bf16[96,3712]{1,0:T(8,128)(2,1)S(1)}, bf16[96,3712]{1,0:T(8,128)(2,1)S(1)}, u32[]{:S(2)}, u32[]{:S(2)}) %collective-permute-start.14) | collective-permute-done | bytes 712736 | tf_op jit(solution)/shard_map/ppermute | solution.py:73
  77.9 13.4 %collective-permute-done.17.refs_10_.refs_16_.refs_20_ = bf16[96,3712]{1,0:T(8,128)(2,1)S(1)} collective-permute-done((bf16[96,3712]{1,0:T(8,128)(2,1)S(1)}, bf16[96,3712]{1,0:T(8,128)(2,1)S(1)}, u32[]{:S(2)}, u32[]{:S(2)}) %collective-permute-start.17) | collective-permute-done | bytes 712736 | tf_op jit(solution)/shard_map/ppermute | solution.py:73
  92.5 5.8 %all-to-all-done = bf16[8,48,2304]{2,1,0:T(8,128)(2,1)} async-done(((bf16[8,48,2304]{2,1,0:T(8,128)(2,1)}), bf16[8,48,2304]{2,1,0:T(8,128)(2,1)}, u32[]{:S(2)}, u32[]{:S(2)}) %all-to-all-start) | async-done | bytes 1769504 | tf_op jit(solution)/shard_map/all_to_all | solution.py:139
  101.2 14.6 %collective-permute-done.18.refs_6_.refs_12_.refs_16_ = bf16[96,3712]{1,0:T(8,128)(2,1)S(1)} collective-permute-done((bf16[96,3712]{1,0:T(8,128)(2,1)S(1)}, bf16[96,3712]{1,0:T(8,128)(2,1)S(1)}, u32[]{:S(2)}, u32[]{:S(2)}) %collective-permute-start.18) | collective-permute-done | bytes 712736 | tf_op jit(solution)/shard_map/ppermute | solution.py:73
  132.1 6.9 %project.1 = (bf16[128,1536]{1,0:T(8,128)(2,1)}, bf16[128,1536]{1,0:T(8,128)(2,1)}, bf16[128,512]{1,0:T(8,128)(2,1)}) custom-call(s32[2]{0:T(128)} %pad_add_fusion.info_ref, bf16[128,1536]{1,0:T(8,128)(2,1)} %bitcast.97, f32[128,128]{1,0:T(8,128)} %copy.44.cos_ref, f32[128,128]{1,0:T(8,128)} %pad_maximum_fusion.4.sin_ref, bf16[96,3712]{1,0:T(8,128)(2,1)} %copy-done, ...), custom_call_target="tpu_custom_call" | custom-call | flops 1 | bytes 1 | tf_op jit(solution)/shard_map/project/pallas_call | solution.py:599
  147.3 5.3 %collective-permute-done.26.refs_2_.refs_6_ = bf16[128,512]{1,0:T(8,128)(2,1)S(1)} collective-permute-done((bf16[128,512]{1,0:T(8,128)(2,1)}, bf16[128,512]{1,0:T(8,128)(2,1)S(1)}, u32[]{:S(2)}, u32[]{:S(2)}) %collective-permute-start.26) | collective-permute-done | bytes 131104 | tf_op jit(solution)/shard_map/ppermute | solution.py:68
  154.7 9.5 %attend.1 = (bf16[128,1536]{1,0:T(8,128)(2,1)}, f32[128,1536]{1,0:T(8,128)}, bf16[128,1536]{1,0:T(8,128)(2,1)}) custom-call(s32[2]{0:T(128)} %pad_add_fusion.info_ref, s32[128,1]{1,0:T(8,128)} %copy.45.place_ref, bf16[128,1536]{1,0:T(8,128)(2,1)} %get-tuple-element.119.q_ref, bf16[128,1536]{1,0:T(8,128)(2,1)} %bitcast.98, ...), custom_call_target="tpu_custom_call" | custom-call | flops 1 | bytes 1 | tf_op jit(solution)/shard_map/attend/pallas_call | solution.py:599
  173.2 8.6 %hidden_grad.1.c_ref = bf16[1024,1152]{1,0:T(8,128)(2,1)} custom-call(s32[2]{0:T(128)} %pad_add_fusion.info_ref, bf16[1024,1536]{1,0:T(8,128)(2,1)} %all-gather.3.cloned.1.call-done.cots_ref, bf16[1120,1536]{1,0:T(8,128)(2,1)} %stack.13.down_ref), custom_call_target="tpu_custom_call" | custom-call | flops 1 | bytes 1 | tf_op jit(solution)/shard_map/hidden_grad/pallas_call | solution.py:599
  181.8 5.5 %collective-permute-done.32.refs_5_ = bf16[8,48,1152]{2,1,0:T(8,128)(2,1)S(1)} collective-permute-done((bf16[8,48,1152]{2,1,0:T(8,128)(2,1)}, bf16[8,48,1152]{2,1,0:T(8,128)(2,1)S(1)}, u32[]{:S(2)}, u32[]{:S(2)}) %collective-permute-start.32) | collective-permute-done | bytes 884768 | tf_op jit(solution)/shard_map/ppermute | solution.py:73
  187.9 17.7 %collective-permute-done.33.refs_7_ = bf16[8,48,1152]{2,1,0:T(8,128)(2,1)S(1)} collective-permute-done((bf16[8,48,1152]{2,1,0:T(8,128)(2,1)S(1)}, bf16[8,48,1152]{2,1,0:T(8,128)(2,1)S(1)}, u32[]{:S(2)}, u32[]{:S(2)}) %collective-permute-start.33) | collective-permute-done | bytes 884768 | tf_op jit(solution)/shard_map/ppermute | solution.py:73
  214.9 18.1 %feed.2 = (bf16[2,128,1536]{2,1,0:T(8,128)(2,1)}, bf16[2,128,1536]{2,1,0:T(8,128)(2,1)}, bf16[1152,512]{1,0:T(8,128)(2,1)}, bf16[512,2304]{1,0:T(8,128)(2,1)}) custom-call(s32[2]{0:T(128)} %pad_add_fusion.info_ref, bf16[1024,1536]{1,0:T(8,128)(2,1)} %all-gather.5.cloned.1.call-done.units_ref, bf16[1024,1152]{1,0:T(8,128)(2,1)} %hidden_grad.1.c_ref, ...), custom_call_target="tpu_custom_call" | custom-call | flops 1 | bytes 1 | tf_op jit(solution)/shard_map/feed/pallas_call | solution.py:599
  245.9 17.6 %feed.3 = (bf16[2,128,1536]{2,1,0:T(8,128)(2,1)}, bf16[2,128,1536]{2,1,0:T(8,128)(2,1)}, bf16[1152,512]{1,0:T(8,128)(2,1)}, bf16[512,2304]{1,0:T(8,128)(2,1)}) custom-call(s32[2]{0:T(128)} %pad_add_fusion.info_ref, bf16[1024,1536]{1,0:T(8,128)(2,1)} %all-gather.5.cloned.1.call-done.units_ref, bf16[1024,1152]{1,0:T(8,128)(2,1)} %hidden_grad.1.c_ref, ...), custom_call_target="tpu_custom_call" | custom-call | flops 1 | bytes 1 | tf_op jit(solution)/shard_map/feed/pallas_call | solution.py:599
  263.5 8.8 %collective-permute-done.35.refs_2_ = bf16[128,1536]{1,0:T(8,128)(2,1)S(1)} collective-permute-done((bf16[128,1536]{1,0:T(8,128)(2,1)}, bf16[128,1536]{1,0:T(8,128)(2,1)S(1)}, u32[]{:S(2)}, u32[]{:S(2)}) %collective-permute-start.35) | collective-permute-done | bytes 393248 | tf_op jit(solution)/shard_map/ppermute | solution.py:62
  272.4 9.1 %wide_grad.2 = (bf16[2,4,48,1152]{3,2,1,0:T(8,128)(2,1)}, bf16[2,4,48,1152]{3,2,1,0:T(8,128)(2,1)}, bf16[2,4,48,1152]{3,2,1,0:T(8,128)(2,1)}, bf16[2,4,48,1152]{3,2,1,0:T(8,128)(2,1)}) custom-call(s32[2]{0:T(128)} %pad_add_fusion.info_ref, bf16[1536,1024]{1,0:T(8,128)(2,1)} %turn.1.turned, bf16[512,2304]{1,0:T(8,128)(2,1)} %get-tuple-element.132.refs_0_, ...), custom_call_target="tpu_custom_call" | custom-call | flops 1 | bytes 1 | tf_op jit(solution)/shard_map/wide_grad/pallas_call | solution.py:815
  288.1 9.1 %wide_grad.3 = (bf16[2,4,48,1152]{3,2,1,0:T(8,128)(2,1)}, bf16[2,4,48,1152]{3,2,1,0:T(8,128)(2,1)}, bf16[2,4,48,1152]{3,2,1,0:T(8,128)(2,1)}, bf16[2,4,48,1152]{3,2,1,0:T(8,128)(2,1)}) custom-call(s32[2]{0:T(128)} %pad_add_fusion.info_ref, bf16[1536,1024]{1,0:T(8,128)(2,1)} %turn.1.turned, bf16[512,2304]{1,0:T(8,128)(2,1)} %get-tuple-element.132.refs_0_, ...), custom_call_target="tpu_custom_call" | custom-call | flops 1 | bytes 1 | tf_op jit(solution)/shard_map/wide_grad/pallas_call | solution.py:815
  301.6 14.2 %middle_back.1 = (f32[128,1536]{1,0:T(8,128)}, bf16[128,1536]{1,0:T(8,128)(2,1)}, f32[128,1536]{1,0:T(8,128)}, bf16[3,128,512]{2,1,0:T(8,128)(2,1)}, bf16[3,128,512]{2,1,0:T(8,128)(2,1)}) custom-call(s32[2]{0:T(128)} %pad_add_fusion.info_ref, s32[128,1]{1,0:T(8,128)} %copy.45.place_ref, bf16[128,1536]{1,0:T(8,128)(2,1)} %get-tuple-element.119.q_ref, ...), custom_call_target="tpu_custom_call" | custom-call | flops 1 | bytes 1 | tf_op jit(solution)/shard_map/middle_back/pallas_call | solution.py:599
  319.6 8.5 %branch.1 = bf16[1024,1536]{1,0:T(8,128)(2,1)} custom-call(s32[2]{0:T(128)} %pad_add_fusion.info_ref, bf16[1120,1536]{1,0:T(8,128)(2,1)} %stack.13.down_ref, bf16[1152,512]{1,0:T(8,128)(2,1)} %get-tuple-element.149.refs_0_, bf16[1152,512]{1,0:T(8,128)(2,1)} %get-tuple-element.150.refs_1_), custom_call_target="tpu_custom_call" | custom-call | flops 1 | bytes 1 | tf_op jit(solution)/shard_map/branch/pallas_call | solution.py:599
  336.4 8.9 %collective-permute-done.43.refs_1_ = bf16[128,512]{1,0:T(8,128)(2,1)S(1)} collective-permute-done((bf16[128,512]{1,0:T(8,128)(2,1)}, bf16[128,512]{1,0:T(8,128)(2,1)S(1)}, u32[]{:S(2)}, u32[]{:S(2)}) %collective-permute-start.43) | collective-permute-done | bytes 131104 | tf_op jit(solution)/shard_map/ppermute | solution.py:68
  348.2 6.7 %projected_back.1 = (bf16[128,2048]{1,0:T(8,128)(2,1)}, bf16[4,2,48,2176]{3,2,1,0:T(8,128)(2,1)}, bf16[4,2,48,2176]{3,2,1,0:T(8,128)(2,1)}, bf16[4,2,48,2176]{3,2,1,0:T(8,128)(2,1)}, bf16[4,2,48,2176]{3,2,1,0:T(8,128)(2,1)}) custom-call(s32[2]{0:T(128)} %pad_add_fusion.info_ref, f32[128,1536]{1,0:T(8,128)} %get-tuple-element.152.dq_ref, ...), custom_call_target="tpu_custom_call" | custom-call | flops 1 | bytes 1 | tf_op jit(solution)/shard_map/projected_back/pallas_call | solution.py:599
  355.1 5.0 out_grad.1
  364.9 6.8 %all-to-all-start.1 = ((bf16[8,48,1152]{2,1,0:T(8,128)(2,1)}), bf16[8,48,1152]{2,1,0:T(8,128)(2,1)S(1)}, u32[]{:S(2)}, u32[]{:S(2)}) async-start(bf16[8,48,1152]{2,1,0:T(8,128)(2,1)} %pad_maximum_fusion), calls=%async_computation.2 | async-start | bytes 1769472 | tf_op jit(solution)/shard_map/all_to_all | solution.py:847
  371.8 8.1 %down_grad.1 = bf16[1120,1536]{1,0:T(8,128)(2,1)} custom-call(s32[2]{0:T(128)} %pad_add_fusion.info_ref, bf16[1024,1536]{1,0:T(8,128)(2,1)} %all-gather.3.cloned.1.call-done.cots_ref, bf16[1152,512]{1,0:T(8,128)(2,1)} %get-tuple-element.149.refs_0_, bf16[1152,512]{1,0:T(8,128)(2,1)} %get-tuple-element.150.refs_1_), custom_call_target="tpu_custom_call" | custom-call | flops 1 | bytes 1 | tf_op jit(solution)/shard_map/down_grad/pallas_call | solution.py:599
  381.5 15.6 %collective-permute-done.51 = bf16[4,48,1152]{2,1,0:T(8,128)(2,1)S(1)} collective-permute-done((bf16[4,48,1152]{2,1,0:T(8,128)(2,1)S(1)}, bf16[4,48,1152]{2,1,0:T(8,128)(2,1)S(1)}, u32[]{:S(2)}, u32[]{:S(2)}) %collective-permute-start.51) | collective-permute-done | bytes 442400 | tf_op jit(solution)/shard_map/ppermute | solution.py:73
  408.3 7.9 %input_back.1 = f32[128,1536]{1,0:T(8,128)} custom-call(s32[2]{0:T(128)} %pad_add_fusion.info_ref, bf16[128,2048]{1,0:T(8,128)(2,1)} %get-tuple-element.154.gp_ref, bf16[128,1536]{1,0:T(8,128)(2,1)} %bitcast.99, f32[128,1536]{1,0:T(8,128)} %get-tuple-element.167.middle_ref, bf16[96,3712]{1,0:T(8,128)(2,1)} %copy-done, bf16[96,3712]{1,0:T(8,128)(2,1)} %copy-done.7, ...), custom_call_target="tpu_custom_call" | custom-call | flops 1 | bytes 1 | tf_op jit(solution)/shard_map/input_back/pallas_call | solution.py:599
  416.9 5.0 all-to-all-start.2
  425.0 8.6 %collective-permute-done.52 = bf16[2,2,48,2176]{3,2,1,0:T(8,128)(2,1)} collective-permute-done((bf16[2,2,48,2176]{3,2,1,0:T(8,128)(2,1)}, bf16[2,2,48,2176]{3,2,1,0:T(8,128)(2,1)}, u32[]{:S(2)}, u32[]{:S(2)}) %collective-permute-start.52) | collective-permute-done | bytes 835616 | tf_op jit(solution)/shard_map/ppermute | solution.py:73
  440.3 7.8 %collective-permute-done.56 = bf16[2,48,2176]{2,1,0:T(8,128)(2,1)S(1)} collective-permute-done((bf16[2,48,2176]{2,1,0:T(8,128)(2,1)S(1)}, bf16[2,48,2176]{2,1,0:T(8,128)(2,1)S(1)}, u32[]{:S(2)}, u32[]{:S(2)}) %collective-permute-start.56) | collective-permute-done | bytes 417824 | tf_op jit(solution)/shard_map/ppermute | solution.py:73
  478.8 6.8 %join.1 = (f32[48,17920]{1,0:T(8,128)}, f32[48,1]{1,0:T(8,128)}) custom-call(bf16[8,48,1152]{2,1,0:T(8,128)(2,1)} %copy-done.16, bf16[8,48,1152]{2,1,0:T(8,128)(2,1)} %copy-done.17, bf16[48,17920]{1,0:T(8,128)(2,1)} %weight_ref.3, f32[48,1]{1,0:T(8,128)} %copy.48.gain_ref), custom_call_target="tpu_custom_call" | custom-call | tf_op jit(solution)/shard_map/join/pallas_call | solution.py:978
  (320 shorter events, 186.8 us)
Async XLA Ops:
  51.4 46.9 %all-to-all-start = ((bf16[8,48,2304]{2,1,0:T(8,128)(2,1)}), bf16[8,48,2304]{2,1,0:T(8,128)(2,1)}, u32[]{:S(2)}, u32[]{:S(2)}) async-start(bf16[8,48,2304]{2,1,0:T(8,128)(2,1)} %split.1), calls=%async_computation | async-start | bytes 3538944 | tf_op jit(solution)/shard_map/all_to_all | solution.py:139
  56.2 108.1 %all-gather.3.cloned.1.call-start = ((), (), s32[]{:S(2)}) async-start(), calls=%async_computation.5 | async-start | bytes 3538944 | tf_op jit(solution)/shard_map/all_gather | solution.py:723
  57.6 18.8 %collective-permute-start.14 = (bf16[96,3712]{1,0:T(8,128)(2,1)S(1)}, bf16[96,3712]{1,0:T(8,128)(2,1)S(1)}, u32[]{:S(2)}, u32[]{:S(2)}) collective-permute-start(bf16[96,3712]{1,0:T(8,128)(2,1)S(1)} %pad_maximum_fusion.2.refs_0_.refs_6_.refs_10_), channel_id=1, source_target_pairs={{0,2},{1,3},{2,0},{3,1},{4,6},{5,7},{6,4},{7,5},{8,10},{9,11},{10,... | collective-permute-start | bytes 2138120 | tf_op jit(solution)/shard_map/ppermute | solution.py:73
  59.1 18.8 %collective-permute-start.12 = (bf16[96,3712]{1,0:T(8,128)(2,1)S(1)}, bf16[96,3712]{1,0:T(8,128)(2,1)S(1)}, u32[]{:S(2)}, u32[]{:S(2)}) collective-permute-start(bf16[96,3712]{1,0:T(8,128)(2,1)S(1)} %pad_maximum_fusion.2.refs_0_.refs_6_.refs_10_), channel_id=1, source_target_pairs={{0,1},{1,0},{2,3},{3,2},{4,5},{5,4},{6,7},{7,6},{8,9},{9,8},{10,11... | collective-permute-start | bytes 2138120 | tf_op jit(solution)/shard_map/ppermute | solution.py:73
  60.6 30.7 %collective-permute-start.17 = (bf16[96,3712]{1,0:T(8,128)(2,1)S(1)}, bf16[96,3712]{1,0:T(8,128)(2,1)S(1)}, u32[]{:S(2)}, u32[]{:S(2)}) collective-permute-start(bf16[96,3712]{1,0:T(8,128)(2,1)S(1)} %pad_maximum_fusion.3.refs_8_.refs_14_.refs_18_), channel_id=1, source_target_pairs={{0,2},{1,3},{2,0},{3,1},{4,6},{5,7},{6,4},{7,5},{8,10},{9,11},{10,... | collective-permute-start | bytes 2138120 | tf_op jit(solution)/shard_map/ppermute | solution.py:73
  61.2 31.3 %collective-permute-start.16 = (bf16[96,3712]{1,0:T(8,128)(2,1)S(1)}, bf16[96,3712]{1,0:T(8,128)(2,1)}, u32[]{:S(2)}, u32[]{:S(2)}) collective-permute-start(bf16[96,3712]{1,0:T(8,128)(2,1)S(1)} %pad_maximum_fusion.3.refs_8_.refs_14_.refs_18_), channel_id=1, source_target_pairs={{0,1},{1,0},{2,3},{3,2},{4,5},{5,4},{6,7},{7,6},{8,9},{9,8},{10,11... | collective-permute-start | bytes 2138120 | tf_op jit(solution)/shard_map/ppermute | solution.py:73
  118.1 92.2 %all-gather.5.cloned.1.call-start = ((), (), s32[]{:S(2)}) async-start(), calls=%async_computation.6 | async-start | bytes 3538944 | tf_op jit(solution)/shard_map/all_gather | solution.py:754
  128.4 24.9 %collective-permute-start.10 = (bf16[8,48,1152]{2,1,0:T(8,128)(2,1)}, bf16[8,48,1152]{2,1,0:T(8,128)(2,1)S(1)}, u32[]{:S(2)}, u32[]{:S(2)}) collective-permute-start(bf16[8,48,1152]{2,1,0:T(8,128)(2,1)} %get-tuple-element.193.refs_4_), channel_id=1, source_target_pairs={{0,2},{1,3},{2,0},{3,1},{4,6},{5,7},{6,4},{7,5},{8,10},{9,11},{10,... | collective-permute-start | bytes 2654216 | tf_op jit(solution)/shard_map/ppermute | solution.py:73
  129.3 24.1 %collective-permute-start.9 = (bf16[8,48,1152]{2,1,0:T(8,128)(2,1)}, bf16[8,48,1152]{2,1,0:T(8,128)(2,1)S(1)}, u32[]{:S(2)}, u32[]{:S(2)}) collective-permute-start(bf16[8,48,1152]{2,1,0:T(8,128)(2,1)} %get-tuple-element.194.refs_0_), channel_id=1, source_target_pairs={{0,1},{1,0},{2,3},{3,2},{4,5},{5,4},{6,7},{7,6},{8,9},{9,8},{10,11... | collective-permute-start | bytes 2654216 | tf_op jit(solution)/shard_map/ppermute | solution.py:73
  164.3 323.5 %reduce-scatter.5.cloned.1.call-start = ((), (), s32[]{:S(2)}) async-start(), calls=%async_computation.7 | async-start | bytes 3538944 | tf_op jit(solution)/shard_map/reduce_scatter | solution.py:976
  164.6 22.8 %collective-permute-start.32 = (bf16[8,48,1152]{2,1,0:T(8,128)(2,1)}, bf16[8,48,1152]{2,1,0:T(8,128)(2,1)S(1)}, u32[]{:S(2)}, u32[]{:S(2)}) collective-permute-start(bf16[8,48,1152]{2,1,0:T(8,128)(2,1)} %get-tuple-element.193.refs_4_), channel_id=1, source_target_pairs={{0,1},{1,0},{2,3},{3,2},{4,5},{5,4},{6,7},{7,6},{8,9},{9,8},{10,11... | collective-permute-start | bytes 2654216 | tf_op jit(solution)/shard_map/ppermute | solution.py:73
  165.2 22.7 %collective-permute-start.30 = (bf16[8,48,1152]{2,1,0:T(8,128)(2,1)}, bf16[8,48,1152]{2,1,0:T(8,128)(2,1)S(1)}, u32[]{:S(2)}, u32[]{:S(2)}) collective-permute-start(bf16[8,48,1152]{2,1,0:T(8,128)(2,1)} %get-tuple-element.194.refs_0_), channel_id=1, source_target_pairs={{0,2},{1,3},{2,0},{3,1},{4,6},{5,7},{6,4},{7,5},{8,10},{9,11},{10,... | collective-permute-start | bytes 2654216 | tf_op jit(solution)/shard_map/ppermute | solution.py:73
  166.3 39.3 %collective-permute-start.33 = (bf16[8,48,1152]{2,1,0:T(8,128)(2,1)S(1)}, bf16[8,48,1152]{2,1,0:T(8,128)(2,1)S(1)}, u32[]{:S(2)}, u32[]{:S(2)}) collective-permute-start(bf16[8,48,1152]{2,1,0:T(8,128)(2,1)S(1)} %collective-permute-done.10.refs_6_), channel_id=1, source_target_pairs={{0,1},{1,0},{2,3},{3,2},{4,5},{5,4},{6,7},{7,6},{8,9},{9,8},{10,11... | collective-permute-start | bytes 2654216 | tf_op jit(solution)/shard_map/ppermute | solution.py:73
  167.7 38.9 %collective-permute-start.31 = (bf16[8,48,1152]{2,1,0:T(8,128)(2,1)S(1)}, bf16[8,48,1152]{2,1,0:T(8,128)(2,1)}, u32[]{:S(2)}, u32[]{:S(2)}) collective-permute-start(bf16[8,48,1152]{2,1,0:T(8,128)(2,1)S(1)} %collective-permute-done.9.refs_1_), channel_id=1, source_target_pairs={{0,2},{1,3},{2,0},{3,1},{4,6},{5,7},{6,4},{7,5},{8,10},{9,11},{10,... | collective-permute-start | bytes 2654216 | tf_op jit(solution)/shard_map/ppermute | solution.py:73
  239.4 24.2 %collective-permute-start.36 = (bf16[128,1536]{1,0:T(8,128)(2,1)}, bf16[128,1536]{1,0:T(8,128)(2,1)S(1)}, u32[]{:S(2)}, u32[]{:S(2)}) collective-permute-start(bf16[128,1536]{1,0:T(8,128)(2,1)} %get-tuple-element.130), channel_id=1, source_target_pairs={{0,24},{4,28},{8,0},{12,4},{16,8},{20,12},{24,16},{28,20},{1,25},{... | collective-permute-start | bytes 1179656 | tf_op jit(solution)/shard_map/ppermute | solution.py:62
  241.5 30.8 %collective-permute-start.35 = (bf16[128,1536]{1,0:T(8,128)(2,1)}, bf16[128,1536]{1,0:T(8,128)(2,1)S(1)}, u32[]{:S(2)}, u32[]{:S(2)}) collective-permute-start(bf16[128,1536]{1,0:T(8,128)(2,1)} %get-tuple-element.129), channel_id=1, source_target_pairs={{0,16},{4,20},{8,24},{12,28},{16,0},{20,4},{24,8},{28,12},{1,17},{... | collective-permute-start | bytes 1179656 | tf_op jit(solution)/shard_map/ppermute | solution.py:62
  281.5 34.3 %collective-permute-start.39 = (bf16[2,4,48,1152]{3,2,1,0:T(8,128)(2,1)}, bf16[2,4,48,1152]{3,2,1,0:T(8,128)(2,1)S(1)}, u32[]{:S(2)}, u32[]{:S(2)}) collective-permute-start(bf16[2,4,48,1152]{3,2,1,0:T(8,128)(2,1)} %get-tuple-element.135), channel_id=1, source_target_pairs={{0,1},{1,0},{2,3},{3,2},{4,5},{5,4},{6,7},{7,6},{8,9},{9,8},{10,11... | collective-permute-start | bytes 2654216 | tf_op jit(solution)/shard_map/ppermute | solution.py:73
  282.7 33.1 %collective-permute-start.40 = (bf16[2,4,48,1152]{3,2,1,0:T(8,128)(2,1)}, bf16[2,4,48,1152]{3,2,1,0:T(8,128)(2,1)S(1)}, u32[]{:S(2)}, u32[]{:S(2)}) collective-permute-start(bf16[2,4,48,1152]{3,2,1,0:T(8,128)(2,1)} %get-tuple-element.146), channel_id=1, source_target_pairs={{0,2},{1,3},{2,0},{3,1},{4,6},{5,7},{6,4},{7,5},{8,10},{9,11},{10,... | collective-permute-start | bytes 2654216 | tf_op jit(solution)/shard_map/ppermute | solution.py:73
  330.2 31.5 %collective-permute-start.48 = (bf16[2,4,48,1152]{3,2,1,0:T(8,128)(2,1)}, bf16[2,4,48,1152]{3,2,1,0:T(8,128)(2,1)S(1)}, u32[]{:S(2)}, u32[]{:S(2)}) collective-permute-start(bf16[2,4,48,1152]{3,2,1,0:T(8,128)(2,1)} %get-tuple-element.170), channel_id=1, source_target_pairs={{0,1},{1,0},{2,3},{3,2},{4,5},{5,4},{6,7},{7,6},{8,9},{9,8},{10,11... | collective-permute-start | bytes 2654216 | tf_op jit(solution)/shard_map/ppermute | solution.py:73
  331.1 31.1 %collective-permute-start.50 = (bf16[2,4,48,1152]{3,2,1,0:T(8,128)(2,1)}, bf16[2,4,48,1152]{3,2,1,0:T(8,128)(2,1)S(1)}, u32[]{:S(2)}, u32[]{:S(2)}) collective-permute-start(bf16[2,4,48,1152]{3,2,1,0:T(8,128)(2,1)} %get-tuple-element.174), channel_id=1, source_target_pairs={{0,2},{1,3},{2,0},{3,1},{4,6},{5,7},{6,4},{7,5},{8,10},{9,11},{10,... | collective-permute-start | bytes 2654216 | tf_op jit(solution)/shard_map/ppermute | solution.py:73
  334.5 27.1 %collective-permute-start.45 = (bf16[4,48,1152]{2,1,0:T(8,128)(2,1)}, bf16[4,48,1152]{2,1,0:T(8,128)(2,1)S(1)}, u32[]{:S(2)}, u32[]{:S(2)}) collective-permute-start(bf16[4,48,1152]{2,1,0:T(8,128)(2,1)} %fusion.10), channel_id=1, source_target_pairs={{0,1},{1,0},{2,3},{3,2},{4,5},{5,4},{6,7},{7,6},{8,9},{9,8},{10,11... | collective-permute-start | bytes 1327112 | tf_op jit(solution)/shard_map/ppermute | solution.py:73
  355.0 43.2 %collective-permute-start.47 = (bf16[4,2,48,2176]{3,2,1,0:T(8,128)(2,1)}, bf16[4,2,48,2176]{3,2,1,0:T(8,128)(2,1)}, u32[]{:S(2)}, u32[]{:S(2)}) collective-permute-start(bf16[4,2,48,2176]{3,2,1,0:T(8,128)(2,1)} %get-tuple-element.165), channel_id=1, source_target_pairs={{0,4},{4,0},{8,12},{12,8},{16,20},{20,16},{24,28},{28,24},{1,5},{5... | collective-permute-start | bytes 5013512 | tf_op jit(solution)/shard_map/ppermute | solution.py:57
  361.6 39.1 %collective-permute-start.46 = (bf16[4,2,48,2176]{3,2,1,0:T(8,128)(2,1)}, bf16[4,2,48,2176]{3,2,1,0:T(8,128)(2,1)}, u32[]{:S(2)}, u32[]{:S(2)}) collective-permute-start(bf16[4,2,48,2176]{3,2,1,0:T(8,128)(2,1)} %get-tuple-element.164), channel_id=1, source_target_pairs={{0,4},{4,0},{8,12},{12,8},{16,20},{20,16},{24,28},{28,24},{1,5},{5... | collective-permute-start | bytes 5013512 | tf_op jit(solution)/shard_map/ppermute | solution.py:57
  361.7 44.7 %collective-permute-start.63 = (bf16[4,2,48,1536]{3,2,1,0:T(8,128)(2,1)}, bf16[4,2,48,1536]{3,2,1,0:T(8,128)(2,1)}, u32[]{:S(2)}, u32[]{:S(2)}) collective-permute-start(bf16[4,2,48,1536]{3,2,1,0:T(8,128)(2,1)} %get-tuple-element.185), channel_id=1, source_target_pairs={{0,4},{4,0},{8,12},{12,8},{16,20},{20,16},{24,28},{28,24},{1,5},{5... | collective-permute-start | bytes 3538952 | tf_op jit(solution)/shard_map/ppermute | solution.py:57
  362.2 42.1 %collective-permute-start.59 = (bf16[4,2,48,1536]{3,2,1,0:T(8,128)(2,1)}, bf16[4,2,48,1536]{3,2,1,0:T(8,128)(2,1)}, u32[]{:S(2)}, u32[]{:S(2)}) collective-permute-start(bf16[4,2,48,1536]{3,2,1,0:T(8,128)(2,1)} %get-tuple-element.181), channel_id=1, source_target_pairs={{0,4},{4,0},{8,12},{12,8},{16,20},{20,16},{24,28},{28,24},{1,5},{5... | collective-permute-start | bytes 3538952 | tf_op jit(solution)/shard_map/ppermute | solution.py:57
  364.9 51.9 %all-to-all-start.1 = ((bf16[8,48,1152]{2,1,0:T(8,128)(2,1)}), bf16[8,48,1152]{2,1,0:T(8,128)(2,1)S(1)}, u32[]{:S(2)}, u32[]{:S(2)}) async-start(bf16[8,48,1152]{2,1,0:T(8,128)(2,1)} %pad_maximum_fusion), calls=%async_computation.2 | async-start | bytes 1769472 | tf_op jit(solution)/shard_map/all_to_all | solution.py:847
  371.7 117.9 %reduce-scatter.7.cloned.1.call-start = ((), (), s32[]{:S(2)}) async-start(), calls=%async_computation.8 | async-start | bytes 4300800
  400.6 24.4 %collective-permute-start.55 = (bf16[2,2,48,2176]{3,2,1,0:T(8,128)(2,1)}, bf16[2,2,48,2176]{3,2,1,0:T(8,128)(2,1)}, u32[]{:S(2)}, u32[]{:S(2)}) collective-permute-start(bf16[2,2,48,2176]{3,2,1,0:T(8,128)(2,1)} %slice_add_fusion), channel_id=1, source_target_pairs={{0,2},{1,3},{2,0},{3,1},{4,6},{5,7},{6,4},{7,5},{8,10},{9,11},{10,... | collective-permute-start | bytes 2506760 | tf_op jit(solution)/shard_map/ppermute | solution.py:73
  403.0 30.6 %collective-permute-start.52 = (bf16[2,2,48,2176]{3,2,1,0:T(8,128)(2,1)}, bf16[2,2,48,2176]{3,2,1,0:T(8,128)(2,1)}, u32[]{:S(2)}, u32[]{:S(2)}) collective-permute-start(bf16[2,2,48,2176]{3,2,1,0:T(8,128)(2,1)} %slice_add_fusion.1), channel_id=1, source_target_pairs={{0,1},{1,0},{2,3},{3,2},{4,5},{5,4},{6,7},{7,6},{8,9},{9,8},{10,11... | collective-permute-start | bytes 2506760 | tf_op jit(solution)/shard_map/ppermute | solution.py:73
  416.9 61.0 %all-to-all-start.2 = ((bf16[8,48,1152]{2,1,0:T(8,128)(2,1)}), bf16[8,48,1152]{2,1,0:T(8,128)(2,1)S(1)}, u32[]{:S(2)}, u32[]{:S(2)}) async-start(bf16[8,48,1152]{2,1,0:T(8,128)(2,1)} %pad_maximum_fusion.1), calls=%async_computation.3 | async-start | bytes 1769472 | tf_op jit(solution)/shard_map/all_to_all | solution.py:847
  437.7 22.3 %collective-permute-start.64 = (bf16[2,2,48,1536]{3,2,1,0:T(8,128)(2,1)S(1)}, bf16[2,2,48,1536]{3,2,1,0:T(8,128)(2,1)S(1)}, u32[]{:S(2)}, u32[]{:S(2)}) collective-permute-start(bf16[2,2,48,1536]{3,2,1,0:T(8,128)(2,1)S(1)} %copy-done.42), channel_id=1, source_target_pairs={{0,2},{1,3},{2,0},{3,1},{4,6},{5,7},{6,4},{7,5},{8,10},{9,11},{10,... | collective-permute-start | bytes 1769480 | tf_op jit(solution)/shard_map/ppermute | solution.py:73
  439.7 21.7 %collective-permute-start.60 = (bf16[2,2,48,1536]{3,2,1,0:T(8,128)(2,1)S(1)}, bf16[2,2,48,1536]{3,2,1,0:T(8,128)(2,1)S(1)}, u32[]{:S(2)}, u32[]{:S(2)}) collective-permute-start(bf16[2,2,48,1536]{3,2,1,0:T(8,128)(2,1)S(1)} %copy-done.41), channel_id=1, source_target_pairs={{0,1},{1,0},{2,3},{3,2},{4,5},{5,4},{6,7},{7,6},{8,9},{9,8},{10,11... | collective-permute-start | bytes 1769480 | tf_op jit(solution)/shard_map/ppermute | solution.py:73
  (104 other events, 1173.5 us)
Sparse Core Ops, SparseCore 0:
  118.2 38.0 all-gather.2
  164.4 45.8 all-gather.4
  328.3 42.2 reduce-scatter.4
  380.1 60.9 reduce-scatter.6
